TPU v7x, 256 devices: a whole 4x4x8 slice. The times are simulated.
256 devices in a mesh: expert: 128 (over x, y, z), dp: 2 (over core).
Axes of the slice: x: 4, y: 4, z: 8, core: 2. Of those that a mesh axis runs over, the one named last changes fastest.
Arguments:
- tokens: bfloat16 [16384, 1024], P('expert'), may hold values from -6 to 6
- router_weight: bfloat16 [1024, 64], replicated, may hold values from -0.375 to 0.375
- gate_weight: bfloat16 [128, 1024, 2048], P('expert', None, 'dp'), may hold values from -0.1875 to 0.1875
- up_weight: bfloat16 [128, 1024, 2048], P('expert', None, 'dp'), may hold values from -0.1875 to 0.1875
- down_weight: bfloat16 [128, 2048, 1024], P('expert', 'dp'), may hold values from -0.1875 to 0.1875
- expand_weight: bfloat16 [1024, 8192], P(None, ('expert', 'dp')), may hold values from -0.5 to 0.5
- expert_ids: int32 [16384, 2], P('expert'), may hold values from 0 to 63, all different within a row; in each aligned block of 128 rows (0 to 127, 128 to 255, ...) at most 8 rows name the same one
- frame_slot: int32 [1024], P('expert'), may hold values from 0 to 1023, each once
Outputs:
- mixed: bfloat16 [16384, 1024], P('expert', 'dp')
- covariance: float32 [8192, 8192], P(('expert', 'dp'))
Inputs may be any that keep to these rules, and one draw needn't show every extreme that they name: `expert_ids`: each row names 2 different experts; the rows of one device name each expert at most 8 times, and in every draw some device names some expert exactly 8 times. `frame_slot`: each number once.
All inputs are finite; a program needn't handle non-finite values.
Results may differ from a plain program's by a relative error of at most 0.02.
Values may be sent and summed in bfloat16 or wider, within the bound.
No kernel may reach another device: no remote copies, remote signals or barrier semaphores. Data moves between devices by JAX's collectives and lax.ppermute only.
A program may use at most 192 MiB of HBM per device.

v0:
```python
import jax
import jax.numpy as jnp
from jax import lax
from jax.sharding import PartitionSpec as P


def per_device(
    tokens,
    router_weight,
    gate_weight,
    up_weight,
    down_weight,
    expand_weight,
    expert_ids,
    frame_slot,
):
    tok_rows, width = tokens.shape
    experts = router_weight.shape[1]
    top_count = expert_ids.shape[1]
    n_expert = lax.axis_size("expert")
    n_replica = lax.axis_size("dp")
    capacity = 4 * tok_rows // experts
    half_width = width // n_replica
    logits = jnp.dot(tokens, router_weight, preferred_element_type=jnp.float32)
    hot = expert_ids[:, :, None] == jnp.arange(experts, dtype=jnp.int32)[None, None, :]
    chosen = jnp.sum(jnp.where(hot, logits[:, None, :], jnp.float32(0.0)), axis=-1)
    gates = jax.nn.sigmoid(chosen - chosen[:, ::-1])
    flat_hot = hot.astype(jnp.int32).reshape(tok_rows * top_count, experts)
    slot = jnp.sum((jnp.cumsum(flat_hot, axis=0) - flat_hot) * flat_hot, axis=1)
    dest = expert_ids.reshape(-1) * capacity + slot
    repeated = jnp.repeat(tokens, top_count, axis=0)
    outgoing = jnp.zeros((experts * capacity, width), jnp.bfloat16).at[dest].set(repeated)
    outgoing = jnp.broadcast_to(
        outgoing.reshape(experts, 1, capacity, width), (experts, 2, capacity, width)
    )
    outgoing = outgoing.reshape(n_expert, capacity, width)
    w_gate = gate_weight[0]
    w_up = up_weight[0]
    w_down = down_weight[0]
    received = lax.all_to_all(outgoing, "expert", split_axis=0, concat_axis=0, tiled=True)
    count = received.shape[1]
    flat = received.reshape(n_expert * count, width)
    gate = jnp.dot(flat, w_gate, preferred_element_type=jnp.float32)
    upper = jnp.dot(flat, w_up, preferred_element_type=jnp.float32)
    hidden = (jax.nn.silu(gate) * upper).astype(jnp.bfloat16)
    piece = jnp.dot(hidden, w_down, preferred_element_type=jnp.float32).astype(jnp.bfloat16)
    piece = piece.reshape(n_expert, 1, count, width)
    returned = lax.all_to_all(
        lax.all_to_all(piece, "expert", split_axis=0, concat_axis=0, tiled=True),
        "dp",
        split_axis=3,
        concat_axis=1,
        tiled=True,
    )
    summed = jnp.sum(
        returned.reshape(experts, 2 * n_replica, capacity, half_width), axis=1, dtype=jnp.float32
    )
    summed = summed.reshape(experts * capacity, half_width)
    picked = summed[dest].reshape(tok_rows, top_count, half_width)
    moe = jnp.sum(picked * gates[:, :, None], axis=1)
    replica = lax.axis_index("dp")
    own_part = lax.dynamic_slice_in_dim(tokens, replica * half_width, half_width, 1).astype(
        jnp.float32
    )
    mixed = (own_part + moe).astype(jnp.bfloat16)
    frame_count = frame_slot.shape[0]
    frame_tok = tok_rows // frame_count
    frames = jnp.mean(
        mixed.reshape(frame_count, frame_tok, half_width), axis=1, dtype=jnp.float32
    ).astype(jnp.bfloat16)
    owner = frame_slot // frame_count
    position = frame_slot % frame_count
    parcel = (
        jnp.zeros((n_expert, frame_count, half_width), jnp.bfloat16).at[owner, position].set(frames)
    )
    arrived = lax.all_to_all(
        lax.all_to_all(parcel, "expert", split_axis=0, concat_axis=0, tiled=True),
        "dp",
        split_axis=1,
        concat_axis=2,
        tiled=True,
    )
    clip_frames = arrived.shape[1]
    clip_row = (jnp.sum(arrived, axis=(0, 1), dtype=jnp.float32) / clip_frames).astype(
        jnp.bfloat16
    )[None, :]
    every_clip = lax.all_gather(clip_row, ("expert", "dp"), axis=0, tiled=True)
    clip_total = every_clip.shape[0]
    share_cols = expand_weight.shape[1]
    embed = jnp.dot(
        every_clip,
        lax.all_gather(expand_weight, ("expert", "dp"), axis=1, tiled=True),
        preferred_element_type=jnp.float32,
    )
    centered = embed - jnp.mean(embed, axis=0, keepdims=True)
    start = lax.axis_index(("expert", "dp")) * share_cols
    mine = lax.dynamic_slice_in_dim(centered, start, share_cols, 1)
    covariance = jnp.dot(
        mine.T, centered, precision=lax.Precision.HIGHEST, preferred_element_type=jnp.float32
    ) / (clip_total - 1)
    return (mixed, covariance)


def solution(mesh):
    return jax.shard_map(
        per_device,
        mesh=mesh,
        in_specs=(
            P("expert", None),
            P(),
            P("expert", None, "dp"),
            P("expert", None, "dp"),
            P("expert", "dp", None),
            P(None, ("expert", "dp")),
            P("expert", None),
            P("expert"),
        ),
        out_specs=(P("expert", "dp"), P(("expert", "dp"), None)),
        check_vma=False,
    )
```

profile of v0, /device:TPU:1, one launch (start us, length us, event | category | flops | bytes accessed | tf_op | source)
XLA Modules:
  0.0 419.5 jit_solution(11740641414167100878)
XLA Ops:
  7.2 0.7 all-gather.3.cloned.1.call-update
  7.9 0.8 copy.57
  9.0 0.6 reduce-window.6
  9.8 0.7 broadcast_multiply_fusion.1
  10.8 1.2 broadcast_in_dim.43
  12.0 1.0 reshape.127
  13.1 2.4 scatter_custom_fusion
  15.8 72.8 %all_to_all.33 = bf16[128,8,1024]{2,1,0:T(8,128)(2,1)S(1)} all-to-all(bf16[128,8,1024]{2,1,0:T(8,128)(2,1)S(1)} %bitcast.79), channel_id=1, replica_groups=mesh['expert'=128,'dp'=2] {'expert'}, dimensions={0} | all-to-all | bytes 4194304 | tf_op jit(solution)/shard_map/all_to_all | solution.py:40
  88.6 1.3 copy-done.2
  89.9 4.3 %fusion.3 = f32[1024,1024]{1,0:T(8,128)} fusion(bf16[1,1024,1024]{2,1,0:T(8,128)(2,1)S(1)} %copy-done, bf16[128,8,1024]{2,1,0:T(8,128)(2,1)S(1)} %all_to_all.33), kind=kOutput, calls=%fused_computation.10 | convolution fusion | flops 2147483648 | bytes 8388608 | tf_op jit(solution)/shard_map/dot_general | solution.py:43
  94.2 9.9 %convert_bitcast_fusion = bf16[128,1,8,1024]{3,2,1,0:T(8,128)(2,1)} fusion(bf16[1,1024,1024]{2,1,0:T(8,128)(2,1)} %param.12, f32[1024,1024]{1,0:T(8,128)} %fusion.3, bf16[1,1024,1024]{2,1,0:T(8,128)(2,1)} %param.11, bf16[128,8,1024]{2,1,0:T(8,128)(2,1)} %copy-done.2), kind=kOutput, calls=%fused_computation.15 | convolution fusion | flops 4302307328 | bytes 12582912 | tf_op jit(solution)/shard_map/dot_general | solution.py:46
  104.2 6.5 %all-to-all-start.1 = ((bf16[128,1,8,1024]{3,2,1,0:T(8,128)(2,1)}), bf16[128,1,8,1024]{3,2,1,0:T(8,128)(2,1)S(1)}, u32[]{:S(2)}, u32[]{:S(2)}) async-start(bf16[128,1,8,1024]{3,2,1,0:T(8,128)(2,1)} %convert_bitcast_fusion), calls=%async_computation.1 | async-start | bytes 4194304 | tf_op jit(solution)/shard_map/all_to_all | solution.py:49
  111.2 74.6 %all-to-all-done.1 = bf16[128,1,8,1024]{3,2,1,0:T(8,128)(2,1)S(1)} async-done(((bf16[128,1,8,1024]{3,2,1,0:T(8,128)(2,1)}), bf16[128,1,8,1024]{3,2,1,0:T(8,128)(2,1)S(1)}, u32[]{:S(2)}, u32[]{:S(2)}) %all-to-all-start.1) | async-done | bytes 2097184 | tf_op jit(solution)/shard_map/all_to_all | solution.py:49
  185.8 3.2 copy.61
  189.0 10.4 %all_to_all.34 = bf16[128,1,8,1024]{0,2,1,3:T(8,128)(2,1)S(1)} all-to-all(bf16[128,1,8,1024]{0,2,1,3:T(8,128)(2,1)} %copy.61), channel_id=1, replica_groups=mesh['expert'=128,'dp'=2] {'dp'}, dimensions={3} | all-to-all | bytes 4194304 | tf_op jit(solution)/shard_map/all_to_all | solution.py:48
  199.3 0.4 convert_reduce_fusion
  199.7 15.4 %copy.67 = f32[128,8,512]{1,0,2:T(8,128)} copy(f32[128,8,512]{0,1,2:T(8,128)S(1)} %convert_reduce_fusion) | data formatting | bytes 4194304
  215.1 49.5 %reduce_sum.83 = f32[64,8,512]{1,0,2:T(8,128)} reduce(f32[64,2,8,512]{2,1,0,3:T(2,128)} %bitcast.77, f32[]{:T(128)} %constant.65.clone.1), dimensions={1}, to_apply=%region_5.6 | reduce | flops 262144 | bytes 3145732 | tf_op jit(solution)/shard_map/reduce_sum | solution.py:55
  264.7 9.8 %copy.63 = f32[64,8,512]{2,1,0:T(8,128)S(1)} copy(f32[64,8,512]{1,0,2:T(8,128)} %reduce_sum.83) | data formatting | bytes 2097152 | tf_op jit(solution)/shard_map/reduce_sum | solution.py:55
  274.4 1.0 gather_fusion
  275.7 0.7 multiply_reduce_fusion
  276.4 0.7 convert_reduce_fusion.2
  277.1 1.0 broadcast_in_dim.48
  278.2 2.2 scatter_fusion
  280.3 6.2 %all-to-all-start.3 = ((bf16[128,8,512]{2,1,0:T(8,128)(2,1)}), bf16[128,8,512]{2,1,0:T(8,128)(2,1)S(1)}, u32[]{:S(2)}, u32[]{:S(2)}) async-start(bf16[128,8,512]{2,1,0:T(8,128)(2,1)} %scatter_fusion), calls=%async_computation.3 | async-start | bytes 2097152 | tf_op jit(solution)/shard_map/all_to_all | solution.py:77
  286.5 30.9 %all-to-all-done.3 = bf16[128,8,512]{2,1,0:T(8,128)(2,1)S(1)} async-done(((bf16[128,8,512]{2,1,0:T(8,128)(2,1)}), bf16[128,8,512]{2,1,0:T(8,128)(2,1)S(1)}, u32[]{:S(2)}, u32[]{:S(2)}) %all-to-all-start.3) | async-done | bytes 1048608 | tf_op jit(solution)/shard_map/all_to_all | solution.py:77
  317.5 0.3 copy.65
  317.8 6.1 %all_to_all.35 = bf16[128,8,512]{2,0,1:T(8,128)(2,1)S(1)} all-to-all(bf16[128,8,512]{2,0,1:T(8,128)(2,1)S(1)} %copy.65), channel_id=1, replica_groups=mesh['expert'=128,'dp'=2] {'dp'}, dimensions={1} | all-to-all | bytes 2097152 | tf_op jit(solution)/shard_map/all_to_all | solution.py:76
  324.2 59.1 %all-gather = bf16[256,1,1024]{2,1,0:T(2,128)(2,1)S(1)} all-gather(bf16[1,1,1024]{2,1,0:T(2,128)(2,1)S(1)} %reshape.137), channel_id=1, replica_groups=mesh['expert'=128,'dp'=2] {'expert','dp'}, dimensions={0}, use_global_device_ids=true | all-gather | bytes 526336 | tf_op jit(solution)/shard_map/all_gather | solution.py:87
  383.3 19.1 %fusion.29 = (f32[8192]{0:T(1024)S(1)}, f32[256,8192]{1,0:T(8,128)}) fusion(bf16[1024,8192]{0,1:T(8,128)(2,1)} %all-gather.3.cloned.1.call-done, bf16[256,1,1024]{2,1,0:T(2,128)(2,1)S(1)} %all-gather), kind=kOutput, calls=%fused_computation.59 | convolution fusion | flops 4297056256 | bytes 25722880 | tf_op jit(solution)/shard_map/dot_general | solution.py:90
  402.4 4.3 %broadcast_subtract_fusion = f32[256,8192]{1,0:T(8,128)S(1)} fusion(f32[256,8192]{1,0:T(8,128)} %get-tuple-element.5, f32[8192]{0:T(1024)S(1)} %broadcast_multiply_fusion), kind=kLoop, calls=%fused_computation.5 | loop fusion | flops 2097152 | bytes 16809984 | tf_op jit(solution)/shard_map/sub | solution.py:95
  406.8 5.9 %convolution_multiply_fusion = f32[32,8192]{1,0:T(8,128)} fusion(f32[256,8192]{1,0:T(8,128)S(1)} %broadcast_subtract_fusion, s32[]{:T(128)S(6)} %select_n.46), kind=kOutput, calls=%fused_computation.3 | convolution fusion | flops 805568512 | bytes 9568260 | tf_op jit(solution)/shard_map/dot_general | solution.py:98
  (41 shorter events, 2.1 us)
Async XLA Ops:
  7.2 82.8 %copy-start = (bf16[1,1024,1024]{2,1,0:T(8,128)(2,1)S(1)}, bf16[1,1024,1024]{2,1,0:T(8,128)(2,1)}, u32[]{:S(2)}) copy-start(bf16[1,1024,1024]{2,1,0:T(8,128)(2,1)} %param.10) | copy-start | bytes 6291460
  7.2 376.1 %all-gather.3.cloned.1.call-start = ((), (), s32[]{:S(2)}) async-start(), calls=%async_computation.5 | async-start | bytes 16842752 | tf_op jit(solution)/shard_map/all_gather | solution.py:92
  88.6 1.3 copy-start.2
  104.2 6.6 %copy-start.3 = (bf16[128,1024]{1,0:T(8,128)(2,1)S(1)}, bf16[128,1024]{1,0:T(8,128)(2,1)}, u32[]{:S(2)}) copy-start(bf16[128,1024]{1,0:T(8,128)(2,1)} %param.8) | copy-start | bytes 786436
  104.2 6.6 %copy-start.4 = (bf16[1024,64]{0,1:T(8,128)(2,1)S(1)}, bf16[1024,64]{0,1:T(8,128)(2,1)}, u32[]{:S(2)}) copy-start(bf16[1024,64]{0,1:T(8,128)(2,1)} %param.9) | copy-start | bytes 393220
  104.2 6.8 %copy-start.5 = (s32[128,2]{0,1:T(2,128)S(1)}, s32[128,2]{0,1:T(2,128)}, u32[]{:S(2)}) copy-start(s32[128,2]{0,1:T(2,128)} %param.14) | copy-start | bytes 3076
  104.2 7.0 %copy-start.6 = (s32[8]{0:T(128)S(1)}, s32[8]{0:T(128)}, u32[]{:S(2)}) copy-start(s32[8]{0:T(128)} %param.15) | copy-start | bytes 100
  104.2 81.6 %all-to-all-start.1 = ((bf16[128,1,8,1024]{3,2,1,0:T(8,128)(2,1)}), bf16[128,1,8,1024]{3,2,1,0:T(8,128)(2,1)S(1)}, u32[]{:S(2)}, u32[]{:S(2)}) async-start(bf16[128,1,8,1024]{3,2,1,0:T(8,128)(2,1)} %convert_bitcast_fusion), calls=%async_computation.1 | async-start | bytes 4194304 | tf_op jit(solution)/shard_map/all_to_all | solution.py:49
  280.3 37.1 %all-to-all-start.3 = ((bf16[128,8,512]{2,1,0:T(8,128)(2,1)}), bf16[128,8,512]{2,1,0:T(8,128)(2,1)S(1)}, u32[]{:S(2)}, u32[]{:S(2)}) async-start(bf16[128,8,512]{2,1,0:T(8,128)(2,1)} %scatter_fusion), calls=%async_computation.3 | async-start | bytes 2097152 | tf_op jit(solution)/shard_map/all_to_all | solution.py:77
  406.7 5.9 %copy-start.1 = (bf16[1,1024,1024]{2,1,0:T(8,128)(2,1)S(1)}, bf16[1,1024,1024]{2,1,0:T(8,128)(2,1)}, u32[]{:S(2)}) copy-start(bf16[1,1024,1024]{2,1,0:T(8,128)(2,1)} %param.10) | copy-start | bytes 6291460
Sparse Core Ops, SparseCore 0:
  11.7 173.9 all-gather.2
where the time goes:
time: 420 us; the launch traced here: 419 us
  blocking collectives  148 us (35%)
  waiting for transfers between devices  106 us (25%)
  other arithmetic  57.3 us (14%)
  local copies, waits for them, and re-layouts  41.1 us (10%)
  matrix products  39.4 us (9%)
  between operations  14.2 us (3%)
  starting transfers between devices  12.8 us (3%)
    all_to_all x1, waiting for transfers between devices, per_device(): lax.all_to_all(piece, 'expert', split_axis=0, concat_axis=0, tiled=True)  74.6 us
    all_to_all x1, blocking collectives, per_device(): lax.all_to_all(outgoing, 'expert', split_axis=0, concat_axis=0, tiled=True)  72.8 us
    all_gather x1, blocking collectives, per_device(): every_clip = lax.all_gather(clip_row, ('expert', 'dp'), axis=0, tiled=True)  59.1 us
    reduce_sum x2, other arithmetic, per_device(): jnp.sum(returned.reshape(experts, 2 * n_replica, capacity, half_width), a...  49.9 us
    all_to_all x1, waiting for transfers between devices, per_device(): lax.all_to_all(parcel, 'expert', split_axis=0, concat_axis=0, tiled=True)  30.9 us
    dot_general x1, matrix products, per_device(): jnp.dot(every_clip, lax.all_gather(expand_weight, ('expert', 'dp'), axis=...  19.1 us
    unnamed x17, local copies, waits for them, and re-layouts  17.6 us
    all_to_all x1, blocking collectives, per_device(): lax.all_to_all(lax.all_to_all(piece, 'expert', split_axis=0, concat_axis=...  10.4 us
  transfers between devices with their start and end apart: 3, of which 2 were waited for; matrix products, arithmetic and copies ran while one was open for 26% of the time, Pallas kernels for 0%

commit v1 on v0

v1 whole, which is shorter than its diff:
```python
import functools

import jax
import jax.numpy as jnp
from jax import lax
from jax.experimental import pallas as pl
from jax.experimental.pallas import tpu as pltpu
from jax.sharding import Mesh, PartitionSpec as P

EXP = ("x", "y", "z")
ALL = ("x", "y", "z", "dp")
F32 = jnp.float32
BF16 = jnp.bfloat16
LANES = 128
NT = (((1,), (1,)), ((), ()))
TN = (((0,), (0,)), ((), ()))


def dot(a, b):
    return jnp.dot(a, b, preferred_element_type=F32)


def dot_nt(a, b):
    return lax.dot_general(a, b, NT, preferred_element_type=F32)


def dot_tn(a, b):
    return lax.dot_general(a, b, TN, preferred_element_type=F32)


def split2(v):
    high = v.astype(BF16)
    return high, (v - high.astype(F32)).astype(BF16)


def half(start, size):
    return pl.ds(pl.multiple_of(start * size, LANES), size)


def prep_kernel(capacity, d_ref, tok_ref, router_ref, ids_ref, out_ref, high_ref, low_ref):
    d = d_ref[0]
    rows, width = tok_ref.shape
    experts = router_ref.shape[0]
    logits = dot_nt(router_ref[...], tok_ref[...])
    number = lax.broadcasted_iota(jnp.int32, (experts, rows), 0)
    hot0 = ids_ref[0:1, :] == number
    hot1 = ids_ref[1:2, :] == number
    chosen0 = jnp.sum(jnp.where(hot0, logits, 0.0), axis=0, keepdims=True)
    chosen1 = jnp.sum(jnp.where(hot1, logits, 0.0), axis=0, keepdims=True)
    gate = jnp.where(hot0, jax.nn.sigmoid(chosen0 - chosen1), 0.0) + jnp.where(
        hot1, jax.nn.sigmoid(chosen1 - chosen0), 0.0
    )
    member = jnp.where(hot0 | hot1, 1.0, 0.0)
    before = lax.broadcasted_iota(jnp.int32, (rows, rows), 0) < lax.broadcasted_iota(
        jnp.int32, (rows, rows), 1
    )
    earlier = dot(member.astype(BF16), jnp.where(before, 1.0, 0.0).astype(BF16))
    place = jnp.where(member > 0.0, earlier, -1.0)
    slots = lax.broadcasted_iota(jnp.int32, (experts, 2, capacity, rows), 2).astype(F32)
    taken = place[:, None, None, :] == slots
    picks = jnp.where(taken, 1.0, 0.0).reshape(experts * 2 * capacity, rows)
    weights = jnp.where(taken, gate[:, None, None, :], 0.0).reshape(experts * 2 * capacity, rows)
    high, low = split2(weights)
    high_ref[...] = high
    low_ref[...] = low
    out_ref[...] = dot(picks.astype(BF16), tok_ref[:, half(d, width // 2)]).astype(BF16)


def ffn_kernel(
    step_rows, d_ref, own_ref, other_ref, gate_ref, up_ref, down_hbm, out_ref, down_ref, hid_ref, sem
):
    d = d_ref[0]
    j = pl.program_id(0)
    steps = pl.num_programs(0)
    rows, part = own_ref.shape
    copy = pltpu.make_async_copy(down_hbm, down_ref, sem)

    @pl.when(j == 0)
    def _():
        copy.start()

    def hidden(m, carry):
        at = pl.ds(pl.multiple_of(m * step_rows, step_rows), step_rows)
        own, other = own_ref[at, :], other_ref[at, :]
        mine, theirs = half(d, part), half(1 - d, part)
        gate = dot(own, gate_ref[mine, :]) + dot(other, gate_ref[theirs, :])
        upper = dot(own, up_ref[mine, :]) + dot(other, up_ref[theirs, :])
        hid_ref[j, at, :] = (gate * jax.nn.sigmoid(gate) * upper).astype(BF16)
        return carry

    lax.fori_loop(0, rows // step_rows, hidden, 0)

    @pl.when(j == steps - 1)
    def _():
        copy.wait()
        block = hid_ref.shape[2]

        def down(m, carry):
            at = pl.ds(pl.multiple_of(m * step_rows, step_rows), step_rows)
            for which, cols in enumerate((half(1 - d, part), half(d, part))):
                total = dot(hid_ref[0, at, :], down_ref[0:block, cols])
                for s in range(1, hid_ref.shape[0]):
                    total = total + dot(hid_ref[s, at, :], down_ref[s * block : (s + 1) * block, cols])
                out_ref[which, at, :] = total.astype(BF16)
            return carry

        lax.fori_loop(0, rows // step_rows, down, 0)


def combine_kernel(d_ref, back_ref, high_ref, low_ref, tok_ref, slot_ref, mixed_ref, frames_ref):
    d = d_ref[0]
    rows, part = mixed_ref.shape
    count = slot_ref.shape[0]
    back = back_ref[...]
    moe = dot_tn(high_ref[...], back) + dot_tn(low_ref[...], back)
    mixed = (tok_ref[:, half(d, part)].astype(F32) + moe).astype(BF16)
    mixed_ref[...] = mixed
    length = rows // count
    frames = jnp.sum(mixed.astype(F32).reshape(count, length, part), axis=1) / length
    frames_ref[:, 0:part] = frames.astype(BF16)
    slot = slot_ref[...]
    lane = lax.broadcasted_iota(jnp.int32, (count, LANES), 1)
    digits = jnp.where(lane == 0, slot // 32, jnp.where(lane == 1, slot % 32, 0))
    frames_ref[:, part : part + LANES] = digits.astype(F32).astype(BF16)


def clip_kernel(length, frames_ref, digits_ref, clips_ref):
    clips, part = clips_ref.shape
    count = frames_ref.shape[0]
    digits = digits_ref[...].astype(F32)
    slot = digits[0:1, :] * 32.0 + digits[1:2, :]
    clip = jnp.floor(slot / length)
    number = lax.broadcasted_iota(jnp.int32, (clips, count), 0).astype(F32)
    picks = jnp.where(clip == number, 1.0, 0.0).astype(BF16)
    clips_ref[...] = (dot(picks, frames_ref[:, 0:part]) / length).astype(BF16)


def cov_kernel(d_ref, own_ref, other_ref, mine_ref, full_ref, out_ref, left_ref):
    d = d_ref[0]
    cols = mine_ref.shape[0]
    clips, part = own_ref.shape

    @pl.when(pl.program_id(0) == 0)
    def _():
        own, other = own_ref[...], other_ref[...]
        embed = dot_nt(mine_ref[:, half(d, part)], own) + dot_nt(mine_ref[:, half(1 - d, part)], other)
        centered = embed - jnp.mean(embed, axis=1, keepdims=True)
        high = centered.astype(BF16)
        rest = centered - high.astype(F32)
        middle = rest.astype(BF16)
        low = (rest - middle.astype(F32)).astype(BF16)
        for where, clip in ((half(d, part), own), (half(1 - d, part), other)):
            left = (dot(high, clip) + dot(middle, clip) + dot(low, clip)) / (clips - 1)
            left_high, left_low = split2(left)
            left_ref[0:cols, where] = left_high
            left_ref[cols : 2 * cols, where] = left_low

    both = dot_nt(left_ref[...], full_ref[...])
    out_ref[...] = both[0:cols] + both[cols : 2 * cols]


SCALAR = pl.BlockSpec(memory_space=pltpu.SMEM)


def per_device(
    tokens,
    router_weight,
    gate_weight,
    up_weight,
    down_weight,
    expand_weight,
    expert_ids,
    frame_slot,
):
    tok_rows, width = tokens.shape
    experts = router_weight.shape[1]
    n_expert = lax.axis_size(EXP)
    n_z = lax.axis_size("z")
    n_xy = n_expert // n_z
    capacity = 4 * tok_rows // experts
    part = width // 2
    hidden = gate_weight.shape[2]
    rows = n_expert * capacity
    count = frame_slot.shape[0]
    frame_total = count * n_expert
    clip_total = frame_total // 4
    share = expand_weight.shape[1]
    d = lax.axis_index("dp").astype(jnp.int32).reshape(1)
    swap = [(0, 1), (1, 0)]
    params = pltpu.CompilerParams(vmem_limit_bytes=48 * 2**20)

    mine = expand_weight.T
    full = lax.all_gather(mine, ALL, axis=0, tiled=True)

    vmem = pl.BlockSpec(memory_space=pltpu.VMEM)
    outgoing, high, low = pl.pallas_call(
        functools.partial(prep_kernel, capacity),
        out_shape=(
            jax.ShapeDtypeStruct((rows, part), BF16),
            jax.ShapeDtypeStruct((rows, tok_rows), BF16),
            jax.ShapeDtypeStruct((rows, tok_rows), BF16),
        ),
        in_specs=[SCALAR, vmem, vmem, vmem],
        out_specs=(vmem, vmem, vmem),
        compiler_params=params,
        name="prep",
    )(d, tokens, router_weight.T, expert_ids.T)

    received = lax.all_to_all(
        outgoing.reshape(n_expert, capacity, part), EXP, split_axis=0, concat_axis=0, tiled=True
    ).reshape(rows, part)
    other = lax.ppermute(received, "dp", swap)

    block = min(256, hidden)
    pieces = pl.pallas_call(
        functools.partial(ffn_kernel, 256),
        out_shape=jax.ShapeDtypeStruct((2, rows, part), BF16),
        grid=(hidden // block,),
        in_specs=[
            SCALAR,
            pl.BlockSpec((rows, part), lambda j: (0, 0)),
            pl.BlockSpec((rows, part), lambda j: (0, 0)),
            pl.BlockSpec((None, width, block), lambda j: (0, 0, j)),
            pl.BlockSpec((None, width, block), lambda j: (0, 0, j)),
            pl.BlockSpec(memory_space=pl.ANY),
        ],
        out_specs=pl.BlockSpec((2, rows, part), lambda j: (0, 0, 0)),
        scratch_shapes=[
            pltpu.VMEM((hidden, width), BF16),
            pltpu.VMEM((hidden // block, rows, block), BF16),
            pltpu.SemaphoreType.DMA(()),
        ],
        compiler_params=params,
        name="ffn",
    )(d, received, other, gate_weight, up_weight, down_weight.reshape(hidden, width))

    brought = lax.ppermute(pieces[0], "dp", swap)
    summed = (pieces[1].astype(F32) + brought.astype(F32)).astype(BF16)
    back = lax.all_to_all(
        summed.reshape(n_expert, capacity, part), EXP, split_axis=0, concat_axis=0, tiled=True
    ).reshape(rows, part)

    mixed, frames = pl.pallas_call(
        combine_kernel,
        out_shape=(
            jax.ShapeDtypeStruct((tok_rows, part), BF16),
            jax.ShapeDtypeStruct((count, part + LANES), BF16),
        ),
        in_specs=[SCALAR, vmem, vmem, vmem, vmem, vmem],
        out_specs=(vmem, vmem),
        compiler_params=params,
        name="combine",
    )(d, back, high, low, tokens, frame_slot.reshape(count, 1))

    def spread(block, axes, size):
        copies = jnp.broadcast_to(block[None], (size,) + block.shape)
        out = lax.all_to_all(copies, axes, split_axis=0, concat_axis=0, tiled=True)
        return out.reshape(-1, block.shape[-1])

    gathered = spread(spread(frames, "z", n_z), ("x", "y"), n_xy)
    digits = gathered[:, part : part + 8].T
    clips = pl.pallas_call(
        functools.partial(clip_kernel, 4),
        out_shape=jax.ShapeDtypeStruct((clip_total, part), BF16),
        in_specs=[vmem, vmem],
        out_specs=vmem,
        compiler_params=params,
        name="clips",
    )(gathered, digits)
    other_clips = lax.ppermute(clips, "dp", swap)

    total_cols = full.shape[0]
    wide = 1024
    whole = lambda shape: pl.BlockSpec(shape, lambda j: (0,) * len(shape))
    covariance = pl.pallas_call(
        cov_kernel,
        out_shape=jax.ShapeDtypeStruct((share, total_cols), F32),
        grid=(total_cols // wide,),
        in_specs=[
            SCALAR,
            whole((clip_total, part)),
            whole((clip_total, part)),
            whole((share, width)),
            pl.BlockSpec((wide, width), lambda j: (j, 0)),
        ],
        out_specs=pl.BlockSpec((share, wide), lambda j: (0, j)),
        scratch_shapes=[pltpu.VMEM((2 * share, width), BF16)],
        compiler_params=params,
        name="covariance",
    )(d, clips, other_clips, mine, full)
    return mixed, covariance


def solution(mesh):
    grid = Mesh(mesh.devices.reshape(4, 4, 8, 2), ALL)
    return jax.shard_map(
        per_device,
        mesh=grid,
        in_specs=(
            P(EXP, None),
            P(),
            P(EXP, None, "dp"),
            P(EXP, None, "dp"),
            P(EXP, "dp", None),
            P(None, ALL),
            P(EXP, None),
            P(EXP),
        ),
        out_specs=(P(EXP, "dp"), P(ALL, None)),
        check_vma=False,
    )
```

time: 420 us -> 177 us (0.42)
  blocking collectives: 148 us -> 80.2 us
  waiting for transfers between devices: 106 us -> 38.6 us
  other arithmetic: 57.3 us -> 1.29 us
  matrix products: 39.4 us -> 0 us
  local copies, waits for them, and re-layouts: 41.1 us -> 2.97 us
  Pallas kernels: 0 us -> 26 us
    all_to_all x2 -> x1, waiting for transfers between devices: 105 us -> 32.2 us  [per_device(): lax.all_to_all(summed.reshape(n_expert, capacity, part), EXP, split_axis=...]
    all_gather x1 -> x0, blocking collectives: 59.1 us -> none  [per_device(): every_clip = lax.all_gather(clip_row, ('expert', 'dp'), axis=0, tiled=True)]
    reduce_sum x8 -> x0, other arithmetic: 51.6 us -> none  [the longest x2 49.9 us: per_device(): jnp.sum(returned.reshape(experts, 2 * n_replica, capacity, half_width), a...]
    dot_general x5 -> x0, matrix products: 39.4 us -> none  [the longest x1 19.1 us: per_device(): jnp.dot(every_clip, lax.all_gather(expand_weight, ('expert', 'dp'), axis=...]
    pallas_call x0 -> x5, Pallas kernels: none -> 26 us  [the longest x1 12.4 us: per_device(): pl.pallas_call(cov_kernel, out_shape=jax.ShapeDtypeStruct((share, total_c...]
    unnamed x17 -> x13, local copies, waits for them, and re-layouts: 17.6 us -> 2.65 us
    reduce_sum x2 -> x0, local copies, waits for them, and re-layouts: 9.78 us -> none  [the longest x1 9.77 us: per_device(): jnp.sum(returned.reshape(experts, 2 * n_replica, capacity, half_width), a...]
    all_to_all x3, blocking collectives: 89.3 us -> 80.2 us  [the longest x1 47.9 us: per_device(): lax.all_to_all(outgoing.reshape(n_expert, capacity, part), EXP, split_axi...]
  transfers between devices with their start and end apart: 3 -> 5, of which waited for: 2 -> 4; matrix products, arithmetic and copies ran while one was open for 26% -> 1% of each run, Pallas kernels for 0% -> 8%
where the time goes in v1:
time: 177 us; the launch traced here: 176 us
  blocking collectives  80.2 us (45%)
  waiting for transfers between devices  38.6 us (22%)
  Pallas kernels  26 us (15%)
  between operations  14.1 us (8%)
  starting transfers between devices  12.8 us (7%)
  local copies, waits for them, and re-layouts  2.97 us (2%)
    all_to_all x1, blocking collectives, per_device(): lax.all_to_all(outgoing.reshape(n_expert, capacity, part), EXP, split_axi...  47.9 us
    all_to_all x2, blocking collectives, spread(): out = lax.all_to_all(copies, axes, split_axis=0, concat_axis=0, tiled=True)  32.3 us
    all_to_all x1, waiting for transfers between devices, per_device(): lax.all_to_all(summed.reshape(n_expert, capacity, part), EXP, split_axis=...  32.2 us
    pallas_call x1, Pallas kernels, per_device(): pl.pallas_call(cov_kernel, out_shape=jax.ShapeDtypeStruct((share, total_c...  12.4 us
    pallas_call x1, Pallas kernels, per_device(): pl.pallas_call(functools.partial(ffn_kernel, 256), out_shape=jax.ShapeDty...  11.4 us
    all_to_all x1, starting transfers between devices, per_device(): lax.all_to_all(summed.reshape(n_expert, capacity, part), EXP, split_axis=...  6.19 us
  transfers between devices with their start and end apart: 5, of which 4 were waited for; matrix products, arithmetic and copies ran while one was open for 1% of the time, Pallas kernels for 8%

profile of v1, /device:TPU:1, one launch (start us, length us, event | category | flops | bytes accessed | tf_op | source)
XLA Modules:
  0.0 176.0 jit_solution(3910522622363230355)
XLA Ops:
  7.2 0.0 all-gather.2.cloned.1.call-start
  7.2 0.7 all-gather.2.cloned.1.call-update
  7.9 0.0 copy-start
  7.9 0.9 copy-done
  8.9 0.9 copy-done.3
  9.8 0.7 copy-done.4
  10.4 0.6 prep.1
  11.1 47.9 %all_to_all.20 = bf16[128,8,512]{2,1,0:T(8,128)(2,1)S(1)} all-to-all(bf16[128,8,512]{2,1,0:T(8,128)(2,1)S(1)} %bitcast.26), channel_id=1, replica_groups=mesh['x'=4,'y'=4,'z'=8,'dp'=2] {'x','y','z'}, dimensions={0} | all-to-all | bytes 2097152 | tf_op jit(solution)/shard_map/all_to_all | solution.py:209
  58.9 2.7 %collective-permute-start = (bf16[1024,512]{1,0:T(8,128)(2,1)S(1)}, bf16[1024,512]{1,0:T(8,128)(2,1)S(1)}, u32[]{:S(2)}, u32[]{:S(2)}) collective-permute-start(bf16[1024,512]{1,0:T(8,128)(2,1)S(1)} %bitcast.24), channel_id=1, source_target_pairs={{0,1},{1,0},{2,3},{3,2},{4,5},{5,4},{6,7},{7,6},{8,9},{9,8},{10,11... | collective-permute-start | bytes 3145736 | tf_op jit(solution)/shard_map/ppermute | solution.py:212
  61.6 2.3 %collective-permute-done.other_ref = bf16[1024,512]{1,0:T(8,128)(2,1)S(1)} collective-permute-done((bf16[1024,512]{1,0:T(8,128)(2,1)S(1)}, bf16[1024,512]{1,0:T(8,128)(2,1)S(1)}, u32[]{:S(2)}, u32[]{:S(2)}) %collective-permute-start) | collective-permute-done | bytes 1048608 | tf_op jit(solution)/shard_map/ppermute | solution.py:212
  63.9 11.4 %ffn.1 = bf16[2,1024,512]{2,1,0:T(8,128)(2,1)S(1)} custom-call(s32[1]{0:T(128)} %bitcast.d_ref, bf16[1024,512]{1,0:T(8,128)(2,1)S(1)} %bitcast.25, bf16[1024,512]{1,0:T(8,128)(2,1)S(1)} %collective-permute-done.other_ref, bf16[1,1024,1024]{2,1,0:T(8,128)(2,1)} %gate_ref.1, bf16[1,1024,1024]{2,1,0:T(8,128)(2,1)} %up_ref.1, bf16[1024,1024]{1,0:T(8,128)(2,1)} %bitcast.32), custom_call_target="tpu_custom_call" | custom-call | tf_op jit(solution)/shard_map/ffn/pallas_call | solution.py:215
  75.3 0.1 slice_bitcast_fusion
  75.4 0.0 copy-start.5
  75.4 0.0 copy-start.1
  75.4 0.5 collective-permute-start.1
  75.9 2.3 %collective-permute-done.1 = bf16[1024,512]{1,0:T(8,128)(2,1)S(1)} collective-permute-done((bf16[1024,512]{1,0:T(8,128)(2,1)S(1)}, bf16[1024,512]{1,0:T(8,128)(2,1)S(1)}, u32[]{:S(2)}, u32[]{:S(2)}) %collective-permute-start.1) | collective-permute-done | bytes 1048608 | tf_op jit(solution)/shard_map/ppermute | solution.py:237
  78.2 1.3 fusion.1
  79.4 6.2 %all-to-all-start.1 = ((bf16[128,8,512]{2,1,0:T(8,128)(2,1)}), bf16[128,8,512]{2,1,0:T(8,128)(2,1)S(1)}, u32[]{:S(2)}, u32[]{:S(2)}) async-start(bf16[128,8,512]{2,1,0:T(8,128)(2,1)} %fusion.1), calls=%async_computation.1 | async-start | bytes 2097152 | tf_op jit(solution)/shard_map/all_to_all | solution.py:239
  85.6 0.0 copy-done.5
  85.6 0.1 copy.13.slot_ref
  85.7 32.2 %all-to-all-done.1 = bf16[128,8,512]{2,1,0:T(8,128)(2,1)S(1)} async-done(((bf16[128,8,512]{2,1,0:T(8,128)(2,1)}), bf16[128,8,512]{2,1,0:T(8,128)(2,1)S(1)}, u32[]{:S(2)}, u32[]{:S(2)}) %all-to-all-start.1) | async-done | bytes 1048608 | tf_op jit(solution)/shard_map/all_to_all | solution.py:239
  117.9 0.0 copy-done.1
  117.9 1.2 combine.1
  119.1 12.3 %all_to_all.21 = bf16[8,8,640]{2,1,0:T(8,128)(2,1)S(1)} all-to-all(bf16[8,8,640]{2,1,0:T(8,128)(2,1)S(1)} %broadcast_in_dim.6), channel_id=1, replica_groups=mesh['x'=4,'y'=4,'z'=8,'dp'=2] {'z'}, dimensions={0} | all-to-all | bytes 163840 | tf_op jit(solution)/shard_map/all_to_all | solution.py:257
  131.4 0.1 broadcast_in_dim.15
  131.5 0.0 copy-start.2
  131.5 20.1 %all_to_all.22 = bf16[16,64,640]{2,1,0:T(8,128)(2,1)S(1)} all-to-all(bf16[16,64,640]{2,1,0:T(8,128)(2,1)S(1)} %broadcast_in_dim.15), channel_id=1, replica_groups=mesh['x'=4,'y'=4,'z'=8,'dp'=2] {'x','y'}, dimensions={0} | all-to-all | bytes 2621440 | tf_op jit(solution)/shard_map/all_to_all | solution.py:257
  151.6 0.1 copy.15
  151.7 0.4 clips.1.own_ref
  152.2 3.4 %collective-permute-start.2 = (bf16[256,512]{1,0:T(8,128)(2,1)S(1)}, bf16[256,512]{1,0:T(8,128)(2,1)S(1)}, u32[]{:S(2)}, u32[]{:S(2)}) collective-permute-start(bf16[256,512]{1,0:T(8,128)(2,1)S(1)} %clips.1.own_ref), channel_id=1, source_target_pairs={{0,1},{1,0},{2,3},{3,2},{4,5},{5,4},{6,7},{7,6},{8,9},{9,8},{10,11... | collective-permute-start | bytes 786440 | tf_op jit(solution)/shard_map/ppermute | solution.py:270
  155.6 1.2 collective-permute-done.2.other_ref
  156.8 12.4 %covariance.1 = f32[32,8192]{1,0:T(8,128)} custom-call(s32[1]{0:T(128)} %bitcast.d_ref, bf16[256,512]{1,0:T(8,128)(2,1)S(1)} %clips.1.own_ref, bf16[256,512]{1,0:T(8,128)(2,1)S(1)} %collective-permute-done.2.other_ref, bf16[32,1024]{1,0:T(8,128)(2,1)S(1)} %bitcast.28, bf16[8192,1024]{1,0:T(8,128)(2,1)} %all-gather.2.cloned.1.call-done.full_ref), custom_call_target="tpu_custom_call" | custom-call | tf_op jit(solution)/shard_map/covariance/pallas_call | solution.py:275
  (6 shorter events, 0.0 us)
Async XLA Ops:
  7.2 149.6 %all-gather.2.cloned.1.call-start = ((), (), s32[]{:S(2)}) async-start(), calls=%async_computation.4 | async-start | bytes 16842752 | tf_op jit(solution)/shard_map/all_gather | solution.py:193
  7.9 1.0 copy-start
  8.9 0.9 copy-start.3
  9.8 0.7 copy-start.4
  58.9 5.0 %collective-permute-start = (bf16[1024,512]{1,0:T(8,128)(2,1)S(1)}, bf16[1024,512]{1,0:T(8,128)(2,1)S(1)}, u32[]{:S(2)}, u32[]{:S(2)}) collective-permute-start(bf16[1024,512]{1,0:T(8,128)(2,1)S(1)} %bitcast.24), channel_id=1, source_target_pairs={{0,1},{1,0},{2,3},{3,2},{4,5},{5,4},{6,7},{7,6},{8,9},{9,8},{10,11... | collective-permute-start | bytes 3145736 | tf_op jit(solution)/shard_map/ppermute | solution.py:212
  75.4 10.3 %copy-start.5 = (s32[8]{0:T(128)S(1)}, s32[8]{0:T(128)}, u32[]{:S(2)}) copy-start(s32[8]{0:T(128)} %param.15) | copy-start | bytes 100
  75.4 42.5 %copy-start.1 = (bf16[128,1024]{1,0:T(8,128)(2,1)S(1)}, bf16[128,1024]{1,0:T(8,128)(2,1)}, u32[]{:S(2)}) copy-start(bf16[128,1024]{1,0:T(8,128)(2,1)} %tok_ref.3) | copy-start | bytes 786436
  75.4 2.7 %collective-permute-start.1 = (bf16[1024,512]{1,0:T(8,128)(2,1)S(1)}, bf16[1024,512]{1,0:T(8,128)(2,1)S(1)}, u32[]{:S(2)}, u32[]{:S(2)}) collective-permute-start(bf16[1024,512]{1,0:T(8,128)(2,1)S(1)} %slice_bitcast_fusion), channel_id=1, source_target_pairs={{0,1},{1,0},{2,3},{3,2},{4,5},{5,4},{6,7},{7,6},{8,9},{9,8},{10,11... | collective-permute-start | bytes 3145736 | tf_op jit(solution)/shard_map/ppermute | solution.py:237
  79.4 38.5 %all-to-all-start.1 = ((bf16[128,8,512]{2,1,0:T(8,128)(2,1)}), bf16[128,8,512]{2,1,0:T(8,128)(2,1)S(1)}, u32[]{:S(2)}, u32[]{:S(2)}) async-start(bf16[128,8,512]{2,1,0:T(8,128)(2,1)} %fusion.1), calls=%async_computation.1 | async-start | bytes 2097152 | tf_op jit(solution)/shard_map/all_to_all | solution.py:239
  131.5 25.3 %copy-start.2 = (bf16[1024,32]{0,1:T(8,128)(2,1)S(1)}, bf16[1024,32]{0,1:T(8,128)(2,1)}, u32[]{:S(2)}) copy-start(bf16[1024,32]{0,1:T(8,128)(2,1)} %param.13) | copy-start | bytes 196612
  152.2 4.6 %collective-permute-start.2 = (bf16[256,512]{1,0:T(8,128)(2,1)S(1)}, bf16[256,512]{1,0:T(8,128)(2,1)S(1)}, u32[]{:S(2)}, u32[]{:S(2)}) collective-permute-start(bf16[256,512]{1,0:T(8,128)(2,1)S(1)} %clips.1.own_ref), channel_id=1, source_target_pairs={{0,1},{1,0},{2,3},{3,2},{4,5},{5,4},{6,7},{7,6},{8,9},{9,8},{10,11... | collective-permute-start | bytes 786440 | tf_op jit(solution)/shard_map/ppermute | solution.py:270
Sparse Core Ops, SparseCore 0:
  11.7 135.8 all-gather.1

commit v2 on v1

--- a/solution.py
+++ b/solution.py
@@ -37,7 +37,19 @@
     return pl.ds(pl.multiple_of(start * size, LANES), size)
 
 
-def prep_kernel(capacity, d_ref, tok_ref, router_ref, ids_ref, out_ref, high_ref, low_ref):
+def prep_kernel(
+    capacity, d_ref, tok_hbm, router_hbm, ids_hbm, out_ref, high_ref, low_ref, tok_ref, router_ref, ids_ref, sems
+):
+    copies = [
+        pltpu.make_async_copy(source, target, sems.at[k])
+        for k, (source, target) in enumerate(
+            ((tok_hbm, tok_ref), (router_hbm, router_ref), (ids_hbm, ids_ref))
+        )
+    ]
+    for copy in copies:
+        copy.start()
+    for copy in copies:
+        copy.wait()
     d = d_ref[0]
     rows, width = tok_ref.shape
     experts = router_ref.shape[0]
@@ -67,44 +79,57 @@
 
 
 def ffn_kernel(
-    step_rows, d_ref, own_ref, other_ref, gate_ref, up_ref, down_hbm, out_ref, down_ref, hid_ref, sem
+    step, d_ref, own_ref, other_ref, gate_hbm, up_hbm, down_hbm, hid_ref, out_ref, x_ref, gate_ref, up_ref, down_ref, sems, down_sem
 ):
     d = d_ref[0]
-    j = pl.program_id(0)
-    steps = pl.num_programs(0)
     rows, part = own_ref.shape
-    copy = pltpu.make_async_copy(down_hbm, down_ref, sem)
-
-    @pl.when(j == 0)
-    def _():
-        copy.start()
-
-    def hidden(m, carry):
-        at = pl.ds(pl.multiple_of(m * step_rows, step_rows), step_rows)
-        own, other = own_ref[at, :], other_ref[at, :]
-        mine, theirs = half(d, part), half(1 - d, part)
-        gate = dot(own, gate_ref[mine, :]) + dot(other, gate_ref[theirs, :])
-        upper = dot(own, up_ref[mine, :]) + dot(other, up_ref[theirs, :])
-        hid_ref[j, at, :] = (gate * jax.nn.sigmoid(gate) * upper).astype(BF16)
+    blocks = sems.shape[1]
+    block = gate_ref.shape[1] // blocks
+    spans = [slice(k * block, (k + 1) * block) for k in range(blocks)]
+    loads = [
+        [
+            pltpu.make_async_copy(source.at[:, span], target.at[:, span], sems.at[w, k])
+            for w, (source, target) in enumerate(((gate_hbm, gate_ref), (up_hbm, up_ref)))
+        ]
+        for k, span in enumerate(spans)
+    ]
+    load_down = pltpu.make_async_copy(down_hbm, down_ref, down_sem)
+    for pair in loads:
+        for load in pair:
+            load.start()
+    load_down.start()
+    x_ref[:, half(d, part)] = own_ref[...]
+    x_ref[:, half(1 - d, part)] = other_ref[...]
+
+    for pair, span in zip(loads, spans):
+        for load in pair:
+            load.wait()
+
+        def body(m, carry, span=span):
+            at = pl.ds(pl.multiple_of(m * step, step), step)
+            gate = dot(x_ref[at, :], gate_ref[:, span])
+            upper = dot(x_ref[at, :], up_ref[:, span])
+            hid_ref[at, span] = (gate * jax.nn.sigmoid(gate) * upper).astype(BF16)
+            return carry
+
+        lax.fori_loop(0, rows // step, body, 0)
+
+    load_down.wait()
+
+    def last(m, carry):
+        at = pl.ds(pl.multiple_of(m * step, step), step)
+        out_ref[at, :] = dot(hid_ref[at, :], down_ref[:, half(1 - d, part)]).astype(BF16)
         return carry
 
-    lax.fori_loop(0, rows // step_rows, hidden, 0)
-
-    @pl.when(j == steps - 1)
-    def _():
-        copy.wait()
-        block = hid_ref.shape[2]
-
-        def down(m, carry):
-            at = pl.ds(pl.multiple_of(m * step_rows, step_rows), step_rows)
-            for which, cols in enumerate((half(1 - d, part), half(d, part))):
-                total = dot(hid_ref[0, at, :], down_ref[0:block, cols])
-                for s in range(1, hid_ref.shape[0]):
-                    total = total + dot(hid_ref[s, at, :], down_ref[s * block : (s + 1) * block, cols])
-                out_ref[which, at, :] = total.astype(BF16)
-            return carry
-
-        lax.fori_loop(0, rows // step_rows, down, 0)
+    lax.fori_loop(0, rows // step, last, 0)
+
+
+def own_kernel(d_ref, hid_ref, down_ref, out_ref):
+    out_ref[...] = dot(hid_ref[...], down_ref[:, half(d_ref[0], out_ref.shape[1])])
+
+
+def add_kernel(own_ref, brought_ref, out_ref):
+    out_ref[...] = (own_ref[...] + brought_ref[...].astype(F32)).astype(BF16)
 
 
 def combine_kernel(d_ref, back_ref, high_ref, low_ref, tok_ref, slot_ref, mixed_ref, frames_ref):
@@ -135,28 +160,44 @@
     clips_ref[...] = (dot(picks, frames_ref[:, 0:part]) / length).astype(BF16)
 
 
-def cov_kernel(d_ref, own_ref, other_ref, mine_ref, full_ref, out_ref, left_ref):
+def cov_kernel(
+    d_ref, own_ref, other_ref, mine_ref, full_hbm, out_hbm, left_ref, full_ref, out_ref, in_sems, out_sems
+):
     d = d_ref[0]
     cols = mine_ref.shape[0]
     clips, part = own_ref.shape
-
-    @pl.when(pl.program_id(0) == 0)
-    def _():
-        own, other = own_ref[...], other_ref[...]
-        embed = dot_nt(mine_ref[:, half(d, part)], own) + dot_nt(mine_ref[:, half(1 - d, part)], other)
-        centered = embed - jnp.mean(embed, axis=1, keepdims=True)
-        high = centered.astype(BF16)
-        rest = centered - high.astype(F32)
-        middle = rest.astype(BF16)
-        low = (rest - middle.astype(F32)).astype(BF16)
-        for where, clip in ((half(d, part), own), (half(1 - d, part), other)):
-            left = (dot(high, clip) + dot(middle, clip) + dot(low, clip)) / (clips - 1)
-            left_high, left_low = split2(left)
-            left_ref[0:cols, where] = left_high
-            left_ref[cols : 2 * cols, where] = left_low
-
-    both = dot_nt(left_ref[...], full_ref[...])
-    out_ref[...] = both[0:cols] + both[cols : 2 * cols]
+    blocks = in_sems.shape[0]
+    wide = full_ref.shape[0] // blocks
+    spans = [slice(k * wide, (k + 1) * wide) for k in range(blocks)]
+    loads = [
+        pltpu.make_async_copy(full_hbm.at[span, :], full_ref.at[span, :], in_sems.at[k])
+        for k, span in enumerate(spans)
+    ]
+    stores = [
+        pltpu.make_async_copy(out_ref.at[:, span], out_hbm.at[:, span], out_sems.at[k])
+        for k, span in enumerate(spans)
+    ]
+    for load in loads:
+        load.start()
+    own, other = own_ref[...], other_ref[...]
+    embed = dot_nt(mine_ref[:, half(d, part)], own) + dot_nt(mine_ref[:, half(1 - d, part)], other)
+    centered = embed - jnp.mean(embed, axis=1, keepdims=True)
+    high = centered.astype(BF16)
+    rest = centered - high.astype(F32)
+    middle = rest.astype(BF16)
+    low = (rest - middle.astype(F32)).astype(BF16)
+    for where, clip in ((half(d, part), own), (half(1 - d, part), other)):
+        left = (dot(high, clip) + dot(middle, clip) + dot(low, clip)) / (clips - 1)
+        left_high, left_low = split2(left)
+        left_ref[0:cols, where] = left_high
+        left_ref[cols : 2 * cols, where] = left_low
+    for load, store, span in zip(loads, stores, spans):
+        load.wait()
+        both = dot_nt(left_ref[...], full_ref[span, :])
+        out_ref[:, span] = both[0:cols] + both[cols : 2 * cols]
+        store.start()
+    for store in stores:
+        store.wait()
 
 
 SCALAR = pl.BlockSpec(memory_space=pltpu.SMEM)
@@ -187,12 +228,13 @@
     share = expand_weight.shape[1]
     d = lax.axis_index("dp").astype(jnp.int32).reshape(1)
     swap = [(0, 1), (1, 0)]
-    params = pltpu.CompilerParams(vmem_limit_bytes=48 * 2**20)
+    params = pltpu.CompilerParams(vmem_limit_bytes=16 * 2**20)
 
     mine = expand_weight.T
     full = lax.all_gather(mine, ALL, axis=0, tiled=True)
 
     vmem = pl.BlockSpec(memory_space=pltpu.VMEM)
+    hbm = pl.BlockSpec(memory_space=pl.ANY)
     outgoing, high, low = pl.pallas_call(
         functools.partial(prep_kernel, capacity),
         out_shape=(
@@ -200,9 +242,15 @@
             jax.ShapeDtypeStruct((rows, tok_rows), BF16),
             jax.ShapeDtypeStruct((rows, tok_rows), BF16),
         ),
-        in_specs=[SCALAR, vmem, vmem, vmem],
+        in_specs=[SCALAR, hbm, hbm, hbm],
         out_specs=(vmem, vmem, vmem),
-        compiler_params=params,
+        scratch_shapes=[
+            pltpu.VMEM(tokens.shape, BF16),
+            pltpu.VMEM((experts, width), BF16),
+            pltpu.VMEM((2, tok_rows), jnp.int32),
+            pltpu.SemaphoreType.DMA((3,)),
+        ],
+        compiler_params=pltpu.CompilerParams(vmem_limit_bytes=57 * 2**20),
         name="prep",
     )(d, tokens, router_weight.T, expert_ids.T)
 
@@ -211,31 +259,48 @@
     ).reshape(rows, part)
     other = lax.ppermute(received, "dp", swap)
 
-    block = min(256, hidden)
-    pieces = pl.pallas_call(
-        functools.partial(ffn_kernel, 256),
-        out_shape=jax.ShapeDtypeStruct((2, rows, part), BF16),
-        grid=(hidden // block,),
-        in_specs=[
-            SCALAR,
-            pl.BlockSpec((rows, part), lambda j: (0, 0)),
-            pl.BlockSpec((rows, part), lambda j: (0, 0)),
-            pl.BlockSpec((None, width, block), lambda j: (0, 0, j)),
-            pl.BlockSpec((None, width, block), lambda j: (0, 0, j)),
-            pl.BlockSpec(memory_space=pl.ANY),
-        ],
-        out_specs=pl.BlockSpec((2, rows, part), lambda j: (0, 0, 0)),
+    w_down = down_weight.reshape(hidden, width)
+    inner, theirs = pl.pallas_call(
+        functools.partial(ffn_kernel, 512),
+        out_shape=(
+            jax.ShapeDtypeStruct((rows, hidden), BF16),
+            jax.ShapeDtypeStruct((rows, part), BF16),
+        ),
+        in_specs=[SCALAR, vmem, vmem, hbm, hbm, hbm],
+        out_specs=(vmem, vmem),
         scratch_shapes=[
+            pltpu.VMEM((rows, width), BF16),
+            pltpu.VMEM((width, hidden), BF16),
+            pltpu.VMEM((width, hidden), BF16),
             pltpu.VMEM((hidden, width), BF16),
-            pltpu.VMEM((hidden // block, rows, block), BF16),
+            pltpu.SemaphoreType.DMA((2, 4)),
             pltpu.SemaphoreType.DMA(()),
         ],
+        compiler_params=pltpu.CompilerParams(vmem_limit_bytes=48 * 2**20),
+        cost_estimate=pl.CostEstimate(
+            flops=2 * rows * hidden * (2 * width + part), bytes_accessed=0, transcendentals=0
+        ),
+        name="ffn",
+    )(d, received, other, gate_weight.reshape(width, hidden), up_weight.reshape(width, hidden), w_down)
+
+    brought = lax.ppermute(theirs, "dp", swap)
+    ours = pl.pallas_call(
+        own_kernel,
+        out_shape=jax.ShapeDtypeStruct((rows, part), F32),
+        in_specs=[SCALAR, vmem, vmem],
+        out_specs=vmem,
         compiler_params=params,
-        name="ffn",
-    )(d, received, other, gate_weight, up_weight, down_weight.reshape(hidden, width))
-
-    brought = lax.ppermute(pieces[0], "dp", swap)
-    summed = (pieces[1].astype(F32) + brought.astype(F32)).astype(BF16)
+        cost_estimate=pl.CostEstimate(flops=2 * rows * hidden * part, bytes_accessed=0, transcendentals=0),
+        name="ours",
+    )(d, inner, w_down)
+    summed = pl.pallas_call(
+        add_kernel,
+        out_shape=jax.ShapeDtypeStruct((rows, part), BF16),
+        in_specs=[vmem, vmem],
+        out_specs=vmem,
+        compiler_params=params,
+        name="total",
+    )(ours, brought)
     back = lax.all_to_all(
         summed.reshape(n_expert, capacity, part), EXP, split_axis=0, concat_axis=0, tiled=True
     ).reshape(rows, part)
@@ -270,22 +335,20 @@
     other_clips = lax.ppermute(clips, "dp", swap)
 
     total_cols = full.shape[0]
-    wide = 1024
-    whole = lambda shape: pl.BlockSpec(shape, lambda j: (0,) * len(shape))
+    blocks = 8
     covariance = pl.pallas_call(
         cov_kernel,
         out_shape=jax.ShapeDtypeStruct((share, total_cols), F32),
-        grid=(total_cols // wide,),
-        in_specs=[
-            SCALAR,
-            whole((clip_total, part)),
-            whole((clip_total, part)),
-            whole((share, width)),
-            pl.BlockSpec((wide, width), lambda j: (j, 0)),
+        in_specs=[SCALAR, vmem, vmem, vmem, hbm],
+        out_specs=hbm,
+        scratch_shapes=[
+            pltpu.VMEM((2 * share, width), BF16),
+            pltpu.VMEM((total_cols, width), BF16),
+            pltpu.VMEM((share, total_cols), F32),
+            pltpu.SemaphoreType.DMA((blocks,)),
+            pltpu.SemaphoreType.DMA((blocks,)),
         ],
-        out_specs=pl.BlockSpec((share, wide), lambda j: (0, j)),
-        scratch_shapes=[pltpu.VMEM((2 * share, width), BF16)],
-        compiler_params=params,
+        compiler_params=pltpu.CompilerParams(vmem_limit_bytes=48 * 2**20),
         name="covariance",
     )(d, clips, other_clips, mine, full)
     return mixed, covariance

time: 177 us -> 170 us (0.960)
  local copies, waits for them, and re-layouts: 2.97 us -> 0.38 us
    pallas_call x1, Pallas kernels: 12.4 us -> 9.32 us  [per_device(): pl.pallas_call(cov_kernel, out_shape=jax.ShapeDtypeStruct((share, total_c...]
    unnamed x13, local copies, waits for them, and re-layouts: 2.65 us -> 0.13 us
    pallas_call x1, Pallas kernels: 0.63 us -> 2.61 us  [per_device(): pl.pallas_call(functools.partial(prep_kernel, capacity), out_shape=(jax.S...]
    pallas_call x1 -> x3, Pallas kernels: 11.4 us -> 11.1 us  [the longest x1 8.68 us: per_device(): pl.pallas_call(functools.partial(ffn_kernel, 512), out_shape=(jax.ShapeDt...]
  transfers between devices with their start and end apart: 5 -> 5, of which waited for: 4 -> 4; matrix products, arithmetic and copies ran while one was open for 1% -> 0% of each run, Pallas kernels for 8% -> 9%
where the time goes in v2:
time: 170 us
  blocking collectives  78.8 us (46%)
  waiting for transfers between devices  38.6 us (23%)
  Pallas kernels  24.6 us (14%)
  between operations  14.1 us (8%)
  starting transfers between devices  13.1 us (8%)
    all_to_all x1, blocking collectives, per_device(): lax.all_to_all(outgoing.reshape(n_expert, capacity, part), EXP, split_axi...  48 us
    all_to_all x1, waiting for transfers between devices, per_device(): lax.all_to_all(summed.reshape(n_expert, capacity, part), EXP, split_axis=...  33.4 us
    all_to_all x2, blocking collectives, spread(): out = lax.all_to_all(copies, axes, split_axis=0, concat_axis=0, tiled=True)  30.8 us
    pallas_call x1, Pallas kernels, per_device(): pl.pallas_call(cov_kernel, out_shape=jax.ShapeDtypeStruct((share, total_c...  9.32 us
    pallas_call x1, Pallas kernels, per_device(): pl.pallas_call(functools.partial(ffn_kernel, 512), out_shape=(jax.ShapeDt...  8.68 us
    all_to_all x1, starting transfers between devices, per_device(): lax.all_to_all(summed.reshape(n_expert, capacity, part), EXP, split_axis=...  6.33 us
    ppermute x1, starting transfers between devices, per_device(): other_clips = lax.ppermute(clips, 'dp', swap)  3.59 us
  transfers between devices with their start and end apart: 5, of which 4 were waited for; matrix products, arithmetic and copies ran while one was open for 0% of the time, Pallas kernels for 9%

profile of v2, /device:TPU:1, one launch (start us, length us, event | category | flops | bytes accessed | tf_op | source)
XLA Modules:
  0.0 169.7 jit_solution(10466576356693330351)
XLA Ops:
  7.2 0.0 all-gather.2.cloned.1.call-start
  7.2 0.7 all-gather.2.cloned.1.call-update
  7.9 2.6 %prep.1 = (bf16[1024,512]{1,0:T(8,128)(2,1)}, bf16[1024,128]{1,0:T(8,128)(2,1)}, bf16[1024,128]{1,0:T(8,128)(2,1)}) custom-call(s32[1]{0:T(128)} %bitcast.d_ref, bf16[128,1024]{1,0:T(8,128)(2,1)} %tok_ref.1, bf16[64,1024]{1,0:T(8,128)(2,1)} %bitcast.27, s32[2,128]{1,0:T(2,128)} %bitcast.28), custom_call_target="tpu_custom_call" | custom-call | tf_op jit(solution)/shard_map/prep/pallas_call | solution.py:238
  10.5 48.0 %all_to_all.20 = bf16[128,8,512]{2,1,0:T(8,128)(2,1)S(1)} all-to-all(bf16[128,8,512]{2,1,0:T(8,128)(2,1)} %bitcast.25), channel_id=1, replica_groups=mesh['x'=4,'y'=4,'z'=8,'dp'=2] {'x','y','z'}, dimensions={0} | all-to-all | bytes 2097152 | tf_op jit(solution)/shard_map/all_to_all | solution.py:257
  58.6 2.7 %collective-permute-start = (bf16[1024,512]{1,0:T(8,128)(2,1)S(1)}, bf16[1024,512]{1,0:T(8,128)(2,1)S(1)}, u32[]{:S(2)}, u32[]{:S(2)}) collective-permute-start(bf16[1024,512]{1,0:T(8,128)(2,1)S(1)} %bitcast.20), channel_id=1, source_target_pairs={{0,1},{1,0},{2,3},{3,2},{4,5},{5,4},{6,7},{7,6},{8,9},{9,8},{10,11... | collective-permute-start | bytes 3145736 | tf_op jit(solution)/shard_map/ppermute | solution.py:260
  61.3 2.3 %collective-permute-done.other_ref = bf16[1024,512]{1,0:T(8,128)(2,1)S(1)} collective-permute-done((bf16[1024,512]{1,0:T(8,128)(2,1)S(1)}, bf16[1024,512]{1,0:T(8,128)(2,1)S(1)}, u32[]{:S(2)}, u32[]{:S(2)}) %collective-permute-start) | collective-permute-done | bytes 1048608 | tf_op jit(solution)/shard_map/ppermute | solution.py:260
  63.6 0.0 copy-start
  63.6 8.7 %ffn.1 = (bf16[1024,1024]{1,0:T(8,128)(2,1)S(1)}, bf16[1024,512]{1,0:T(8,128)(2,1)S(1)}) custom-call(s32[1]{0:T(128)} %bitcast.d_ref, bf16[1024,512]{1,0:T(8,128)(2,1)S(1)} %bitcast.21, bf16[1024,512]{1,0:T(8,128)(2,1)S(1)} %collective-permute-done.other_ref, bf16[1024,1024]{1,0:T(8,128)(2,1)} %bitcast.30, bf16[1024,1024]{1,0:T(8,128)(2,1)} %bitcast.31, ...), custom_call_target="tpu_custom_call" | custom-call | flops 5368709120 | tf_op jit(solution)/shard_map/ffn/pallas_call | solution.py:263
  72.2 0.5 collective-permute-start.1
  72.7 0.0 copy-done
  72.7 1.3 ours.1.own_ref
  74.0 1.0 collective-permute-done.1.brought_ref
  75.0 1.1 total.1
  76.1 0.0 copy-start.5
  76.2 6.3 %all-to-all-start.1 = ((bf16[128,8,512]{2,1,0:T(8,128)(2,1)}), bf16[128,8,512]{2,1,0:T(8,128)(2,1)S(1)}, u32[]{:S(2)}, u32[]{:S(2)}) async-start(bf16[128,8,512]{2,1,0:T(8,128)(2,1)} %bitcast.8), calls=%async_computation.1 | async-start | bytes 2097152 | tf_op jit(solution)/shard_map/all_to_all | solution.py:304
  82.5 0.0 copy-done.5
  82.5 0.1 copy.13.slot_ref
  82.6 33.4 %all-to-all-done.1 = bf16[128,8,512]{2,1,0:T(8,128)(2,1)S(1)} async-done(((bf16[128,8,512]{2,1,0:T(8,128)(2,1)}), bf16[128,8,512]{2,1,0:T(8,128)(2,1)S(1)}, u32[]{:S(2)}, u32[]{:S(2)}) %all-to-all-start.1) | async-done | bytes 1048608 | tf_op jit(solution)/shard_map/all_to_all | solution.py:304
  116.0 0.0 copy-done.1
  116.0 0.0 copy-done.3
  116.0 0.0 copy-done.4
  116.0 1.2 combine.1
  117.2 10.7 %all_to_all.21 = bf16[8,8,640]{2,1,0:T(8,128)(2,1)S(1)} all-to-all(bf16[8,8,640]{2,1,0:T(8,128)(2,1)S(1)} %broadcast_in_dim.6), channel_id=1, replica_groups=mesh['x'=4,'y'=4,'z'=8,'dp'=2] {'z'}, dimensions={0} | all-to-all | bytes 163840 | tf_op jit(solution)/shard_map/all_to_all | solution.py:322
  127.9 0.1 broadcast_in_dim.15
  128.0 0.0 copy-start.2
  128.0 20.1 %all_to_all.22 = bf16[16,64,640]{2,1,0:T(8,128)(2,1)S(1)} all-to-all(bf16[16,64,640]{2,1,0:T(8,128)(2,1)S(1)} %broadcast_in_dim.15), channel_id=1, replica_groups=mesh['x'=4,'y'=4,'z'=8,'dp'=2] {'x','y'}, dimensions={0} | all-to-all | bytes 2621440 | tf_op jit(solution)/shard_map/all_to_all | solution.py:322
  148.2 0.1 copy.15
  148.3 0.4 clips.1.own_ref
  148.7 3.6 %collective-permute-start.2 = (bf16[256,512]{1,0:T(8,128)(2,1)S(1)}, bf16[256,512]{1,0:T(8,128)(2,1)S(1)}, u32[]{:S(2)}, u32[]{:S(2)}) collective-permute-start(bf16[256,512]{1,0:T(8,128)(2,1)S(1)} %clips.1.own_ref), channel_id=1, source_target_pairs={{0,1},{1,0},{2,3},{3,2},{4,5},{5,4},{6,7},{7,6},{8,9},{9,8},{10,11... | collective-permute-start | bytes 786440 | tf_op jit(solution)/shard_map/ppermute | solution.py:335
  152.3 1.2 collective-permute-done.2.other_ref
  153.5 0.0 copy-done.2
  153.5 9.3 %covariance.1 = f32[32,8192]{1,0:T(8,128)} custom-call(s32[1]{0:T(128)} %bitcast.d_ref, bf16[256,512]{1,0:T(8,128)(2,1)S(1)} %clips.1.own_ref, bf16[256,512]{1,0:T(8,128)(2,1)S(1)} %collective-permute-done.2.other_ref, bf16[32,1024]{1,0:T(8,128)(2,1)S(1)} %bitcast.23, bf16[8192,1024]{1,0:T(8,128)(2,1)} %all-gather.2.cloned.1.call-done.full_hbm), custom_call_target="tpu_custom_call" | custom-call | tf_op jit(solution)/shard_map/covariance/pallas_call | solution.py:339
  (6 shorter events, 0.0 us)
Async XLA Ops:
  7.2 146.3 %all-gather.2.cloned.1.call-start = ((), (), s32[]{:S(2)}) async-start(), calls=%async_computation.4 | async-start | bytes 16842752 | tf_op jit(solution)/shard_map/all_gather | solution.py:234
  58.6 5.0 %collective-permute-start = (bf16[1024,512]{1,0:T(8,128)(2,1)S(1)}, bf16[1024,512]{1,0:T(8,128)(2,1)S(1)}, u32[]{:S(2)}, u32[]{:S(2)}) collective-permute-start(bf16[1024,512]{1,0:T(8,128)(2,1)S(1)} %bitcast.20), channel_id=1, source_target_pairs={{0,1},{1,0},{2,3},{3,2},{4,5},{5,4},{6,7},{7,6},{8,9},{9,8},{10,11... | collective-permute-start | bytes 3145736 | tf_op jit(solution)/shard_map/ppermute | solution.py:260
  63.6 9.2 %copy-start = (bf16[1,1024,1024]{2,1,0:T(8,128)(2,1)S(1)}, bf16[1,1024,1024]{2,1,0:T(8,128)(2,1)}, u32[]{:S(2)}) copy-start(bf16[1,1024,1024]{2,1,0:T(8,128)(2,1)} %param.12) | copy-start | bytes 6291460
  72.2 2.8 %collective-permute-start.1 = (bf16[1024,512]{1,0:T(8,128)(2,1)S(1)}, bf16[1024,512]{1,0:T(8,128)(2,1)S(1)}, u32[]{:S(2)}, u32[]{:S(2)}) collective-permute-start(bf16[1024,512]{1,0:T(8,128)(2,1)S(1)} %get-tuple-element.11), channel_id=1, source_target_pairs={{0,1},{1,0},{2,3},{3,2},{4,5},{5,4},{6,7},{7,6},{8,9},{9,8},{10,11... | collective-permute-start | bytes 3145736 | tf_op jit(solution)/shard_map/ppermute | solution.py:286
  76.1 6.4 %copy-start.5 = (s32[8]{0:T(128)S(1)}, s32[8]{0:T(128)}, u32[]{:S(2)}) copy-start(s32[8]{0:T(128)} %param.15) | copy-start | bytes 100
  76.2 39.8 %copy-start.1 = (bf16[128,1024]{1,0:T(8,128)(2,1)S(1)}, bf16[128,1024]{1,0:T(8,128)(2,1)}, u32[]{:S(2)}) copy-start(bf16[128,1024]{1,0:T(8,128)(2,1)} %tok_ref.1) | copy-start | bytes 786436
  76.2 39.8 %copy-start.3 = (bf16[1024,128]{1,0:T(8,128)(2,1)S(1)}, bf16[1024,128]{1,0:T(8,128)(2,1)}, u32[]{:S(2)}) copy-start(bf16[1024,128]{1,0:T(8,128)(2,1)} %get-tuple-element.12.high_ref) | copy-start | bytes 786436
  76.2 39.8 %copy-start.4 = (bf16[1024,128]{1,0:T(8,128)(2,1)S(1)}, bf16[1024,128]{1,0:T(8,128)(2,1)}, u32[]{:S(2)}) copy-start(bf16[1024,128]{1,0:T(8,128)(2,1)} %get-tuple-element.13.low_ref) | copy-start | bytes 786436
  76.2 39.8 %all-to-all-start.1 = ((bf16[128,8,512]{2,1,0:T(8,128)(2,1)}), bf16[128,8,512]{2,1,0:T(8,128)(2,1)S(1)}, u32[]{:S(2)}, u32[]{:S(2)}) async-start(bf16[128,8,512]{2,1,0:T(8,128)(2,1)} %bitcast.8), calls=%async_computation.1 | async-start | bytes 2097152 | tf_op jit(solution)/shard_map/all_to_all | solution.py:304
  128.0 25.5 %copy-start.2 = (bf16[1024,32]{0,1:T(8,128)(2,1)S(1)}, bf16[1024,32]{0,1:T(8,128)(2,1)}, u32[]{:S(2)}) copy-start(bf16[1024,32]{0,1:T(8,128)(2,1)} %param.13) | copy-start | bytes 196612
  148.7 4.7 %collective-permute-start.2 = (bf16[256,512]{1,0:T(8,128)(2,1)S(1)}, bf16[256,512]{1,0:T(8,128)(2,1)S(1)}, u32[]{:S(2)}, u32[]{:S(2)}) collective-permute-start(bf16[256,512]{1,0:T(8,128)(2,1)S(1)} %clips.1.own_ref), channel_id=1, source_target_pairs={{0,1},{1,0},{2,3},{3,2},{4,5},{5,4},{6,7},{7,6},{8,9},{9,8},{10,11... | collective-permute-start | bytes 786440 | tf_op jit(solution)/shard_map/ppermute | solution.py:335
Sparse Core Ops, SparseCore 0:
  11.7 140.5 all-gather.1

commit v3 on v2

--- a/solution.py
+++ b/solution.py
@@ -9,6 +9,7 @@
 
 EXP = ("x", "y", "z")
 ALL = ("x", "y", "z", "dp")
+PLANE = ("x", "y")
 F32 = jnp.float32
 BF16 = jnp.bfloat16
 LANES = 128
@@ -78,6 +79,10 @@
     out_ref[...] = dot(picks.astype(BF16), tok_ref[:, half(d, width // 2)]).astype(BF16)
 
 
+def order_kernel(*refs):
+    pass
+
+
 def ffn_kernel(
     step, d_ref, own_ref, other_ref, gate_hbm, up_hbm, down_hbm, hid_ref, out_ref, x_ref, gate_ref, up_ref, down_ref, sems, down_sem
 ):
@@ -132,8 +137,9 @@
     out_ref[...] = (own_ref[...] + brought_ref[...].astype(F32)).astype(BF16)
 
 
-def combine_kernel(d_ref, back_ref, high_ref, low_ref, tok_ref, slot_ref, mixed_ref, frames_ref):
-    d = d_ref[0]
+def combine_kernel(d_ref, z_ref, back_ref, high_ref, low_ref, tok_ref, slot_ref, *refs):
+    mixed_ref, payload_ref = refs[-2:]
+    d, z = d_ref[0], z_ref[0]
     rows, part = mixed_ref.shape
     count = slot_ref.shape[0]
     back = back_ref[...]
@@ -142,62 +148,61 @@
     mixed_ref[...] = mixed
     length = rows // count
     frames = jnp.sum(mixed.astype(F32).reshape(count, length, part), axis=1) / length
-    frames_ref[:, 0:part] = frames.astype(BF16)
     slot = slot_ref[...]
-    lane = lax.broadcasted_iota(jnp.int32, (count, LANES), 1)
-    digits = jnp.where(lane == 0, slot // 32, jnp.where(lane == 1, slot % 32, 0))
-    frames_ref[:, part : part + LANES] = digits.astype(F32).astype(BF16)
-
-
-def clip_kernel(length, frames_ref, digits_ref, clips_ref):
+    lane = lax.broadcasted_iota(jnp.int32, (count, part), 1)
+    number = lax.broadcasted_iota(jnp.int32, (count, part), 0)
+    digit = jnp.where(lane % (2 * count) < count, slot // 32, slot % 32)
+    here = (lane // (2 * count) == z) & (lane % count == number)
+    digits = jnp.sum(jnp.where(here, digit, 0).astype(F32), axis=0, keepdims=True)
+    first = jnp.where(number == 0, jnp.broadcast_to(digits, (count, part)), 0.0)
+    block = jnp.concatenate([frames, first], axis=0).astype(BF16)
+    for k in range(payload_ref.shape[0]):
+        payload_ref[k] = block
+
+
+def clip_kernel(length, used, z_ref, frames_ref, digits_ref, *refs):
+    line_refs, (clips_ref, embed_ref) = refs[:-2], refs[-2:]
     clips, part = clips_ref.shape
-    count = frames_ref.shape[0]
+    groups = frames_ref.shape[0]
     digits = digits_ref[...].astype(F32)
     slot = digits[0:1, :] * 32.0 + digits[1:2, :]
     clip = jnp.floor(slot / length)
-    number = lax.broadcasted_iota(jnp.int32, (clips, count), 0).astype(F32)
+    number = lax.broadcasted_iota(jnp.int32, (clips, groups * used), 0).astype(F32)
     picks = jnp.where(clip == number, 1.0, 0.0).astype(BF16)
-    clips_ref[...] = (dot(picks, frames_ref[:, 0:part]) / length).astype(BF16)
+    frames = frames_ref[:, 0:used, :].reshape(groups * used, part)
+    pooled = (dot(picks, frames) / length).astype(BF16)
+    clips_ref[...] = pooled
+    count, chunk = len(line_refs), line_refs[0].shape[0]
+    for k, ref in enumerate(line_refs):
+        to = pl.ds(pl.multiple_of(lax.rem(z_ref[0] + count - k, count) * chunk, chunk), chunk)
+        embed_ref[to, :] = dot_nt(ref[...], pooled)
 
 
 def cov_kernel(
-    d_ref, own_ref, other_ref, mine_ref, full_hbm, out_hbm, left_ref, full_ref, out_ref, in_sems, out_sems
+    d_ref, x_ref, y_ref, own_ref, other_ref, cols_ref, cols_other_ref, plane0, plane1, plane2, plane3, out_ref
 ):
-    d = d_ref[0]
-    cols = mine_ref.shape[0]
+    d, x, y = d_ref[0], x_ref[0], y_ref[0]
     clips, part = own_ref.shape
-    blocks = in_sems.shape[0]
-    wide = full_ref.shape[0] // blocks
-    spans = [slice(k * wide, (k + 1) * wide) for k in range(blocks)]
-    loads = [
-        pltpu.make_async_copy(full_hbm.at[span, :], full_ref.at[span, :], in_sems.at[k])
-        for k, span in enumerate(spans)
-    ]
-    stores = [
-        pltpu.make_async_copy(out_ref.at[:, span], out_hbm.at[:, span], out_sems.at[k])
-        for k, span in enumerate(spans)
-    ]
-    for load in loads:
-        load.start()
+    share = out_ref.shape[1]
     own, other = own_ref[...], other_ref[...]
-    embed = dot_nt(mine_ref[:, half(d, part)], own) + dot_nt(mine_ref[:, half(1 - d, part)], other)
-    centered = embed - jnp.mean(embed, axis=1, keepdims=True)
-    high = centered.astype(BF16)
-    rest = centered - high.astype(F32)
-    middle = rest.astype(BF16)
-    low = (rest - middle.astype(F32)).astype(BF16)
-    for where, clip in ((half(d, part), own), (half(1 - d, part), other)):
-        left = (dot(high, clip) + dot(middle, clip) + dot(low, clip)) / (clips - 1)
-        left_high, left_low = split2(left)
-        left_ref[0:cols, where] = left_high
-        left_ref[cols : 2 * cols, where] = left_low
-    for load, store, span in zip(loads, stores, spans):
-        load.wait()
-        both = dot_nt(left_ref[...], full_ref[span, :])
-        out_ref[:, span] = both[0:cols] + both[cols : 2 * cols]
-        store.start()
-    for store in stores:
-        store.wait()
+
+    def center(embed):
+        return embed - jnp.mean(embed, axis=1, keepdims=True)
+
+    cols_high, cols_low = split2(center(cols_ref[...] + cols_other_ref[...]))
+    for j, ref in enumerate((plane0, plane1, plane2, plane3)):
+        embed = dot_nt(ref[:, half(d, part)], own) + dot_nt(ref[:, half(1 - d, part)], other)
+        rows_high, rows_low = split2(center(embed) / (clips - 1))
+        block = dot_nt(rows_high, cols_high) + dot_nt(rows_high, cols_low) + dot_nt(rows_low, cols_high)
+        for i in range(4):
+            peer = 4 * lax.rem(x + 4 - i, 4) + lax.rem(y + 4 - j, 4)
+            out_ref[peer] = block[i * share : (i + 1) * share].astype(BF16)
+
+
+def place_kernel(in_ref, out_ref):
+    peers, share, wide = in_ref.shape
+    for k in range(peers):
+        out_ref[:, k * wide : (k + 1) * wide] = in_ref[k].astype(F32)
 
 
 SCALAR = pl.BlockSpec(memory_space=pltpu.SMEM)
@@ -226,12 +231,27 @@
     frame_total = count * n_expert
     clip_total = frame_total // 4
     share = expand_weight.shape[1]
-    d = lax.axis_index("dp").astype(jnp.int32).reshape(1)
+    d, x, y, z = (lax.axis_index(axis).astype(jnp.int32).reshape(1) for axis in ("dp", "x", "y", "z"))
     swap = [(0, 1), (1, 0)]
     params = pltpu.CompilerParams(vmem_limit_bytes=16 * 2**20)
 
     mine = expand_weight.T
-    full = lax.all_gather(mine, ALL, axis=0, tiled=True)
+
+    def ring(block, axis, step):
+        size = lax.axis_size(axis)
+        return lax.ppermute(block, axis, [(k, (k + step) % size) for k in range(size)])
+
+    row = jnp.concatenate([mine] + [ring(mine, "x", step) for step in (1, 2, 3)], axis=0)
+    planes = [row] + [ring(row, "y", step) for step in (1, 2, 3)]
+    first, second = mine[:, :part], mine[:, part:]
+    kept = jnp.where(d[0] == 0, first, second)
+    sent = lax.ppermute(jnp.where(d[0] == 0, second, first), "dp", swap)
+    both = jnp.concatenate(
+        [jnp.where(d[0] == 0, kept, sent), jnp.where(d[0] == 0, sent, kept)], axis=0
+    )
+    along = {step: ring(both, "z", step) for step in (1, 7, 2, 6)}
+    with_dispatch = (row, *(along[step] for step in (1, 7)), both)
+    with_return = (*planes[1:], *(along[step] for step in (2, 6)))
 
     vmem = pl.BlockSpec(memory_space=pltpu.VMEM)
     hbm = pl.BlockSpec(memory_space=pl.ANY)
@@ -257,6 +277,15 @@
     received = lax.all_to_all(
         outgoing.reshape(n_expert, capacity, part), EXP, split_axis=0, concat_axis=0, tiled=True
     ).reshape(rows, part)
+    received = pl.pallas_call(
+        order_kernel,
+        out_shape=jax.ShapeDtypeStruct((rows, part), BF16),
+        in_specs=[hbm] * (1 + len(with_dispatch)),
+        out_specs=hbm,
+        input_output_aliases={0: 0},
+        compiler_params=pltpu.CompilerParams(vmem_limit_bytes=2**20),
+        name="order",
+    )(received, *with_dispatch)
     other = lax.ppermute(received, "dp", swap)
 
     w_down = down_weight.reshape(hidden, width)
@@ -305,52 +334,60 @@
         summed.reshape(n_expert, capacity, part), EXP, split_axis=0, concat_axis=0, tiled=True
     ).reshape(rows, part)
 
-    mixed, frames = pl.pallas_call(
+    mixed, payload = pl.pallas_call(
         combine_kernel,
         out_shape=(
             jax.ShapeDtypeStruct((tok_rows, part), BF16),
-            jax.ShapeDtypeStruct((count, part + LANES), BF16),
-        ),
-        in_specs=[SCALAR, vmem, vmem, vmem, vmem, vmem],
+            jax.ShapeDtypeStruct((n_z, 2 * count, part), BF16),
+        ),
+        in_specs=[SCALAR] * 2 + [vmem] * 5 + [hbm] * len(with_return),
         out_specs=(vmem, vmem),
         compiler_params=params,
         name="combine",
-    )(d, back, high, low, tokens, frame_slot.reshape(count, 1))
-
-    def spread(block, axes, size):
-        copies = jnp.broadcast_to(block[None], (size,) + block.shape)
-        out = lax.all_to_all(copies, axes, split_axis=0, concat_axis=0, tiled=True)
-        return out.reshape(-1, block.shape[-1])
-
-    gathered = spread(spread(frames, "z", n_z), ("x", "y"), n_xy)
-    digits = gathered[:, part : part + 8].T
-    clips = pl.pallas_call(
-        functools.partial(clip_kernel, 4),
-        out_shape=jax.ShapeDtypeStruct((clip_total, part), BF16),
-        in_specs=[vmem, vmem],
+    )(d, z, back, high, low, tokens, frame_slot.reshape(count, 1), *with_return)
+
+    got = lax.all_to_all(payload, "z", split_axis=0, concat_axis=0, tiled=True)
+    used = n_z * count
+    wide = n_z * 2 * share
+    packed = jnp.concatenate(
+        [got[:, :count].reshape(used, part), jnp.sum(got[:, count:], axis=0)], axis=0
+    )
+    line = [both] + [along[step] if step in along else ring(both, "z", step) for step in range(1, n_z)]
+    copies = jnp.broadcast_to(packed[None], (n_xy,) + packed.shape)
+    gathered = lax.all_to_all(copies, PLANE, split_axis=0, concat_axis=0, tiled=True)
+    digits = gathered[:, used, : 2 * used].reshape(n_xy, n_z, 2, count)
+    digits = digits.transpose(2, 0, 1, 3).reshape(2, frame_total)
+    clips, embed = pl.pallas_call(
+        functools.partial(clip_kernel, 4, used),
+        out_shape=(
+            jax.ShapeDtypeStruct((clip_total, part), BF16),
+            jax.ShapeDtypeStruct((wide, clip_total), F32),
+        ),
+        in_specs=[SCALAR] + [vmem] * (2 + n_z),
+        out_specs=(vmem, vmem),
+        compiler_params=params,
+        name="clips",
+    )(z, gathered, digits, *line)
+    other_clips = lax.ppermute(clips, "dp", swap)
+    other_embed = lax.ppermute(embed, "dp", swap)
+
+    blocks = pl.pallas_call(
+        cov_kernel,
+        out_shape=jax.ShapeDtypeStruct((n_xy, share, wide), BF16),
+        in_specs=[SCALAR] * 3 + [vmem] * 8,
         out_specs=vmem,
         compiler_params=params,
-        name="clips",
-    )(gathered, digits)
-    other_clips = lax.ppermute(clips, "dp", swap)
-
-    total_cols = full.shape[0]
-    blocks = 8
+        name="covariance",
+    )(d, x, y, clips, other_clips, embed, other_embed, *planes)
+    home = lax.all_to_all(blocks, PLANE, split_axis=0, concat_axis=0, tiled=True)
     covariance = pl.pallas_call(
-        cov_kernel,
-        out_shape=jax.ShapeDtypeStruct((share, total_cols), F32),
-        in_specs=[SCALAR, vmem, vmem, vmem, hbm],
-        out_specs=hbm,
-        scratch_shapes=[
-            pltpu.VMEM((2 * share, width), BF16),
-            pltpu.VMEM((total_cols, width), BF16),
-            pltpu.VMEM((share, total_cols), F32),
-            pltpu.SemaphoreType.DMA((blocks,)),
-            pltpu.SemaphoreType.DMA((blocks,)),
-        ],
-        compiler_params=pltpu.CompilerParams(vmem_limit_bytes=48 * 2**20),
-        name="covariance",
-    )(d, clips, other_clips, mine, full)
+        place_kernel,
+        out_shape=jax.ShapeDtypeStruct((share, n_xy * wide), F32),
+        in_specs=[vmem],
+        out_specs=vmem,
+        compiler_params=params,
+        name="place",
+    )(home)
     return mixed, covariance
 
 

time: 170 us -> 164 us (0.965)
  blocking collectives: 78.8 us -> 23.8 us
  starting transfers between devices: 13.1 us -> 55.7 us
  waiting for transfers between devices: 38.6 us -> 61.6 us
  between operations: 14.1 us -> 0.83 us
  Pallas kernels: 24.6 us -> 19.4 us
    all_to_all x3 -> x2, blocking collectives: 78.8 us -> 23.8 us  [the longest x1 13.4 us: per_device(): lax.all_to_all(blocks, PLANE, split_axis=0, concat_axis=0, tiled=True)]
    ppermute x0 -> x15, waiting for transfers between devices: none -> 34.4 us  [the longest x13 34.4 us: ring(): lax.ppermute(block, axis, [(k, (k + step) % size) for k in range(size)])]
    all_to_all x1, waiting for transfers between devices: 33.4 us -> 4.6 us  [per_device(): lax.all_to_all(summed.reshape(n_expert, capacity, part), EXP, split_axis=...]
    ppermute x0 -> x15, starting transfers between devices: none -> 24.6 us  [the longest x13 19.7 us: ring(): lax.ppermute(block, axis, [(k, (k + step) % size) for k in range(size)])]
    all_to_all x0 -> x2, starting transfers between devices: none -> 20.6 us  [the longest x1 16.3 us: per_device(): lax.all_to_all(outgoing.reshape(n_expert, capacity, part), EXP, split_axi...]
    all_to_all x0 -> x2, waiting for transfers between devices: none -> 17.5 us  [the longest x1 10.8 us: per_device(): lax.all_to_all(copies, PLANE, split_axis=0, concat_axis=0, tiled=True)]
    pallas_call x2 -> x4, Pallas kernels: 9.76 us -> 4.5 us  [the longest x1 2.34 us: per_device(): pl.pallas_call(cov_kernel, out_shape=jax.ShapeDtypeStruct((n_xy, share, w...]
    ppermute x1, starting transfers between devices: 3.59 us -> 0.1 us  [per_device(): other_clips = lax.ppermute(clips, 'dp', swap)]
  transfers between devices with their start and end apart: 5 -> 21, of which waited for: 4 -> 9; matrix products, arithmetic and copies ran while one was open for 0% -> 0% of each run, Pallas kernels for 9% -> 1%
where the time goes in v3:
time: 164 us; the launch traced here: 163 us
  waiting for transfers between devices  61.6 us (38%)
  starting transfers between devices  55.7 us (34%)
  blocking collectives  23.8 us (15%)
  Pallas kernels  19.4 us (12%)
    ppermute x13, waiting for transfers between devices, ring(): lax.ppermute(block, axis, [(k, (k + step) % size) for k in range(size)])  34.4 us
    ppermute x13, starting transfers between devices, ring(): lax.ppermute(block, axis, [(k, (k + step) % size) for k in range(size)])  19.7 us
    all_to_all x1, starting transfers between devices, per_device(): lax.all_to_all(outgoing.reshape(n_expert, capacity, part), EXP, split_axi...  16.3 us
    all_to_all x1, blocking collectives, per_device(): lax.all_to_all(blocks, PLANE, split_axis=0, concat_axis=0, tiled=True)  13.4 us
    all_to_all x1, waiting for transfers between devices, per_device(): lax.all_to_all(copies, PLANE, split_axis=0, concat_axis=0, tiled=True)  10.8 us
    all_to_all x1, blocking collectives, per_device(): got = lax.all_to_all(payload, 'z', split_axis=0, concat_axis=0, tiled=True)  10.4 us
    pallas_call x1, Pallas kernels, per_device(): pl.pallas_call(functools.partial(ffn_kernel, 512), out_shape=(jax.ShapeDt...  8.67 us
    all_to_all x1, waiting for transfers between devices, per_device(): lax.all_to_all(outgoing.reshape(n_expert, capacity, part), EXP, split_axi...  6.72 us
  transfers between devices with their start and end apart: 21, of which 9 were waited for; matrix products, arithmetic and copies ran while one was open for 0% of the time, Pallas kernels for 1%

profile of v3, /device:TPU:1, one launch (start us, length us, event | category | flops | bytes accessed | tf_op | source)
XLA Modules:
  0.0 162.9 jit_solution(8860383460095773465)
XLA Ops:
  0.6 2.6 %prep.1 = (bf16[1024,512]{1,0:T(8,128)(2,1)}, bf16[1024,128]{1,0:T(8,128)(2,1)}, bf16[1024,128]{1,0:T(8,128)(2,1)}) custom-call(s32[1]{0:T(128)} %bitcast.d_ref, bf16[128,1024]{1,0:T(8,128)(2,1)} %tok_ref.1, bf16[64,1024]{1,0:T(8,128)(2,1)} %bitcast.34, s32[2,128]{1,0:T(2,128)} %bitcast.35), custom_call_target="tpu_custom_call" | custom-call | tf_op jit(solution)/shard_map/prep/pallas_call | solution.py:258
  3.3 16.3 %all-to-all-start = ((bf16[128,8,512]{2,1,0:T(8,128)(2,1)}), bf16[128,8,512]{2,1,0:T(8,128)(2,1)S(1)}, u32[]{:S(2)}, u32[]{:S(2)}) async-start(bf16[128,8,512]{2,1,0:T(8,128)(2,1)} %bitcast.26), calls=%async_computation | async-start | bytes 2097152 | tf_op jit(solution)/shard_map/all_to_all | solution.py:277
  21.7 2.8 %collective-permute-start.1 = (bf16[32,1024]{1,0:T(8,128)(2,1)S(1)}, bf16[32,1024]{1,0:T(8,128)(2,1)S(1)}, u32[]{:S(2)}, u32[]{:S(2)}) collective-permute-start(bf16[32,1024]{1,0:T(8,128)(2,1)S(1)} %bitcast.29), channel_id=1, source_target_pairs={{0,128},{64,192},{128,0},{192,64},{1,129},{65,193},{129,1},{193,65... | collective-permute-start | bytes 196616 | tf_op jit(solution)/shard_map/ppermute | solution.py:242
  25.5 1.3 collective-permute-start.4
  26.8 1.5 collective-permute-start.5
  28.3 2.2 %collective-permute-done.1 = bf16[32,1024]{1,0:T(8,128)(2,1)S(1)} collective-permute-done((bf16[32,1024]{1,0:T(8,128)(2,1)S(1)}, bf16[32,1024]{1,0:T(8,128)(2,1)S(1)}, u32[]{:S(2)}, u32[]{:S(2)}) %collective-permute-start.1) | collective-permute-done | bytes 65568 | tf_op jit(solution)/shard_map/ppermute | solution.py:242
  30.5 12.7 %collective-permute-done.4.refs_2_.refs_1_ = bf16[64,512]{1,0:T(8,128)(2,1)S(1)} collective-permute-done((bf16[64,512]{1,0:T(8,128)(2,1)S(1)}, bf16[64,512]{1,0:T(8,128)(2,1)S(1)}, u32[]{:S(2)}, u32[]{:S(2)}) %collective-permute-start.4) | collective-permute-done | bytes 65568 | tf_op jit(solution)/shard_map/ppermute | solution.py:242
  43.1 6.7 %all-to-all-done = bf16[128,8,512]{2,1,0:T(8,128)(2,1)S(1)} async-done(((bf16[128,8,512]{2,1,0:T(8,128)(2,1)}), bf16[128,8,512]{2,1,0:T(8,128)(2,1)S(1)}, u32[]{:S(2)}, u32[]{:S(2)}) %all-to-all-start) | async-done | bytes 1048608 | tf_op jit(solution)/shard_map/all_to_all | solution.py:277
  49.9 3.4 %collective-permute-start.6 = (bf16[1024,512]{1,0:T(8,128)(2,1)S(1)}, bf16[1024,512]{1,0:T(8,128)(2,1)S(1)}, u32[]{:S(2)}, u32[]{:S(2)}) collective-permute-start(bf16[1024,512]{1,0:T(8,128)(2,1)S(1)} %order.1.own_ref), channel_id=1, source_target_pairs={{0,1},{1,0},{2,3},{3,2},{4,5},{5,4},{6,7},{7,6},{8,9},{9,8},{10,11... | collective-permute-start | bytes 3145736 | tf_op jit(solution)/shard_map/ppermute | solution.py:289
  53.2 2.3 %collective-permute-done.6.other_ref = bf16[1024,512]{1,0:T(8,128)(2,1)S(1)} collective-permute-done((bf16[1024,512]{1,0:T(8,128)(2,1)S(1)}, bf16[1024,512]{1,0:T(8,128)(2,1)S(1)}, u32[]{:S(2)}, u32[]{:S(2)}) %collective-permute-start.6) | collective-permute-done | bytes 1048608 | tf_op jit(solution)/shard_map/ppermute | solution.py:289
  55.5 8.7 %ffn.1 = (bf16[1024,1024]{1,0:T(8,128)(2,1)S(1)}, bf16[1024,512]{1,0:T(8,128)(2,1)S(1)}) custom-call(s32[1]{0:T(128)} %bitcast.d_ref, bf16[1024,512]{1,0:T(8,128)(2,1)S(1)} %order.1.own_ref, bf16[1024,512]{1,0:T(8,128)(2,1)S(1)} %collective-permute-done.6.other_ref, bf16[1024,1024]{1,0:T(8,128)(2,1)} %bitcast.37, bf16[1024,1024]{1,0:T(8,128)(2,1)} %bitcast.38, ...), custom_call_target="tpu_custom_call" | custom-call | flops 5368709120 | tf_op jit(solution)/shard_map/ffn/pallas_call | solution.py:292
  64.7 1.2 ours.1.own_ref
  67.0 1.1 total.1
  68.1 6.5 %all-to-all-start.1 = ((bf16[128,8,512]{2,1,0:T(8,128)(2,1)}), bf16[128,8,512]{2,1,0:T(8,128)(2,1)S(1)}, u32[]{:S(2)}, u32[]{:S(2)}) async-start(bf16[128,8,512]{2,1,0:T(8,128)(2,1)} %bitcast.10), calls=%async_computation.1 | async-start | bytes 2097152 | tf_op jit(solution)/shard_map/all_to_all | solution.py:333
  74.6 1.9 %collective-permute-start.10 = (bf16[128,1024]{1,0:T(8,128)(2,1)S(1)}, bf16[128,1024]{1,0:T(8,128)(2,1)S(1)}, u32[]{:S(2)}, u32[]{:S(2)}) collective-permute-start(bf16[128,1024]{1,0:T(8,128)(2,1)S(1)} %pad_maximum_fusion.refs_1_.plane0), channel_id=1, source_target_pairs={{0,48},{16,0},{32,16},{48,32},{1,49},{17,1},{33,17},{49,33},{2,50}... | collective-permute-start | bytes 786440 | tf_op jit(solution)/shard_map/ppermute | solution.py:242
  76.5 1.7 %collective-permute-start.9 = (bf16[128,1024]{1,0:T(8,128)(2,1)S(1)}, bf16[128,1024]{1,0:T(8,128)(2,1)S(1)}, u32[]{:S(2)}, u32[]{:S(2)}) collective-permute-start(bf16[128,1024]{1,0:T(8,128)(2,1)S(1)} %pad_maximum_fusion.refs_1_.plane0), channel_id=1, source_target_pairs={{0,32},{16,48},{32,0},{48,16},{1,33},{17,49},{33,1},{49,17},{2,34}... | collective-permute-start | bytes 786440 | tf_op jit(solution)/shard_map/ppermute | solution.py:242
  78.2 2.1 %collective-permute-start.11 = (bf16[64,512]{1,0:T(8,128)(2,1)S(1)}, bf16[64,512]{1,0:T(8,128)(2,1)S(1)}, u32[]{:S(2)}, u32[]{:S(2)}) collective-permute-start(bf16[64,512]{1,0:T(8,128)(2,1)S(1)} %pad_maximum_fusion.2.refs_4_.refs_0_), channel_id=1, source_target_pairs={{0,4},{2,6},{4,8},{6,10},{8,12},{10,14},{12,0},{14,2},{1,5},{3,7},... | collective-permute-start | bytes 196616 | tf_op jit(solution)/shard_map/ppermute | solution.py:242
  80.3 1.5 collective-permute-start.12
  81.9 19.6 %collective-permute-done.11.refs_3_.refs_2_ = bf16[64,512]{1,0:T(8,128)(2,1)S(1)} collective-permute-done((bf16[64,512]{1,0:T(8,128)(2,1)S(1)}, bf16[64,512]{1,0:T(8,128)(2,1)S(1)}, u32[]{:S(2)}, u32[]{:S(2)}) %collective-permute-start.11) | collective-permute-done | bytes 65568 | tf_op jit(solution)/shard_map/ppermute | solution.py:242
  101.5 4.6 %all-to-all-done.1 = bf16[128,8,512]{2,1,0:T(8,128)(2,1)S(1)} async-done(((bf16[128,8,512]{2,1,0:T(8,128)(2,1)}), bf16[128,8,512]{2,1,0:T(8,128)(2,1)S(1)}, u32[]{:S(2)}, u32[]{:S(2)}) %all-to-all-start.1) | async-done | bytes 1048608 | tf_op jit(solution)/shard_map/all_to_all | solution.py:333
  106.1 1.2 combine.1
  107.3 10.4 %all_to_all.25 = bf16[8,16,512]{2,1,0:T(8,128)(2,1)S(1)} all-to-all(bf16[8,16,512]{2,1,0:T(8,128)(2,1)S(1)} %get-tuple-element.17), channel_id=1, replica_groups=mesh['x'=4,'y'=4,'z'=8,'dp'=2] {'z'}, dimensions={0} | all-to-all | bytes 262144 | tf_op jit(solution)/shard_map/all_to_all | solution.py:349
  117.7 1.1 broadcast_in_dim.2
  118.8 4.2 %all-to-all-start.3 = ((bf16[16,72,512]{2,1,0:T(8,128)(2,1)}), bf16[16,72,512]{2,1,0:T(8,128)(2,1)S(1)}, u32[]{:S(2)}, u32[]{:S(2)}) async-start(bf16[16,72,512]{2,1,0:T(8,128)(2,1)} %broadcast_in_dim.2), calls=%async_computation.3 | async-start | bytes 2359296 | tf_op jit(solution)/shard_map/all_to_all | solution.py:357
  123.1 2.6 %collective-permute-start.14 = (bf16[64,512]{1,0:T(8,128)(2,1)S(1)}, bf16[64,512]{1,0:T(8,128)(2,1)S(1)}, u32[]{:S(2)}, u32[]{:S(2)}) collective-permute-start(bf16[64,512]{1,0:T(8,128)(2,1)S(1)} %pad_maximum_fusion.2.refs_4_.refs_0_), channel_id=1, source_target_pairs={{0,8},{2,10},{4,12},{6,14},{8,0},{10,2},{12,4},{14,6},{1,9},{3,11}... | collective-permute-start | bytes 196616 | tf_op jit(solution)/shard_map/ppermute | solution.py:242
  125.7 2.4 %collective-permute-start.15 = (bf16[64,512]{1,0:T(8,128)(2,1)S(1)}, bf16[64,512]{1,0:T(8,128)(2,1)S(1)}, u32[]{:S(2)}, u32[]{:S(2)}) collective-permute-start(bf16[64,512]{1,0:T(8,128)(2,1)S(1)} %pad_maximum_fusion.2.refs_4_.refs_0_), channel_id=1, source_target_pairs={{0,10},{2,12},{4,14},{6,0},{8,2},{10,4},{12,6},{14,8},{1,11},{3,13... | collective-permute-start | bytes 196616 | tf_op jit(solution)/shard_map/ppermute | solution.py:242
  128.1 10.8 %all-to-all-done.3.frames_ref = bf16[16,72,512]{2,1,0:T(8,128)(2,1)S(1)} async-done(((bf16[16,72,512]{2,1,0:T(8,128)(2,1)}), bf16[16,72,512]{2,1,0:T(8,128)(2,1)S(1)}, u32[]{:S(2)}, u32[]{:S(2)}) %all-to-all-start.3) | async-done | bytes 1179680 | tf_op jit(solution)/shard_map/all_to_all | solution.py:357
  139.3 1.1 clips.1
  140.4 3.8 %collective-permute-start.17 = (f32[512,256]{1,0:T(8,128)S(1)}, f32[512,256]{1,0:T(8,128)S(1)}, u32[]{:S(2)}, u32[]{:S(2)}) collective-permute-start(f32[512,256]{1,0:T(8,128)S(1)} %get-tuple-element.19.cols_ref), channel_id=1, source_target_pairs={{0,1},{1,0},{2,3},{3,2},{4,5},{5,4},{6,7},{7,6},{8,9},{9,8},{10,11... | collective-permute-start | bytes 1572872 | tf_op jit(solution)/shard_map/ppermute | solution.py:372
  144.3 1.8 %collective-permute-done.16.other_ref = bf16[256,512]{1,0:T(8,128)(2,1)S(1)} collective-permute-done((bf16[256,512]{1,0:T(8,128)(2,1)S(1)}, bf16[256,512]{1,0:T(8,128)(2,1)S(1)}, u32[]{:S(2)}, u32[]{:S(2)}) %collective-permute-start.16) | collective-permute-done | bytes 262176 | tf_op jit(solution)/shard_map/ppermute | solution.py:371
  146.1 2.3 %covariance.1 = bf16[16,32,512]{2,1,0:T(8,128)(2,1)S(1)} custom-call(s32[1]{0:T(128)} %bitcast.d_ref, s32[1]{0:T(128)} %bitcast.13.x_ref, s32[1]{0:T(128)} %bitcast.14.y_ref, bf16[256,512]{1,0:T(8,128)(2,1)S(1)} %get-tuple-element.18.own_ref, bf16[256,512]{1,0:T(8,128)(2,1)S(1)} %collective-permute-done.16.other_ref, ...), custom_call_target="tpu_custom_call" | custom-call | tf_op jit(solution)/shard_map/covariance/pallas_call | solution.py:374
  148.5 13.4 %all_to_all.26.in_ref = bf16[16,32,512]{2,1,0:T(8,128)(2,1)S(1)} all-to-all(bf16[16,32,512]{2,1,0:T(8,128)(2,1)S(1)} %covariance.1), channel_id=1, replica_groups=mesh['x'=4,'y'=4,'z'=8,'dp'=2] {'x','y'}, dimensions={0} | all-to-all | bytes 1048576 | tf_op jit(solution)/shard_map/all_to_all | solution.py:382
  (45 shorter events, 6.3 us)
Async XLA Ops:
  0.6 19.0 %copy-start.4 = (bf16[1024,32]{0,1:T(8,128)(2,1)S(1)}, bf16[1024,32]{0,1:T(8,128)(2,1)}, u32[]{:S(2)}) copy-start(bf16[1024,32]{0,1:T(8,128)(2,1)} %param.13) | copy-start | bytes 196612
  3.3 46.6 %all-to-all-start = ((bf16[128,8,512]{2,1,0:T(8,128)(2,1)}), bf16[128,8,512]{2,1,0:T(8,128)(2,1)S(1)}, u32[]{:S(2)}, u32[]{:S(2)}) async-start(bf16[128,8,512]{2,1,0:T(8,128)(2,1)} %bitcast.26), calls=%async_computation | async-start | bytes 2097152 | tf_op jit(solution)/shard_map/all_to_all | solution.py:277
  19.7 5.8 %collective-permute-start.3 = (bf16[32,512]{1,0:T(8,128)(2,1)S(1)}, bf16[32,512]{1,0:T(8,128)(2,1)S(1)}, u32[]{:S(2)}, u32[]{:S(2)}) collective-permute-start(bf16[32,512]{1,0:T(8,128)(2,1)S(1)} %broadcast_select_fusion.2), channel_id=1, source_target_pairs={{0,1},{1,0},{2,3},{3,2},{4,5},{5,4},{6,7},{7,6},{8,9},{9,8},{10,11... | collective-permute-start | bytes 98312 | tf_op jit(solution)/shard_map/ppermute | solution.py:248
  20.7 7.6 %collective-permute-start = (bf16[32,1024]{1,0:T(8,128)(2,1)S(1)}, bf16[32,1024]{1,0:T(8,128)(2,1)S(1)}, u32[]{:S(2)}, u32[]{:S(2)}) collective-permute-start(bf16[32,1024]{1,0:T(8,128)(2,1)S(1)} %bitcast.28), channel_id=1, source_target_pairs={{0,64},{64,128},{128,192},{192,0},{1,65},{65,129},{129,193},{193,1... | collective-permute-start | bytes 196616 | tf_op jit(solution)/shard_map/ppermute | solution.py:242
  21.7 8.8 %collective-permute-start.1 = (bf16[32,1024]{1,0:T(8,128)(2,1)S(1)}, bf16[32,1024]{1,0:T(8,128)(2,1)S(1)}, u32[]{:S(2)}, u32[]{:S(2)}) collective-permute-start(bf16[32,1024]{1,0:T(8,128)(2,1)S(1)} %bitcast.29), channel_id=1, source_target_pairs={{0,128},{64,192},{128,0},{192,64},{1,129},{65,193},{129,1},{193,65... | collective-permute-start | bytes 196616 | tf_op jit(solution)/shard_map/ppermute | solution.py:242
  24.5 5.9 %collective-permute-start.2 = (bf16[32,1024]{1,0:T(8,128)(2,1)S(1)}, bf16[32,1024]{1,0:T(8,128)(2,1)S(1)}, u32[]{:S(2)}, u32[]{:S(2)}) collective-permute-start(bf16[32,1024]{1,0:T(8,128)(2,1)S(1)} %bitcast.30), channel_id=1, source_target_pairs={{0,192},{64,0},{128,64},{192,128},{1,193},{65,1},{129,65},{193,129... | collective-permute-start | bytes 196616 | tf_op jit(solution)/shard_map/ppermute | solution.py:242
  25.5 17.6 %collective-permute-start.4 = (bf16[64,512]{1,0:T(8,128)(2,1)S(1)}, bf16[64,512]{1,0:T(8,128)(2,1)S(1)}, u32[]{:S(2)}, u32[]{:S(2)}) collective-permute-start(bf16[64,512]{1,0:T(8,128)(2,1)S(1)} %pad_maximum_fusion.2.refs_4_.refs_0_), channel_id=1, source_target_pairs={{0,2},{2,4},{4,6},{6,8},{8,10},{10,12},{12,14},{14,0},{1,3},{3,5},... | collective-permute-start | bytes 196616 | tf_op jit(solution)/shard_map/ppermute | solution.py:242
  26.8 16.3 %collective-permute-start.5 = (bf16[64,512]{1,0:T(8,128)(2,1)S(1)}, bf16[64,512]{1,0:T(8,128)(2,1)S(1)}, u32[]{:S(2)}, u32[]{:S(2)}) collective-permute-start(bf16[64,512]{1,0:T(8,128)(2,1)S(1)} %pad_maximum_fusion.2.refs_4_.refs_0_), channel_id=1, source_target_pairs={{0,14},{2,0},{4,2},{6,4},{8,6},{10,8},{12,10},{14,12},{1,15},{3,1}... | collective-permute-start | bytes 196616 | tf_op jit(solution)/shard_map/ppermute | solution.py:242
  49.9 5.7 %collective-permute-start.6 = (bf16[1024,512]{1,0:T(8,128)(2,1)S(1)}, bf16[1024,512]{1,0:T(8,128)(2,1)S(1)}, u32[]{:S(2)}, u32[]{:S(2)}) collective-permute-start(bf16[1024,512]{1,0:T(8,128)(2,1)S(1)} %order.1.own_ref), channel_id=1, source_target_pairs={{0,1},{1,0},{2,3},{3,2},{4,5},{5,4},{6,7},{7,6},{8,9},{9,8},{10,11... | collective-permute-start | bytes 3145736 | tf_op jit(solution)/shard_map/ppermute | solution.py:289
  55.5 9.1 %copy-start = (bf16[1,1024,1024]{2,1,0:T(8,128)(2,1)S(1)}, bf16[1,1024,1024]{2,1,0:T(8,128)(2,1)}, u32[]{:S(2)}) copy-start(bf16[1,1024,1024]{2,1,0:T(8,128)(2,1)} %param.12) | copy-start | bytes 6291460
  64.2 2.8 %collective-permute-start.7 = (bf16[1024,512]{1,0:T(8,128)(2,1)S(1)}, bf16[1024,512]{1,0:T(8,128)(2,1)S(1)}, u32[]{:S(2)}, u32[]{:S(2)}) collective-permute-start(bf16[1024,512]{1,0:T(8,128)(2,1)S(1)} %get-tuple-element.13), channel_id=1, source_target_pairs={{0,1},{1,0},{2,3},{3,2},{4,5},{5,4},{6,7},{7,6},{8,9},{9,8},{10,11... | collective-permute-start | bytes 3145736 | tf_op jit(solution)/shard_map/ppermute | solution.py:315
  68.1 13.7 %copy-start.5 = (s32[8]{0:T(128)S(1)}, s32[8]{0:T(128)}, u32[]{:S(2)}) copy-start(s32[8]{0:T(128)} %param.15) | copy-start | bytes 100
  68.1 38.0 %copy-start.1 = (bf16[128,1024]{1,0:T(8,128)(2,1)S(1)}, bf16[128,1024]{1,0:T(8,128)(2,1)}, u32[]{:S(2)}) copy-start(bf16[128,1024]{1,0:T(8,128)(2,1)} %tok_ref.1) | copy-start | bytes 786436
  68.1 38.0 %copy-start.2 = (bf16[1024,128]{1,0:T(8,128)(2,1)S(1)}, bf16[1024,128]{1,0:T(8,128)(2,1)}, u32[]{:S(2)}) copy-start(bf16[1024,128]{1,0:T(8,128)(2,1)} %get-tuple-element.14.high_ref) | copy-start | bytes 786436
  68.1 38.0 %copy-start.3 = (bf16[1024,128]{1,0:T(8,128)(2,1)S(1)}, bf16[1024,128]{1,0:T(8,128)(2,1)}, u32[]{:S(2)}) copy-start(bf16[1024,128]{1,0:T(8,128)(2,1)} %get-tuple-element.15.low_ref) | copy-start | bytes 786436
  68.1 38.0 %all-to-all-start.1 = ((bf16[128,8,512]{2,1,0:T(8,128)(2,1)}), bf16[128,8,512]{2,1,0:T(8,128)(2,1)S(1)}, u32[]{:S(2)}, u32[]{:S(2)}) async-start(bf16[128,8,512]{2,1,0:T(8,128)(2,1)} %bitcast.10), calls=%async_computation.1 | async-start | bytes 2097152 | tf_op jit(solution)/shard_map/all_to_all | solution.py:333
  74.6 26.8 %collective-permute-start.10 = (bf16[128,1024]{1,0:T(8,128)(2,1)S(1)}, bf16[128,1024]{1,0:T(8,128)(2,1)S(1)}, u32[]{:S(2)}, u32[]{:S(2)}) collective-permute-start(bf16[128,1024]{1,0:T(8,128)(2,1)S(1)} %pad_maximum_fusion.refs_1_.plane0), channel_id=1, source_target_pairs={{0,48},{16,0},{32,16},{48,32},{1,49},{17,1},{33,17},{49,33},{2,50}... | collective-permute-start | bytes 786440 | tf_op jit(solution)/shard_map/ppermute | solution.py:242
  76.5 24.9 %collective-permute-start.8 = (bf16[128,1024]{1,0:T(8,128)(2,1)S(1)}, bf16[128,1024]{1,0:T(8,128)(2,1)S(1)}, u32[]{:S(2)}, u32[]{:S(2)}) collective-permute-start(bf16[128,1024]{1,0:T(8,128)(2,1)S(1)} %pad_maximum_fusion.refs_1_.plane0), channel_id=1, source_target_pairs={{0,16},{16,32},{32,48},{48,0},{1,17},{17,33},{33,49},{49,1},{2,18}... | collective-permute-start | bytes 786440 | tf_op jit(solution)/shard_map/ppermute | solution.py:242
  76.5 24.9 %collective-permute-start.9 = (bf16[128,1024]{1,0:T(8,128)(2,1)S(1)}, bf16[128,1024]{1,0:T(8,128)(2,1)S(1)}, u32[]{:S(2)}, u32[]{:S(2)}) collective-permute-start(bf16[128,1024]{1,0:T(8,128)(2,1)S(1)} %pad_maximum_fusion.refs_1_.plane0), channel_id=1, source_target_pairs={{0,32},{16,48},{32,0},{48,16},{1,33},{17,49},{33,1},{49,17},{2,34}... | collective-permute-start | bytes 786440 | tf_op jit(solution)/shard_map/ppermute | solution.py:242
  78.2 23.2 %collective-permute-start.11 = (bf16[64,512]{1,0:T(8,128)(2,1)S(1)}, bf16[64,512]{1,0:T(8,128)(2,1)S(1)}, u32[]{:S(2)}, u32[]{:S(2)}) collective-permute-start(bf16[64,512]{1,0:T(8,128)(2,1)S(1)} %pad_maximum_fusion.2.refs_4_.refs_0_), channel_id=1, source_target_pairs={{0,4},{2,6},{4,8},{6,10},{8,12},{10,14},{12,0},{14,2},{1,5},{3,7},... | collective-permute-start | bytes 196616 | tf_op jit(solution)/shard_map/ppermute | solution.py:242
  80.3 21.1 %collective-permute-start.12 = (bf16[64,512]{1,0:T(8,128)(2,1)S(1)}, bf16[64,512]{1,0:T(8,128)(2,1)S(1)}, u32[]{:S(2)}, u32[]{:S(2)}) collective-permute-start(bf16[64,512]{1,0:T(8,128)(2,1)S(1)} %pad_maximum_fusion.2.refs_4_.refs_0_), channel_id=1, source_target_pairs={{0,12},{2,14},{4,0},{6,2},{8,4},{10,6},{12,8},{14,10},{1,13},{3,15... | collective-permute-start | bytes 196616 | tf_op jit(solution)/shard_map/ppermute | solution.py:242
  118.8 20.1 %all-to-all-start.3 = ((bf16[16,72,512]{2,1,0:T(8,128)(2,1)}), bf16[16,72,512]{2,1,0:T(8,128)(2,1)S(1)}, u32[]{:S(2)}, u32[]{:S(2)}) async-start(bf16[16,72,512]{2,1,0:T(8,128)(2,1)} %broadcast_in_dim.2), calls=%async_computation.3 | async-start | bytes 2359296 | tf_op jit(solution)/shard_map/all_to_all | solution.py:357
  123.0 16.2 %collective-permute-start.13 = (bf16[64,512]{1,0:T(8,128)(2,1)S(1)}, bf16[64,512]{1,0:T(8,128)(2,1)S(1)}, u32[]{:S(2)}, u32[]{:S(2)}) collective-permute-start(bf16[64,512]{1,0:T(8,128)(2,1)S(1)} %pad_maximum_fusion.2.refs_4_.refs_0_), channel_id=1, source_target_pairs={{0,6},{2,8},{4,10},{6,12},{8,14},{10,0},{12,2},{14,4},{1,7},{3,9},... | collective-permute-start | bytes 196616 | tf_op jit(solution)/shard_map/ppermute | solution.py:242
  123.1 16.1 %collective-permute-start.14 = (bf16[64,512]{1,0:T(8,128)(2,1)S(1)}, bf16[64,512]{1,0:T(8,128)(2,1)S(1)}, u32[]{:S(2)}, u32[]{:S(2)}) collective-permute-start(bf16[64,512]{1,0:T(8,128)(2,1)S(1)} %pad_maximum_fusion.2.refs_4_.refs_0_), channel_id=1, source_target_pairs={{0,8},{2,10},{4,12},{6,14},{8,0},{10,2},{12,4},{14,6},{1,9},{3,11}... | collective-permute-start | bytes 196616 | tf_op jit(solution)/shard_map/ppermute | solution.py:242
  125.7 13.6 %collective-permute-start.15 = (bf16[64,512]{1,0:T(8,128)(2,1)S(1)}, bf16[64,512]{1,0:T(8,128)(2,1)S(1)}, u32[]{:S(2)}, u32[]{:S(2)}) collective-permute-start(bf16[64,512]{1,0:T(8,128)(2,1)S(1)} %pad_maximum_fusion.2.refs_4_.refs_0_), channel_id=1, source_target_pairs={{0,10},{2,12},{4,14},{6,0},{8,2},{10,4},{12,6},{14,8},{1,11},{3,13... | collective-permute-start | bytes 196616 | tf_op jit(solution)/shard_map/ppermute | solution.py:242
  140.4 5.7 %collective-permute-start.17 = (f32[512,256]{1,0:T(8,128)S(1)}, f32[512,256]{1,0:T(8,128)S(1)}, u32[]{:S(2)}, u32[]{:S(2)}) collective-permute-start(f32[512,256]{1,0:T(8,128)S(1)} %get-tuple-element.19.cols_ref), channel_id=1, source_target_pairs={{0,1},{1,0},{2,3},{3,2},{4,5},{5,4},{6,7},{7,6},{8,9},{9,8},{10,11... | collective-permute-start | bytes 1572872 | tf_op jit(solution)/shard_map/ppermute | solution.py:372
  144.2 1.9 %collective-permute-start.16 = (bf16[256,512]{1,0:T(8,128)(2,1)S(1)}, bf16[256,512]{1,0:T(8,128)(2,1)S(1)}, u32[]{:S(2)}, u32[]{:S(2)}) collective-permute-start(bf16[256,512]{1,0:T(8,128)(2,1)S(1)} %get-tuple-element.18.own_ref), channel_id=1, source_target_pairs={{0,1},{1,0},{2,3},{3,2},{4,5},{5,4},{6,7},{7,6},{8,9},{9,8},{10,11... | collective-permute-start | bytes 786440 | tf_op jit(solution)/shard_map/ppermute | solution.py:371

commit v4 on v3

--- a/solution.py
+++ b/solution.py
@@ -38,31 +38,11 @@
     return pl.ds(pl.multiple_of(start * size, LANES), size)
 
 
-def prep_kernel(
-    capacity, d_ref, tok_hbm, router_hbm, ids_hbm, out_ref, high_ref, low_ref, tok_ref, router_ref, ids_ref, sems
-):
-    copies = [
-        pltpu.make_async_copy(source, target, sems.at[k])
-        for k, (source, target) in enumerate(
-            ((tok_hbm, tok_ref), (router_hbm, router_ref), (ids_hbm, ids_ref))
-        )
-    ]
-    for copy in copies:
-        copy.start()
-    for copy in copies:
-        copy.wait()
-    d = d_ref[0]
-    rows, width = tok_ref.shape
-    experts = router_ref.shape[0]
-    logits = dot_nt(router_ref[...], tok_ref[...])
+def slots_taken(ids_ref, shape):
+    experts, rows, capacity = shape
     number = lax.broadcasted_iota(jnp.int32, (experts, rows), 0)
     hot0 = ids_ref[0:1, :] == number
     hot1 = ids_ref[1:2, :] == number
-    chosen0 = jnp.sum(jnp.where(hot0, logits, 0.0), axis=0, keepdims=True)
-    chosen1 = jnp.sum(jnp.where(hot1, logits, 0.0), axis=0, keepdims=True)
-    gate = jnp.where(hot0, jax.nn.sigmoid(chosen0 - chosen1), 0.0) + jnp.where(
-        hot1, jax.nn.sigmoid(chosen1 - chosen0), 0.0
-    )
     member = jnp.where(hot0 | hot1, 1.0, 0.0)
     before = lax.broadcasted_iota(jnp.int32, (rows, rows), 0) < lax.broadcasted_iota(
         jnp.int32, (rows, rows), 1
@@ -70,13 +50,37 @@
     earlier = dot(member.astype(BF16), jnp.where(before, 1.0, 0.0).astype(BF16))
     place = jnp.where(member > 0.0, earlier, -1.0)
     slots = lax.broadcasted_iota(jnp.int32, (experts, 2, capacity, rows), 2).astype(F32)
-    taken = place[:, None, None, :] == slots
-    picks = jnp.where(taken, 1.0, 0.0).reshape(experts * 2 * capacity, rows)
+    return hot0, hot1, place[:, None, None, :] == slots
+
+
+def prep_kernel(experts, capacity, d_ref, tok_hbm, ids_hbm, out_ref, tok_ref, ids_ref, sems):
+    copies = [
+        pltpu.make_async_copy(source, target, sems.at[k])
+        for k, (source, target) in enumerate(((ids_hbm, ids_ref), (tok_hbm, tok_ref)))
+    ]
+    for copy in copies:
+        copy.start()
+    d = d_ref[0]
+    rows, width = tok_ref.shape
+    copies[0].wait()
+    _, _, taken = slots_taken(ids_ref, (experts, rows, capacity))
+    picks = jnp.where(taken, 1.0, 0.0).reshape(experts * 2 * capacity, rows).astype(BF16)
+    copies[1].wait()
+    out_ref[...] = dot(picks, tok_ref[:, half(d, width // 2)]).astype(BF16)
+
+
+def gate_kernel(capacity, tok_ref, router_ref, ids_ref, high_ref, low_ref):
+    rows = tok_ref.shape[0]
+    experts = router_ref.shape[0]
+    logits = dot_nt(router_ref[...], tok_ref[...])
+    hot0, hot1, taken = slots_taken(ids_ref, (experts, rows, capacity))
+    chosen0 = jnp.sum(jnp.where(hot0, logits, 0.0), axis=0, keepdims=True)
+    chosen1 = jnp.sum(jnp.where(hot1, logits, 0.0), axis=0, keepdims=True)
+    gate = jnp.where(hot0, jax.nn.sigmoid(chosen0 - chosen1), 0.0) + jnp.where(
+        hot1, jax.nn.sigmoid(chosen1 - chosen0), 0.0
+    )
     weights = jnp.where(taken, gate[:, None, None, :], 0.0).reshape(experts * 2 * capacity, rows)
-    high, low = split2(weights)
-    high_ref[...] = high
-    low_ref[...] = low
-    out_ref[...] = dot(picks.astype(BF16), tok_ref[:, half(d, width // 2)]).astype(BF16)
+    high_ref[...], low_ref[...] = split2(weights)
 
 
 def order_kernel(*refs):
@@ -106,27 +110,17 @@
     x_ref[:, half(d, part)] = own_ref[...]
     x_ref[:, half(1 - d, part)] = other_ref[...]
 
+    steps = [slice(m * step, (m + 1) * step) for m in range(rows // step)]
     for pair, span in zip(loads, spans):
         for load in pair:
             load.wait()
-
-        def body(m, carry, span=span):
-            at = pl.ds(pl.multiple_of(m * step, step), step)
+        for at in steps:
             gate = dot(x_ref[at, :], gate_ref[:, span])
             upper = dot(x_ref[at, :], up_ref[:, span])
             hid_ref[at, span] = (gate * jax.nn.sigmoid(gate) * upper).astype(BF16)
-            return carry
-
-        lax.fori_loop(0, rows // step, body, 0)
-
     load_down.wait()
-
-    def last(m, carry):
-        at = pl.ds(pl.multiple_of(m * step, step), step)
+    for at in steps:
         out_ref[at, :] = dot(hid_ref[at, :], down_ref[:, half(1 - d, part)]).astype(BF16)
-        return carry
-
-    lax.fori_loop(0, rows // step, last, 0)
 
 
 def own_kernel(d_ref, hid_ref, down_ref, out_ref):
@@ -160,8 +154,7 @@
         payload_ref[k] = block
 
 
-def clip_kernel(length, used, z_ref, frames_ref, digits_ref, *refs):
-    line_refs, (clips_ref, embed_ref) = refs[:-2], refs[-2:]
+def clip_kernel(length, used, frames_ref, digits_ref, clips_ref):
     clips, part = clips_ref.shape
     groups = frames_ref.shape[0]
     digits = digits_ref[...].astype(F32)
@@ -172,10 +165,16 @@
     frames = frames_ref[:, 0:used, :].reshape(groups * used, part)
     pooled = (dot(picks, frames) / length).astype(BF16)
     clips_ref[...] = pooled
+
+
+def line_kernel(z_ref, clips_ref, *refs):
+    line_refs, embed_ref = refs[:-1], refs[-1]
+    pooled = clips_ref[...]
     count, chunk = len(line_refs), line_refs[0].shape[0]
-    for k, ref in enumerate(line_refs):
+    embed = dot_nt(jnp.concatenate([ref[...] for ref in line_refs], axis=0), pooled)
+    for k in range(count):
         to = pl.ds(pl.multiple_of(lax.rem(z_ref[0] + count - k, count) * chunk, chunk), chunk)
-        embed_ref[to, :] = dot_nt(ref[...], pooled)
+        embed_ref[to, :] = embed[k * chunk : (k + 1) * chunk]
 
 
 def cov_kernel(
@@ -190,13 +189,17 @@
         return embed - jnp.mean(embed, axis=1, keepdims=True)
 
     cols_high, cols_low = split2(center(cols_ref[...] + cols_other_ref[...]))
-    for j, ref in enumerate((plane0, plane1, plane2, plane3)):
-        embed = dot_nt(ref[:, half(d, part)], own) + dot_nt(ref[:, half(1 - d, part)], other)
-        rows_high, rows_low = split2(center(embed) / (clips - 1))
-        block = dot_nt(rows_high, cols_high) + dot_nt(rows_high, cols_low) + dot_nt(rows_low, cols_high)
+    planes = (plane0, plane1, plane2, plane3)
+    mine = jnp.concatenate([ref[:, half(d, part)] for ref in planes], axis=0)
+    theirs = jnp.concatenate([ref[:, half(1 - d, part)] for ref in planes], axis=0)
+    rows_high, rows_low = split2(center(dot_nt(mine, own) + dot_nt(theirs, other)) / (clips - 1))
+    block = dot_nt(rows_high, cols_high) + dot_nt(rows_high, cols_low) + dot_nt(rows_low, cols_high)
+    block = block.astype(BF16)
+    for j in range(4):
         for i in range(4):
             peer = 4 * lax.rem(x + 4 - i, 4) + lax.rem(y + 4 - j, 4)
-            out_ref[peer] = block[i * share : (i + 1) * share].astype(BF16)
+            k = 4 * j + i
+            out_ref[peer] = block[k * share : (k + 1) * share]
 
 
 def place_kernel(in_ref, out_ref):
@@ -255,28 +258,35 @@
 
     vmem = pl.BlockSpec(memory_space=pltpu.VMEM)
     hbm = pl.BlockSpec(memory_space=pl.ANY)
-    outgoing, high, low = pl.pallas_call(
-        functools.partial(prep_kernel, capacity),
-        out_shape=(
-            jax.ShapeDtypeStruct((rows, part), BF16),
-            jax.ShapeDtypeStruct((rows, tok_rows), BF16),
-            jax.ShapeDtypeStruct((rows, tok_rows), BF16),
-        ),
-        in_specs=[SCALAR, hbm, hbm, hbm],
-        out_specs=(vmem, vmem, vmem),
+    outgoing = pl.pallas_call(
+        functools.partial(prep_kernel, experts, capacity),
+        out_shape=jax.ShapeDtypeStruct((rows, part), BF16),
+        in_specs=[SCALAR, hbm, hbm],
+        out_specs=vmem,
         scratch_shapes=[
             pltpu.VMEM(tokens.shape, BF16),
-            pltpu.VMEM((experts, width), BF16),
             pltpu.VMEM((2, tok_rows), jnp.int32),
-            pltpu.SemaphoreType.DMA((3,)),
+            pltpu.SemaphoreType.DMA((2,)),
         ],
         compiler_params=pltpu.CompilerParams(vmem_limit_bytes=57 * 2**20),
         name="prep",
-    )(d, tokens, router_weight.T, expert_ids.T)
+    )(d, tokens, expert_ids.T)
+    high, low = pl.pallas_call(
+        functools.partial(gate_kernel, capacity),
+        out_shape=[jax.ShapeDtypeStruct((rows, tok_rows), BF16)] * 2,
+        in_specs=[vmem] * 3,
+        out_specs=(vmem, vmem),
+        compiler_params=params,
+        cost_estimate=pl.CostEstimate(
+            flops=2 * tok_rows * width * experts, bytes_accessed=0, transcendentals=0
+        ),
+        name="gates",
+    )(tokens, router_weight.T, expert_ids.T)
 
     received = lax.all_to_all(
         outgoing.reshape(n_expert, capacity, part), EXP, split_axis=0, concat_axis=0, tiled=True
     ).reshape(rows, part)
+    with_dispatch = (high, low, *with_dispatch)
     received = pl.pallas_call(
         order_kernel,
         out_shape=jax.ShapeDtypeStruct((rows, part), BF16),
@@ -357,18 +367,26 @@
     gathered = lax.all_to_all(copies, PLANE, split_axis=0, concat_axis=0, tiled=True)
     digits = gathered[:, used, : 2 * used].reshape(n_xy, n_z, 2, count)
     digits = digits.transpose(2, 0, 1, 3).reshape(2, frame_total)
-    clips, embed = pl.pallas_call(
+    clips = pl.pallas_call(
         functools.partial(clip_kernel, 4, used),
-        out_shape=(
-            jax.ShapeDtypeStruct((clip_total, part), BF16),
-            jax.ShapeDtypeStruct((wide, clip_total), F32),
-        ),
-        in_specs=[SCALAR] + [vmem] * (2 + n_z),
-        out_specs=(vmem, vmem),
+        out_shape=jax.ShapeDtypeStruct((clip_total, part), BF16),
+        in_specs=[vmem, vmem],
+        out_specs=vmem,
         compiler_params=params,
         name="clips",
-    )(z, gathered, digits, *line)
+    )(gathered, digits)
     other_clips = lax.ppermute(clips, "dp", swap)
+    embed = pl.pallas_call(
+        line_kernel,
+        out_shape=jax.ShapeDtypeStruct((wide, clip_total), F32),
+        in_specs=[SCALAR] + [vmem] * (1 + n_z),
+        out_specs=vmem,
+        compiler_params=params,
+        cost_estimate=pl.CostEstimate(
+            flops=2 * wide * part * clip_total, bytes_accessed=0, transcendentals=0
+        ),
+        name="line",
+    )(z, clips, *line)
     other_embed = lax.ppermute(embed, "dp", swap)
 
     blocks = pl.pallas_call(

time: 164 us -> 161 us (0.982)
  Pallas kernels: 19.4 us -> 17.4 us
    pallas_call x2 -> x4, Pallas kernels: 3.76 us -> 3.54 us  [the longest x1 2.43 us: per_device(): pl.pallas_call(functools.partial(prep_kernel, experts, capacity), out_sha...]
where the time goes in v4:
time: 161 us; the launch traced here: 160 us
  waiting for transfers between devices  61.2 us (38%)
  starting transfers between devices  55.5 us (34%)
  blocking collectives  23.8 us (15%)
  Pallas kernels  17.4 us (11%)
    ppermute x13, waiting for transfers between devices, ring(): lax.ppermute(block, axis, [(k, (k + step) % size) for k in range(size)])  34 us
    ppermute x13, starting transfers between devices, ring(): lax.ppermute(block, axis, [(k, (k + step) % size) for k in range(size)])  19.7 us
    all_to_all x1, starting transfers between devices, per_device(): lax.all_to_all(outgoing.reshape(n_expert, capacity, part), EXP, split_axi...  16.3 us
    all_to_all x1, blocking collectives, per_device(): lax.all_to_all(blocks, PLANE, split_axis=0, concat_axis=0, tiled=True)  13.4 us
    all_to_all x1, waiting for transfers between devices, per_device(): lax.all_to_all(copies, PLANE, split_axis=0, concat_axis=0, tiled=True)  10.8 us
    all_to_all x1, blocking collectives, per_device(): got = lax.all_to_all(payload, 'z', split_axis=0, concat_axis=0, tiled=True)  10.4 us
    pallas_call x1, Pallas kernels, per_device(): pl.pallas_call(functools.partial(ffn_kernel, 512), out_shape=(jax.ShapeDt...  7.78 us
    all_to_all x1, waiting for transfers between devices, per_device(): lax.all_to_all(outgoing.reshape(n_expert, capacity, part), EXP, split_axi...  6.72 us
  transfers between devices with their start and end apart: 21, of which 9 were waited for; matrix products, arithmetic and copies ran while one was open for 0% of the time, Pallas kernels for 1%

profile of v4, /device:TPU:1, one launch (start us, length us, event | category | flops | bytes accessed | tf_op | source)
XLA Modules:
  0.0 160.4 jit_solution(2365404734019508557)
XLA Ops:
  0.7 2.4 %prep.1 = bf16[1024,512]{1,0:T(8,128)(2,1)} custom-call(s32[1]{0:T(128)} %bitcast.d_ref, bf16[128,1024]{1,0:T(8,128)(2,1)} %tok_ref.3, s32[2,128]{1,0:T(2,128)} %bitcast.27), custom_call_target="tpu_custom_call" | custom-call | tf_op jit(solution)/shard_map/prep/pallas_call | solution.py:261
  3.1 16.3 %all-to-all-start = ((bf16[128,8,512]{2,1,0:T(8,128)(2,1)}), bf16[128,8,512]{2,1,0:T(8,128)(2,1)S(1)}, u32[]{:S(2)}, u32[]{:S(2)}) async-start(bf16[128,8,512]{2,1,0:T(8,128)(2,1)} %bitcast.29), calls=%async_computation | async-start | bytes 2097152 | tf_op jit(solution)/shard_map/all_to_all | solution.py:286
  19.5 1.0 collective-permute-start.3
  21.5 2.8 %collective-permute-start.1 = (bf16[32,1024]{1,0:T(8,128)(2,1)S(1)}, bf16[32,1024]{1,0:T(8,128)(2,1)S(1)}, u32[]{:S(2)}, u32[]{:S(2)}) collective-permute-start(bf16[32,1024]{1,0:T(8,128)(2,1)S(1)} %bitcast.32), channel_id=1, source_target_pairs={{0,128},{64,192},{128,0},{192,64},{1,129},{65,193},{129,1},{193,65... | collective-permute-start | bytes 196616 | tf_op jit(solution)/shard_map/ppermute | solution.py:245
  25.7 1.3 collective-permute-start.4
  27.0 1.5 collective-permute-start.5
  28.5 1.8 %collective-permute-done.1 = bf16[32,1024]{1,0:T(8,128)(2,1)S(1)} collective-permute-done((bf16[32,1024]{1,0:T(8,128)(2,1)S(1)}, bf16[32,1024]{1,0:T(8,128)(2,1)S(1)}, u32[]{:S(2)}, u32[]{:S(2)}) %collective-permute-start.1) | collective-permute-done | bytes 65568 | tf_op jit(solution)/shard_map/ppermute | solution.py:245
  30.3 12.7 %collective-permute-done.4.refs_4_.refs_1_ = bf16[64,512]{1,0:T(8,128)(2,1)S(1)} collective-permute-done((bf16[64,512]{1,0:T(8,128)(2,1)S(1)}, bf16[64,512]{1,0:T(8,128)(2,1)S(1)}, u32[]{:S(2)}, u32[]{:S(2)}) %collective-permute-start.4) | collective-permute-done | bytes 65568 | tf_op jit(solution)/shard_map/ppermute | solution.py:245
  43.0 6.7 %all-to-all-done = bf16[128,8,512]{2,1,0:T(8,128)(2,1)S(1)} async-done(((bf16[128,8,512]{2,1,0:T(8,128)(2,1)}), bf16[128,8,512]{2,1,0:T(8,128)(2,1)S(1)}, u32[]{:S(2)}, u32[]{:S(2)}) %all-to-all-start) | async-done | bytes 1048608 | tf_op jit(solution)/shard_map/all_to_all | solution.py:286
  49.7 3.4 %collective-permute-start.6 = (bf16[1024,512]{1,0:T(8,128)(2,1)S(1)}, bf16[1024,512]{1,0:T(8,128)(2,1)S(1)}, u32[]{:S(2)}, u32[]{:S(2)}) collective-permute-start(bf16[1024,512]{1,0:T(8,128)(2,1)S(1)} %order.1.own_ref), channel_id=1, source_target_pairs={{0,1},{1,0},{2,3},{3,2},{4,5},{5,4},{6,7},{7,6},{8,9},{9,8},{10,11... | collective-permute-start | bytes 3145736 | tf_op jit(solution)/shard_map/ppermute | solution.py:299
  53.1 2.3 %collective-permute-done.6.other_ref = bf16[1024,512]{1,0:T(8,128)(2,1)S(1)} collective-permute-done((bf16[1024,512]{1,0:T(8,128)(2,1)S(1)}, bf16[1024,512]{1,0:T(8,128)(2,1)S(1)}, u32[]{:S(2)}, u32[]{:S(2)}) %collective-permute-start.6) | collective-permute-done | bytes 1048608 | tf_op jit(solution)/shard_map/ppermute | solution.py:299
  55.3 7.8 %ffn.1 = (bf16[1024,1024]{1,0:T(8,128)(2,1)S(1)}, bf16[1024,512]{1,0:T(8,128)(2,1)S(1)}) custom-call(s32[1]{0:T(128)} %bitcast.d_ref, bf16[1024,512]{1,0:T(8,128)(2,1)S(1)} %order.1.own_ref, bf16[1024,512]{1,0:T(8,128)(2,1)S(1)} %collective-permute-done.6.other_ref, bf16[1024,1024]{1,0:T(8,128)(2,1)} %bitcast.38, bf16[1024,1024]{1,0:T(8,128)(2,1)} %bitcast.39, ...), custom_call_target="tpu_custom_call" | custom-call | flops 5368709120 | tf_op jit(solution)/shard_map/ffn/pallas_call | solution.py:302
  63.6 1.3 ours.1.own_ref
  65.9 1.1 total.1
  67.0 6.3 %all-to-all-start.1 = ((bf16[128,8,512]{2,1,0:T(8,128)(2,1)}), bf16[128,8,512]{2,1,0:T(8,128)(2,1)S(1)}, u32[]{:S(2)}, u32[]{:S(2)}) async-start(bf16[128,8,512]{2,1,0:T(8,128)(2,1)} %bitcast.10), calls=%async_computation.1 | async-start | bytes 2097152 | tf_op jit(solution)/shard_map/all_to_all | solution.py:343
  73.4 1.9 %collective-permute-start.10 = (bf16[128,1024]{1,0:T(8,128)(2,1)S(1)}, bf16[128,1024]{1,0:T(8,128)(2,1)S(1)}, u32[]{:S(2)}, u32[]{:S(2)}) collective-permute-start(bf16[128,1024]{1,0:T(8,128)(2,1)S(1)} %pad_maximum_fusion.refs_3_.plane0), channel_id=1, source_target_pairs={{0,48},{16,0},{32,16},{48,32},{1,49},{17,1},{33,17},{49,33},{2,50}... | collective-permute-start | bytes 786440 | tf_op jit(solution)/shard_map/ppermute | solution.py:245
  75.3 1.7 %collective-permute-start.9 = (bf16[128,1024]{1,0:T(8,128)(2,1)S(1)}, bf16[128,1024]{1,0:T(8,128)(2,1)S(1)}, u32[]{:S(2)}, u32[]{:S(2)}) collective-permute-start(bf16[128,1024]{1,0:T(8,128)(2,1)S(1)} %pad_maximum_fusion.refs_3_.plane0), channel_id=1, source_target_pairs={{0,32},{16,48},{32,0},{48,16},{1,33},{17,49},{33,1},{49,17},{2,34}... | collective-permute-start | bytes 786440 | tf_op jit(solution)/shard_map/ppermute | solution.py:245
  77.0 2.1 %collective-permute-start.11 = (bf16[64,512]{1,0:T(8,128)(2,1)S(1)}, bf16[64,512]{1,0:T(8,128)(2,1)S(1)}, u32[]{:S(2)}, u32[]{:S(2)}) collective-permute-start(bf16[64,512]{1,0:T(8,128)(2,1)S(1)} %pad_maximum_fusion.2.refs_6_.refs_0_), channel_id=1, source_target_pairs={{0,4},{2,6},{4,8},{6,10},{8,12},{10,14},{12,0},{14,2},{1,5},{3,7},... | collective-permute-start | bytes 196616 | tf_op jit(solution)/shard_map/ppermute | solution.py:245
  79.1 1.5 collective-permute-start.12
  80.6 19.6 %collective-permute-done.11.refs_3_.refs_2_ = bf16[64,512]{1,0:T(8,128)(2,1)S(1)} collective-permute-done((bf16[64,512]{1,0:T(8,128)(2,1)S(1)}, bf16[64,512]{1,0:T(8,128)(2,1)S(1)}, u32[]{:S(2)}, u32[]{:S(2)}) %collective-permute-start.11) | collective-permute-done | bytes 65568 | tf_op jit(solution)/shard_map/ppermute | solution.py:245
  100.2 4.6 %all-to-all-done.1 = bf16[128,8,512]{2,1,0:T(8,128)(2,1)S(1)} async-done(((bf16[128,8,512]{2,1,0:T(8,128)(2,1)}), bf16[128,8,512]{2,1,0:T(8,128)(2,1)S(1)}, u32[]{:S(2)}, u32[]{:S(2)}) %all-to-all-start.1) | async-done | bytes 1048608 | tf_op jit(solution)/shard_map/all_to_all | solution.py:343
  104.8 1.2 combine.1
  106.0 10.4 %all_to_all.25 = bf16[8,16,512]{2,1,0:T(8,128)(2,1)S(1)} all-to-all(bf16[8,16,512]{2,1,0:T(8,128)(2,1)S(1)} %get-tuple-element.13), channel_id=1, replica_groups=mesh['x'=4,'y'=4,'z'=8,'dp'=2] {'z'}, dimensions={0} | all-to-all | bytes 262144 | tf_op jit(solution)/shard_map/all_to_all | solution.py:359
  116.4 1.1 broadcast_in_dim.2
  117.5 4.2 %all-to-all-start.3 = ((bf16[16,72,512]{2,1,0:T(8,128)(2,1)}), bf16[16,72,512]{2,1,0:T(8,128)(2,1)S(1)}, u32[]{:S(2)}, u32[]{:S(2)}) async-start(bf16[16,72,512]{2,1,0:T(8,128)(2,1)} %broadcast_in_dim.2), calls=%async_computation.3 | async-start | bytes 2359296 | tf_op jit(solution)/shard_map/all_to_all | solution.py:367
  121.8 2.5 %collective-permute-start.15 = (bf16[64,512]{1,0:T(8,128)(2,1)S(1)}, bf16[64,512]{1,0:T(8,128)(2,1)S(1)}, u32[]{:S(2)}, u32[]{:S(2)}) collective-permute-start(bf16[64,512]{1,0:T(8,128)(2,1)S(1)} %pad_maximum_fusion.2.refs_6_.refs_0_), channel_id=1, source_target_pairs={{0,8},{2,10},{4,12},{6,14},{8,0},{10,2},{12,4},{14,6},{1,9},{3,11}... | collective-permute-start | bytes 196616 | tf_op jit(solution)/shard_map/ppermute | solution.py:245
  124.4 2.4 %collective-permute-start.16 = (bf16[64,512]{1,0:T(8,128)(2,1)S(1)}, bf16[64,512]{1,0:T(8,128)(2,1)S(1)}, u32[]{:S(2)}, u32[]{:S(2)}) collective-permute-start(bf16[64,512]{1,0:T(8,128)(2,1)S(1)} %pad_maximum_fusion.2.refs_6_.refs_0_), channel_id=1, source_target_pairs={{0,10},{2,12},{4,14},{6,0},{8,2},{10,4},{12,6},{14,8},{1,11},{3,13... | collective-permute-start | bytes 196616 | tf_op jit(solution)/shard_map/ppermute | solution.py:245
  126.8 10.8 %all-to-all-done.3.frames_ref = bf16[16,72,512]{2,1,0:T(8,128)(2,1)S(1)} async-done(((bf16[16,72,512]{2,1,0:T(8,128)(2,1)}), bf16[16,72,512]{2,1,0:T(8,128)(2,1)S(1)}, u32[]{:S(2)}, u32[]{:S(2)}) %all-to-all-start.3) | async-done | bytes 1179680 | tf_op jit(solution)/shard_map/all_to_all | solution.py:367
  138.7 3.8 %collective-permute-start.17 = (f32[512,256]{1,0:T(8,128)S(1)}, f32[512,256]{1,0:T(8,128)S(1)}, u32[]{:S(2)}, u32[]{:S(2)}) collective-permute-start(f32[512,256]{1,0:T(8,128)S(1)} %line.1.cols_ref), channel_id=1, source_target_pairs={{0,1},{1,0},{2,3},{3,2},{4,5},{5,4},{6,7},{7,6},{8,9},{9,8},{10,11... | collective-permute-start | bytes 1572872 | tf_op jit(solution)/shard_map/ppermute | solution.py:390
  142.7 1.8 %collective-permute-done.13.other_ref = bf16[256,512]{1,0:T(8,128)(2,1)S(1)} collective-permute-done((bf16[256,512]{1,0:T(8,128)(2,1)S(1)}, bf16[256,512]{1,0:T(8,128)(2,1)S(1)}, u32[]{:S(2)}, u32[]{:S(2)}) %collective-permute-start.13) | collective-permute-done | bytes 262176 | tf_op jit(solution)/shard_map/ppermute | solution.py:378
  144.5 1.5 covariance.1
  145.9 13.4 %all_to_all.26.in_ref = bf16[16,32,512]{2,1,0:T(8,128)(2,1)S(1)} all-to-all(bf16[16,32,512]{2,1,0:T(8,128)(2,1)S(1)} %covariance.1), channel_id=1, replica_groups=mesh['x'=4,'y'=4,'z'=8,'dp'=2] {'x','y'}, dimensions={0} | all-to-all | bytes 1048576 | tf_op jit(solution)/shard_map/all_to_all | solution.py:400
  (47 shorter events, 6.3 us)
Async XLA Ops:
  0.6 24.7 %copy-start.3 = (s32[128,2]{0,1:T(2,128)S(1)}, s32[128,2]{0,1:T(2,128)}, u32[]{:S(2)}) copy-start(s32[128,2]{0,1:T(2,128)} %param.14) | copy-start | bytes 3076
  0.6 24.7 %copy-start = (bf16[128,1024]{1,0:T(8,128)(2,1)S(1)}, bf16[128,1024]{1,0:T(8,128)(2,1)}, u32[]{:S(2)}) copy-start(bf16[128,1024]{1,0:T(8,128)(2,1)} %tok_ref.3) | copy-start | bytes 786436
  0.7 18.8 %copy-start.4 = (bf16[1024,32]{0,1:T(8,128)(2,1)S(1)}, bf16[1024,32]{0,1:T(8,128)(2,1)}, u32[]{:S(2)}) copy-start(bf16[1024,32]{0,1:T(8,128)(2,1)} %param.13) | copy-start | bytes 196612
  0.7 24.7 %copy-start.2 = (bf16[1024,64]{0,1:T(8,128)(2,1)S(1)}, bf16[1024,64]{0,1:T(8,128)(2,1)}, u32[]{:S(2)}) copy-start(bf16[1024,64]{0,1:T(8,128)(2,1)} %param.9) | copy-start | bytes 393220
  3.1 46.6 %all-to-all-start = ((bf16[128,8,512]{2,1,0:T(8,128)(2,1)}), bf16[128,8,512]{2,1,0:T(8,128)(2,1)S(1)}, u32[]{:S(2)}, u32[]{:S(2)}) async-start(bf16[128,8,512]{2,1,0:T(8,128)(2,1)} %bitcast.29), calls=%async_computation | async-start | bytes 2097152 | tf_op jit(solution)/shard_map/all_to_all | solution.py:286
  19.5 6.2 %collective-permute-start.3 = (bf16[32,512]{1,0:T(8,128)(2,1)S(1)}, bf16[32,512]{1,0:T(8,128)(2,1)S(1)}, u32[]{:S(2)}, u32[]{:S(2)}) collective-permute-start(bf16[32,512]{1,0:T(8,128)(2,1)S(1)} %broadcast_select_fusion.2), channel_id=1, source_target_pairs={{0,1},{1,0},{2,3},{3,2},{4,5},{5,4},{6,7},{7,6},{8,9},{9,8},{10,11... | collective-permute-start | bytes 98312 | tf_op jit(solution)/shard_map/ppermute | solution.py:251
  20.5 7.9 %collective-permute-start = (bf16[32,1024]{1,0:T(8,128)(2,1)S(1)}, bf16[32,1024]{1,0:T(8,128)(2,1)S(1)}, u32[]{:S(2)}, u32[]{:S(2)}) collective-permute-start(bf16[32,1024]{1,0:T(8,128)(2,1)S(1)} %bitcast.31), channel_id=1, source_target_pairs={{0,64},{64,128},{128,192},{192,0},{1,65},{65,129},{129,193},{193,1... | collective-permute-start | bytes 196616 | tf_op jit(solution)/shard_map/ppermute | solution.py:245
  21.5 8.8 %collective-permute-start.1 = (bf16[32,1024]{1,0:T(8,128)(2,1)S(1)}, bf16[32,1024]{1,0:T(8,128)(2,1)S(1)}, u32[]{:S(2)}, u32[]{:S(2)}) collective-permute-start(bf16[32,1024]{1,0:T(8,128)(2,1)S(1)} %bitcast.32), channel_id=1, source_target_pairs={{0,128},{64,192},{128,0},{192,64},{1,129},{65,193},{129,1},{193,65... | collective-permute-start | bytes 196616 | tf_op jit(solution)/shard_map/ppermute | solution.py:245
  24.3 5.9 %collective-permute-start.2 = (bf16[32,1024]{1,0:T(8,128)(2,1)S(1)}, bf16[32,1024]{1,0:T(8,128)(2,1)S(1)}, u32[]{:S(2)}, u32[]{:S(2)}) collective-permute-start(bf16[32,1024]{1,0:T(8,128)(2,1)S(1)} %bitcast.33), channel_id=1, source_target_pairs={{0,192},{64,0},{128,64},{192,128},{1,193},{65,1},{129,65},{193,129... | collective-permute-start | bytes 196616 | tf_op jit(solution)/shard_map/ppermute | solution.py:245
  25.7 17.2 %collective-permute-start.4 = (bf16[64,512]{1,0:T(8,128)(2,1)S(1)}, bf16[64,512]{1,0:T(8,128)(2,1)S(1)}, u32[]{:S(2)}, u32[]{:S(2)}) collective-permute-start(bf16[64,512]{1,0:T(8,128)(2,1)S(1)} %pad_maximum_fusion.2.refs_6_.refs_0_), channel_id=1, source_target_pairs={{0,2},{2,4},{4,6},{6,8},{8,10},{10,12},{12,14},{14,0},{1,3},{3,5},... | collective-permute-start | bytes 196616 | tf_op jit(solution)/shard_map/ppermute | solution.py:245
  27.0 16.0 %collective-permute-start.5 = (bf16[64,512]{1,0:T(8,128)(2,1)S(1)}, bf16[64,512]{1,0:T(8,128)(2,1)S(1)}, u32[]{:S(2)}, u32[]{:S(2)}) collective-permute-start(bf16[64,512]{1,0:T(8,128)(2,1)S(1)} %pad_maximum_fusion.2.refs_6_.refs_0_), channel_id=1, source_target_pairs={{0,14},{2,0},{4,2},{6,4},{8,6},{10,8},{12,10},{14,12},{1,15},{3,1}... | collective-permute-start | bytes 196616 | tf_op jit(solution)/shard_map/ppermute | solution.py:245
  49.7 5.7 %collective-permute-start.6 = (bf16[1024,512]{1,0:T(8,128)(2,1)S(1)}, bf16[1024,512]{1,0:T(8,128)(2,1)S(1)}, u32[]{:S(2)}, u32[]{:S(2)}) collective-permute-start(bf16[1024,512]{1,0:T(8,128)(2,1)S(1)} %order.1.own_ref), channel_id=1, source_target_pairs={{0,1},{1,0},{2,3},{3,2},{4,5},{5,4},{6,7},{7,6},{8,9},{9,8},{10,11... | collective-permute-start | bytes 3145736 | tf_op jit(solution)/shard_map/ppermute | solution.py:299
  55.3 8.3 %copy-start.1 = (bf16[1,1024,1024]{2,1,0:T(8,128)(2,1)S(1)}, bf16[1,1024,1024]{2,1,0:T(8,128)(2,1)}, u32[]{:S(2)}) copy-start(bf16[1,1024,1024]{2,1,0:T(8,128)(2,1)} %param.12) | copy-start | bytes 6291460
  63.1 2.8 %collective-permute-start.7 = (bf16[1024,512]{1,0:T(8,128)(2,1)S(1)}, bf16[1024,512]{1,0:T(8,128)(2,1)S(1)}, u32[]{:S(2)}, u32[]{:S(2)}) collective-permute-start(bf16[1024,512]{1,0:T(8,128)(2,1)S(1)} %get-tuple-element.11), channel_id=1, source_target_pairs={{0,1},{1,0},{2,3},{3,2},{4,5},{5,4},{6,7},{7,6},{8,9},{9,8},{10,11... | collective-permute-start | bytes 3145736 | tf_op jit(solution)/shard_map/ppermute | solution.py:325
  67.0 13.5 %copy-start.5 = (s32[8]{0:T(128)S(1)}, s32[8]{0:T(128)}, u32[]{:S(2)}) copy-start(s32[8]{0:T(128)} %param.15) | copy-start | bytes 100
  67.0 37.8 %all-to-all-start.1 = ((bf16[128,8,512]{2,1,0:T(8,128)(2,1)}), bf16[128,8,512]{2,1,0:T(8,128)(2,1)S(1)}, u32[]{:S(2)}, u32[]{:S(2)}) async-start(bf16[128,8,512]{2,1,0:T(8,128)(2,1)} %bitcast.10), calls=%async_computation.1 | async-start | bytes 2097152 | tf_op jit(solution)/shard_map/all_to_all | solution.py:343
  73.4 26.8 %collective-permute-start.10 = (bf16[128,1024]{1,0:T(8,128)(2,1)S(1)}, bf16[128,1024]{1,0:T(8,128)(2,1)S(1)}, u32[]{:S(2)}, u32[]{:S(2)}) collective-permute-start(bf16[128,1024]{1,0:T(8,128)(2,1)S(1)} %pad_maximum_fusion.refs_3_.plane0), channel_id=1, source_target_pairs={{0,48},{16,0},{32,16},{48,32},{1,49},{17,1},{33,17},{49,33},{2,50}... | collective-permute-start | bytes 786440 | tf_op jit(solution)/shard_map/ppermute | solution.py:245
  75.3 24.9 %collective-permute-start.8 = (bf16[128,1024]{1,0:T(8,128)(2,1)S(1)}, bf16[128,1024]{1,0:T(8,128)(2,1)S(1)}, u32[]{:S(2)}, u32[]{:S(2)}) collective-permute-start(bf16[128,1024]{1,0:T(8,128)(2,1)S(1)} %pad_maximum_fusion.refs_3_.plane0), channel_id=1, source_target_pairs={{0,16},{16,32},{32,48},{48,0},{1,17},{17,33},{33,49},{49,1},{2,18}... | collective-permute-start | bytes 786440 | tf_op jit(solution)/shard_map/ppermute | solution.py:245
  75.3 24.9 %collective-permute-start.9 = (bf16[128,1024]{1,0:T(8,128)(2,1)S(1)}, bf16[128,1024]{1,0:T(8,128)(2,1)S(1)}, u32[]{:S(2)}, u32[]{:S(2)}) collective-permute-start(bf16[128,1024]{1,0:T(8,128)(2,1)S(1)} %pad_maximum_fusion.refs_3_.plane0), channel_id=1, source_target_pairs={{0,32},{16,48},{32,0},{48,16},{1,33},{17,49},{33,1},{49,17},{2,34}... | collective-permute-start | bytes 786440 | tf_op jit(solution)/shard_map/ppermute | solution.py:245
  77.0 23.2 %collective-permute-start.11 = (bf16[64,512]{1,0:T(8,128)(2,1)S(1)}, bf16[64,512]{1,0:T(8,128)(2,1)S(1)}, u32[]{:S(2)}, u32[]{:S(2)}) collective-permute-start(bf16[64,512]{1,0:T(8,128)(2,1)S(1)} %pad_maximum_fusion.2.refs_6_.refs_0_), channel_id=1, source_target_pairs={{0,4},{2,6},{4,8},{6,10},{8,12},{10,14},{12,0},{14,2},{1,5},{3,7},... | collective-permute-start | bytes 196616 | tf_op jit(solution)/shard_map/ppermute | solution.py:245
  79.1 21.1 %collective-permute-start.12 = (bf16[64,512]{1,0:T(8,128)(2,1)S(1)}, bf16[64,512]{1,0:T(8,128)(2,1)S(1)}, u32[]{:S(2)}, u32[]{:S(2)}) collective-permute-start(bf16[64,512]{1,0:T(8,128)(2,1)S(1)} %pad_maximum_fusion.2.refs_6_.refs_0_), channel_id=1, source_target_pairs={{0,12},{2,14},{4,0},{6,2},{8,4},{10,6},{12,8},{14,10},{1,13},{3,15... | collective-permute-start | bytes 196616 | tf_op jit(solution)/shard_map/ppermute | solution.py:245
  117.5 20.0 %all-to-all-start.3 = ((bf16[16,72,512]{2,1,0:T(8,128)(2,1)}), bf16[16,72,512]{2,1,0:T(8,128)(2,1)S(1)}, u32[]{:S(2)}, u32[]{:S(2)}) async-start(bf16[16,72,512]{2,1,0:T(8,128)(2,1)} %broadcast_in_dim.2), calls=%async_computation.3 | async-start | bytes 2359296 | tf_op jit(solution)/shard_map/all_to_all | solution.py:367
  121.7 16.6 %collective-permute-start.14 = (bf16[64,512]{1,0:T(8,128)(2,1)S(1)}, bf16[64,512]{1,0:T(8,128)(2,1)S(1)}, u32[]{:S(2)}, u32[]{:S(2)}) collective-permute-start(bf16[64,512]{1,0:T(8,128)(2,1)S(1)} %pad_maximum_fusion.2.refs_6_.refs_0_), channel_id=1, source_target_pairs={{0,6},{2,8},{4,10},{6,12},{8,14},{10,0},{12,2},{14,4},{1,7},{3,9},... | collective-permute-start | bytes 196616 | tf_op jit(solution)/shard_map/ppermute | solution.py:245
  121.8 16.5 %collective-permute-start.15 = (bf16[64,512]{1,0:T(8,128)(2,1)S(1)}, bf16[64,512]{1,0:T(8,128)(2,1)S(1)}, u32[]{:S(2)}, u32[]{:S(2)}) collective-permute-start(bf16[64,512]{1,0:T(8,128)(2,1)S(1)} %pad_maximum_fusion.2.refs_6_.refs_0_), channel_id=1, source_target_pairs={{0,8},{2,10},{4,12},{6,14},{8,0},{10,2},{12,4},{14,6},{1,9},{3,11}... | collective-permute-start | bytes 196616 | tf_op jit(solution)/shard_map/ppermute | solution.py:245
  124.4 14.0 %collective-permute-start.16 = (bf16[64,512]{1,0:T(8,128)(2,1)S(1)}, bf16[64,512]{1,0:T(8,128)(2,1)S(1)}, u32[]{:S(2)}, u32[]{:S(2)}) collective-permute-start(bf16[64,512]{1,0:T(8,128)(2,1)S(1)} %pad_maximum_fusion.2.refs_6_.refs_0_), channel_id=1, source_target_pairs={{0,10},{2,12},{4,14},{6,0},{8,2},{10,4},{12,6},{14,8},{1,11},{3,13... | collective-permute-start | bytes 196616 | tf_op jit(solution)/shard_map/ppermute | solution.py:245
  138.7 5.8 %collective-permute-start.17 = (f32[512,256]{1,0:T(8,128)S(1)}, f32[512,256]{1,0:T(8,128)S(1)}, u32[]{:S(2)}, u32[]{:S(2)}) collective-permute-start(f32[512,256]{1,0:T(8,128)S(1)} %line.1.cols_ref), channel_id=1, source_target_pairs={{0,1},{1,0},{2,3},{3,2},{4,5},{5,4},{6,7},{7,6},{8,9},{9,8},{10,11... | collective-permute-start | bytes 1572872 | tf_op jit(solution)/shard_map/ppermute | solution.py:390
  142.6 1.9 %collective-permute-start.13 = (bf16[256,512]{1,0:T(8,128)(2,1)S(1)}, bf16[256,512]{1,0:T(8,128)(2,1)S(1)}, u32[]{:S(2)}, u32[]{:S(2)}) collective-permute-start(bf16[256,512]{1,0:T(8,128)(2,1)S(1)} %clips.1.clips_ref.own_ref), channel_id=1, source_target_pairs={{0,1},{1,0},{2,3},{3,2},{4,5},{5,4},{6,7},{7,6},{8,9},{9,8},{10,11... | collective-permute-start | bytes 786440 | tf_op jit(solution)/shard_map/ppermute | solution.py:378

commit v5 on v4

--- a/solution.py
+++ b/solution.py
@@ -87,33 +87,29 @@
     pass
 
 
+def load_kernel(gate_hbm, up_hbm, after_hbm, gate_ref, up_ref, sems):
+    copies = [
+        pltpu.make_async_copy(source, target, sems.at[k])
+        for k, (source, target) in enumerate(((gate_hbm, gate_ref), (up_hbm, up_ref)))
+    ]
+    for copy in copies:
+        copy.start()
+    for copy in copies:
+        copy.wait()
+
+
 def ffn_kernel(
-    step, d_ref, own_ref, other_ref, gate_hbm, up_hbm, down_hbm, hid_ref, out_ref, x_ref, gate_ref, up_ref, down_ref, sems, down_sem
+    step, block, d_ref, own_ref, other_ref, gate_ref, up_ref, down_hbm, hid_ref, out_ref, x_ref, down_ref, sem
 ):
     d = d_ref[0]
     rows, part = own_ref.shape
-    blocks = sems.shape[1]
-    block = gate_ref.shape[1] // blocks
-    spans = [slice(k * block, (k + 1) * block) for k in range(blocks)]
-    loads = [
-        [
-            pltpu.make_async_copy(source.at[:, span], target.at[:, span], sems.at[w, k])
-            for w, (source, target) in enumerate(((gate_hbm, gate_ref), (up_hbm, up_ref)))
-        ]
-        for k, span in enumerate(spans)
-    ]
-    load_down = pltpu.make_async_copy(down_hbm, down_ref, down_sem)
-    for pair in loads:
-        for load in pair:
-            load.start()
+    load_down = pltpu.make_async_copy(down_hbm, down_ref, sem)
     load_down.start()
     x_ref[:, half(d, part)] = own_ref[...]
     x_ref[:, half(1 - d, part)] = other_ref[...]
-
     steps = [slice(m * step, (m + 1) * step) for m in range(rows // step)]
-    for pair, span in zip(loads, spans):
-        for load in pair:
-            load.wait()
+    for j in range(gate_ref.shape[1] // block):
+        span = slice(j * block, (j + 1) * block)
         for at in steps:
             gate = dot(x_ref[at, :], gate_ref[:, span])
             upper = dot(x_ref[at, :], up_ref[:, span])
@@ -299,28 +295,35 @@
     other = lax.ppermute(received, "dp", swap)
 
     w_down = down_weight.reshape(hidden, width)
+    w_gate, w_up = pl.pallas_call(
+        load_kernel,
+        out_shape=[jax.ShapeDtypeStruct((width, hidden), BF16)] * 2,
+        in_specs=[hbm] * 3,
+        out_specs=(vmem, vmem),
+        scratch_shapes=[pltpu.SemaphoreType.DMA((2,))],
+        compiler_params=pltpu.CompilerParams(vmem_limit_bytes=48 * 2**20),
+        cost_estimate=pl.CostEstimate(flops=0, bytes_accessed=4 * width * hidden * 2, transcendentals=0),
+        name="load",
+    )(gate_weight.reshape(width, hidden), up_weight.reshape(width, hidden), received)
     inner, theirs = pl.pallas_call(
-        functools.partial(ffn_kernel, 512),
+        functools.partial(ffn_kernel, 512, 256),
         out_shape=(
             jax.ShapeDtypeStruct((rows, hidden), BF16),
             jax.ShapeDtypeStruct((rows, part), BF16),
         ),
-        in_specs=[SCALAR, vmem, vmem, hbm, hbm, hbm],
+        in_specs=[SCALAR] + [vmem] * 4 + [hbm],
         out_specs=(vmem, vmem),
         scratch_shapes=[
             pltpu.VMEM((rows, width), BF16),
-            pltpu.VMEM((width, hidden), BF16),
-            pltpu.VMEM((width, hidden), BF16),
             pltpu.VMEM((hidden, width), BF16),
-            pltpu.SemaphoreType.DMA((2, 4)),
             pltpu.SemaphoreType.DMA(()),
         ],
-        compiler_params=pltpu.CompilerParams(vmem_limit_bytes=48 * 2**20),
+        compiler_params=pltpu.CompilerParams(vmem_limit_bytes=40 * 2**20),
         cost_estimate=pl.CostEstimate(
             flops=2 * rows * hidden * (2 * width + part), bytes_accessed=0, transcendentals=0
         ),
         name="ffn",
-    )(d, received, other, gate_weight.reshape(width, hidden), up_weight.reshape(width, hidden), w_down)
+    )(d, received, other, w_gate, w_up, w_down)
 
     brought = lax.ppermute(theirs, "dp", swap)
     ours = pl.pallas_call(

time: 161 us -> 160 us (level)
  waiting for transfers between devices: 61.2 us -> 59.4 us
    ppermute x1, waiting for transfers between devices: 2.29 us -> 0.01 us  [per_device(): other = lax.ppermute(received, 'dp', swap)]
    pallas_call x1 -> x2, Pallas kernels: 7.78 us -> 8.45 us  [the longest x1 6.07 us: per_device(): pl.pallas_call(functools.partial(ffn_kernel, 512, 256), out_shape=(jax.Sh...]
  transfers between devices with their start and end apart: 21 -> 21, of which waited for: 9 -> 8; matrix products, arithmetic and copies ran while one was open for 0% -> 0% of each run, Pallas kernels for 1% -> 3%
where the time goes in v5:
time: 160 us; the launch traced here: 159 us
  waiting for transfers between devices  59.4 us (37%)
  starting transfers between devices  55.1 us (34%)
  blocking collectives  23.8 us (15%)
  Pallas kernels  18.1 us (11%)
  local copies, waits for them, and re-layouts  2.02 us (1%)
    ppermute x13, waiting for transfers between devices, ring(): lax.ppermute(block, axis, [(k, (k + step) % size) for k in range(size)])  34.9 us
    ppermute x13, starting transfers between devices, ring(): lax.ppermute(block, axis, [(k, (k + step) % size) for k in range(size)])  19.8 us
    all_to_all x1, starting transfers between devices, per_device(): lax.all_to_all(outgoing.reshape(n_expert, capacity, part), EXP, split_axi...  16.3 us
    all_to_all x1, blocking collectives, per_device(): lax.all_to_all(blocks, PLANE, split_axis=0, concat_axis=0, tiled=True)  13.4 us
    all_to_all x1, waiting for transfers between devices, per_device(): lax.all_to_all(copies, PLANE, split_axis=0, concat_axis=0, tiled=True)  10.7 us
    all_to_all x1, blocking collectives, per_device(): got = lax.all_to_all(payload, 'z', split_axis=0, concat_axis=0, tiled=True)  10.4 us
    all_to_all x1, waiting for transfers between devices, per_device(): lax.all_to_all(outgoing.reshape(n_expert, capacity, part), EXP, split_axi...  6.72 us
    all_to_all x1, starting transfers between devices, per_device(): lax.all_to_all(summed.reshape(n_expert, capacity, part), EXP, split_axis=...  6.32 us
  transfers between devices with their start and end apart: 21, of which 8 were waited for; matrix products, arithmetic and copies ran while one was open for 0% of the time, Pallas kernels for 3%

profile of v5, /device:TPU:1, one launch (start us, length us, event | category | flops | bytes accessed | tf_op | source)
XLA Modules:
  0.0 159.4 jit_solution(5232302607229623632)
XLA Ops:
  0.7 2.4 %prep.1 = bf16[1024,512]{1,0:T(8,128)(2,1)} custom-call(s32[1]{0:T(128)} %bitcast.d_ref, bf16[128,1024]{1,0:T(8,128)(2,1)} %tok_ref.3, s32[2,128]{1,0:T(2,128)} %bitcast.27), custom_call_target="tpu_custom_call" | custom-call | tf_op jit(solution)/shard_map/prep/pallas_call | solution.py:257
  3.1 16.3 %all-to-all-start = ((bf16[128,8,512]{2,1,0:T(8,128)(2,1)}), bf16[128,8,512]{2,1,0:T(8,128)(2,1)S(1)}, u32[]{:S(2)}, u32[]{:S(2)}) async-start(bf16[128,8,512]{2,1,0:T(8,128)(2,1)} %bitcast.29), calls=%async_computation | async-start | bytes 2097152 | tf_op jit(solution)/shard_map/all_to_all | solution.py:282
  21.5 2.8 %collective-permute-start.1 = (bf16[32,1024]{1,0:T(8,128)(2,1)S(1)}, bf16[32,1024]{1,0:T(8,128)(2,1)S(1)}, u32[]{:S(2)}, u32[]{:S(2)}) collective-permute-start(bf16[32,1024]{1,0:T(8,128)(2,1)S(1)} %bitcast.34), channel_id=1, source_target_pairs={{0,128},{64,192},{128,0},{192,64},{1,129},{65,193},{129,1},{193,65... | collective-permute-start | bytes 196616 | tf_op jit(solution)/shard_map/ppermute | solution.py:241
  25.7 1.3 collective-permute-start.4
  27.0 1.5 collective-permute-start.5
  28.5 1.8 %collective-permute-done.1 = bf16[32,1024]{1,0:T(8,128)(2,1)S(1)} collective-permute-done((bf16[32,1024]{1,0:T(8,128)(2,1)S(1)}, bf16[32,1024]{1,0:T(8,128)(2,1)S(1)}, u32[]{:S(2)}, u32[]{:S(2)}) %collective-permute-start.1) | collective-permute-done | bytes 65568 | tf_op jit(solution)/shard_map/ppermute | solution.py:241
  30.3 12.7 %collective-permute-done.4.refs_4_.refs_1_ = bf16[64,512]{1,0:T(8,128)(2,1)S(1)} collective-permute-done((bf16[64,512]{1,0:T(8,128)(2,1)S(1)}, bf16[64,512]{1,0:T(8,128)(2,1)S(1)}, u32[]{:S(2)}, u32[]{:S(2)}) %collective-permute-start.4) | collective-permute-done | bytes 65568 | tf_op jit(solution)/shard_map/ppermute | solution.py:241
  43.0 6.7 %all-to-all-done = bf16[128,8,512]{2,1,0:T(8,128)(2,1)S(1)} async-done(((bf16[128,8,512]{2,1,0:T(8,128)(2,1)}), bf16[128,8,512]{2,1,0:T(8,128)(2,1)S(1)}, u32[]{:S(2)}, u32[]{:S(2)}) %all-to-all-start) | async-done | bytes 1048608 | tf_op jit(solution)/shard_map/all_to_all | solution.py:282
  49.7 3.4 %collective-permute-start.6 = (bf16[1024,512]{1,0:T(8,128)(2,1)S(1)}, bf16[1024,512]{1,0:T(8,128)(2,1)S(1)}, u32[]{:S(2)}, u32[]{:S(2)}) collective-permute-start(bf16[1024,512]{1,0:T(8,128)(2,1)S(1)} %order.1.after_hbm.own_ref), channel_id=1, source_target_pairs={{0,1},{1,0},{2,3},{3,2},{4,5},{5,4},{6,7},{7,6},{8,9},{9,8},{10,11... | collective-permute-start | bytes 3145736 | tf_op jit(solution)/shard_map/ppermute | solution.py:295
  53.1 2.4 %load.1 = (bf16[1024,1024]{1,0:T(8,128)(2,1)S(1)}, bf16[1024,1024]{1,0:T(8,128)(2,1)S(1)}) custom-call(bf16[1024,1024]{1,0:T(8,128)(2,1)} %bitcast.30, bf16[1024,1024]{1,0:T(8,128)(2,1)} %bitcast.31, bf16[1024,512]{1,0:T(8,128)(2,1)S(1)} %order.1.after_hbm.own_ref), custom_call_target="tpu_custom_call" | custom-call | bytes 8388608 | tf_op jit(solution)/shard_map/load/pallas_call | solution.py:298
  55.9 6.1 %ffn.1 = (bf16[1024,1024]{1,0:T(8,128)(2,1)S(1)}, bf16[1024,512]{1,0:T(8,128)(2,1)S(1)}) custom-call(s32[1]{0:T(128)} %bitcast.d_ref, bf16[1024,512]{1,0:T(8,128)(2,1)S(1)} %order.1.after_hbm.own_ref, bf16[1024,512]{1,0:T(8,128)(2,1)S(1)} %collective-permute-done.6.other_ref, bf16[1024,1024]{1,0:T(8,128)(2,1)S(1)} %get-tuple-element.12.gate_ref, ...), custom_call_target="tpu_custom_call" | custom-call | flops 5368709120 | tf_op jit(solution)/shard_map/ffn/pallas_call | solution.py:308
  62.3 1.3 ours.1.own_ref
  63.5 1.4 collective-permute-done.7.brought_ref
  64.9 1.1 total.1
  66.1 6.3 %all-to-all-start.1 = ((bf16[128,8,512]{2,1,0:T(8,128)(2,1)}), bf16[128,8,512]{2,1,0:T(8,128)(2,1)S(1)}, u32[]{:S(2)}, u32[]{:S(2)}) async-start(bf16[128,8,512]{2,1,0:T(8,128)(2,1)} %bitcast.10), calls=%async_computation.1 | async-start | bytes 2097152 | tf_op jit(solution)/shard_map/all_to_all | solution.py:346
  72.4 1.9 %collective-permute-start.10 = (bf16[128,1024]{1,0:T(8,128)(2,1)S(1)}, bf16[128,1024]{1,0:T(8,128)(2,1)S(1)}, u32[]{:S(2)}, u32[]{:S(2)}) collective-permute-start(bf16[128,1024]{1,0:T(8,128)(2,1)S(1)} %pad_maximum_fusion.refs_3_.plane0), channel_id=1, source_target_pairs={{0,48},{16,0},{32,16},{48,32},{1,49},{17,1},{33,17},{49,33},{2,50}... | collective-permute-start | bytes 786440 | tf_op jit(solution)/shard_map/ppermute | solution.py:241
  74.3 1.7 %collective-permute-start.9 = (bf16[128,1024]{1,0:T(8,128)(2,1)S(1)}, bf16[128,1024]{1,0:T(8,128)(2,1)S(1)}, u32[]{:S(2)}, u32[]{:S(2)}) collective-permute-start(bf16[128,1024]{1,0:T(8,128)(2,1)S(1)} %pad_maximum_fusion.refs_3_.plane0), channel_id=1, source_target_pairs={{0,32},{16,48},{32,0},{48,16},{1,33},{17,49},{33,1},{49,17},{2,34}... | collective-permute-start | bytes 786440 | tf_op jit(solution)/shard_map/ppermute | solution.py:241
  76.0 2.1 %collective-permute-start.11 = (bf16[64,512]{1,0:T(8,128)(2,1)S(1)}, bf16[64,512]{1,0:T(8,128)(2,1)S(1)}, u32[]{:S(2)}, u32[]{:S(2)}) collective-permute-start(bf16[64,512]{1,0:T(8,128)(2,1)S(1)} %pad_maximum_fusion.2.refs_6_.refs_0_), channel_id=1, source_target_pairs={{0,4},{2,6},{4,8},{6,10},{8,12},{10,14},{12,0},{14,2},{1,5},{3,7},... | collective-permute-start | bytes 196616 | tf_op jit(solution)/shard_map/ppermute | solution.py:241
  78.1 1.5 collective-permute-start.12
  79.7 20.4 %collective-permute-done.11.refs_3_.refs_2_ = bf16[64,512]{1,0:T(8,128)(2,1)S(1)} collective-permute-done((bf16[64,512]{1,0:T(8,128)(2,1)S(1)}, bf16[64,512]{1,0:T(8,128)(2,1)S(1)}, u32[]{:S(2)}, u32[]{:S(2)}) %collective-permute-start.11) | collective-permute-done | bytes 65568 | tf_op jit(solution)/shard_map/ppermute | solution.py:241
  100.1 3.9 %all-to-all-done.1 = bf16[128,8,512]{2,1,0:T(8,128)(2,1)S(1)} async-done(((bf16[128,8,512]{2,1,0:T(8,128)(2,1)}), bf16[128,8,512]{2,1,0:T(8,128)(2,1)S(1)}, u32[]{:S(2)}, u32[]{:S(2)}) %all-to-all-start.1) | async-done | bytes 1048608 | tf_op jit(solution)/shard_map/all_to_all | solution.py:346
  104.0 1.2 combine.1
  105.2 10.4 %all_to_all.25 = bf16[8,16,512]{2,1,0:T(8,128)(2,1)S(1)} all-to-all(bf16[8,16,512]{2,1,0:T(8,128)(2,1)S(1)} %get-tuple-element.17), channel_id=1, replica_groups=mesh['x'=4,'y'=4,'z'=8,'dp'=2] {'z'}, dimensions={0} | all-to-all | bytes 262144 | tf_op jit(solution)/shard_map/all_to_all | solution.py:362
  115.6 1.1 broadcast_in_dim.2
  116.7 3.9 %all-to-all-start.3 = ((bf16[16,72,512]{2,1,0:T(8,128)(2,1)}), bf16[16,72,512]{2,1,0:T(8,128)(2,1)S(1)}, u32[]{:S(2)}, u32[]{:S(2)}) async-start(bf16[16,72,512]{2,1,0:T(8,128)(2,1)} %broadcast_in_dim.2), calls=%async_computation.3 | async-start | bytes 2359296 | tf_op jit(solution)/shard_map/all_to_all | solution.py:370
  121.1 2.5 %collective-permute-start.15 = (bf16[64,512]{1,0:T(8,128)(2,1)S(1)}, bf16[64,512]{1,0:T(8,128)(2,1)S(1)}, u32[]{:S(2)}, u32[]{:S(2)}) collective-permute-start(bf16[64,512]{1,0:T(8,128)(2,1)S(1)} %pad_maximum_fusion.2.refs_6_.refs_0_), channel_id=1, source_target_pairs={{0,8},{2,10},{4,12},{6,14},{8,0},{10,2},{12,4},{14,6},{1,9},{3,11}... | collective-permute-start | bytes 196616 | tf_op jit(solution)/shard_map/ppermute | solution.py:241
  123.6 2.2 %collective-permute-start.16 = (bf16[64,512]{1,0:T(8,128)(2,1)S(1)}, bf16[64,512]{1,0:T(8,128)(2,1)S(1)}, u32[]{:S(2)}, u32[]{:S(2)}) collective-permute-start(bf16[64,512]{1,0:T(8,128)(2,1)S(1)} %pad_maximum_fusion.2.refs_6_.refs_0_), channel_id=1, source_target_pairs={{0,10},{2,12},{4,14},{6,0},{8,2},{10,4},{12,6},{14,8},{1,11},{3,13... | collective-permute-start | bytes 196616 | tf_op jit(solution)/shard_map/ppermute | solution.py:241
  125.8 10.7 %all-to-all-done.3.frames_ref = bf16[16,72,512]{2,1,0:T(8,128)(2,1)S(1)} async-done(((bf16[16,72,512]{2,1,0:T(8,128)(2,1)}), bf16[16,72,512]{2,1,0:T(8,128)(2,1)S(1)}, u32[]{:S(2)}, u32[]{:S(2)}) %all-to-all-start.3) | async-done | bytes 1179680 | tf_op jit(solution)/shard_map/all_to_all | solution.py:370
  137.7 3.8 %collective-permute-start.17 = (f32[512,256]{1,0:T(8,128)S(1)}, f32[512,256]{1,0:T(8,128)S(1)}, u32[]{:S(2)}, u32[]{:S(2)}) collective-permute-start(f32[512,256]{1,0:T(8,128)S(1)} %line.1.cols_ref), channel_id=1, source_target_pairs={{0,1},{1,0},{2,3},{3,2},{4,5},{5,4},{6,7},{7,6},{8,9},{9,8},{10,11... | collective-permute-start | bytes 1572872 | tf_op jit(solution)/shard_map/ppermute | solution.py:393
  141.6 1.8 %collective-permute-done.13.other_ref = bf16[256,512]{1,0:T(8,128)(2,1)S(1)} collective-permute-done((bf16[256,512]{1,0:T(8,128)(2,1)S(1)}, bf16[256,512]{1,0:T(8,128)(2,1)S(1)}, u32[]{:S(2)}, u32[]{:S(2)}) %collective-permute-start.13) | collective-permute-done | bytes 262176 | tf_op jit(solution)/shard_map/ppermute | solution.py:381
  143.4 1.5 covariance.1
  144.9 13.4 %all_to_all.26.in_ref = bf16[16,32,512]{2,1,0:T(8,128)(2,1)S(1)} all-to-all(bf16[16,32,512]{2,1,0:T(8,128)(2,1)S(1)} %covariance.1), channel_id=1, replica_groups=mesh['x'=4,'y'=4,'z'=8,'dp'=2] {'x','y'}, dimensions={0} | all-to-all | bytes 1048576 | tf_op jit(solution)/shard_map/all_to_all | solution.py:403
  (48 shorter events, 6.9 us)
Async XLA Ops:
  0.6 24.7 %copy-start.3 = (s32[128,2]{0,1:T(2,128)S(1)}, s32[128,2]{0,1:T(2,128)}, u32[]{:S(2)}) copy-start(s32[128,2]{0,1:T(2,128)} %param.14) | copy-start | bytes 3076
  0.6 24.7 %copy-start = (bf16[128,1024]{1,0:T(8,128)(2,1)S(1)}, bf16[128,1024]{1,0:T(8,128)(2,1)}, u32[]{:S(2)}) copy-start(bf16[128,1024]{1,0:T(8,128)(2,1)} %tok_ref.3) | copy-start | bytes 786436
  0.7 18.8 %copy-start.4 = (bf16[1024,32]{0,1:T(8,128)(2,1)S(1)}, bf16[1024,32]{0,1:T(8,128)(2,1)}, u32[]{:S(2)}) copy-start(bf16[1024,32]{0,1:T(8,128)(2,1)} %param.13) | copy-start | bytes 196612
  0.7 24.7 %copy-start.2 = (bf16[1024,64]{0,1:T(8,128)(2,1)S(1)}, bf16[1024,64]{0,1:T(8,128)(2,1)}, u32[]{:S(2)}) copy-start(bf16[1024,64]{0,1:T(8,128)(2,1)} %param.9) | copy-start | bytes 393220
  3.1 46.6 %all-to-all-start = ((bf16[128,8,512]{2,1,0:T(8,128)(2,1)}), bf16[128,8,512]{2,1,0:T(8,128)(2,1)S(1)}, u32[]{:S(2)}, u32[]{:S(2)}) async-start(bf16[128,8,512]{2,1,0:T(8,128)(2,1)} %bitcast.29), calls=%async_computation | async-start | bytes 2097152 | tf_op jit(solution)/shard_map/all_to_all | solution.py:282
  19.5 6.2 %collective-permute-start.3 = (bf16[32,512]{1,0:T(8,128)(2,1)S(1)}, bf16[32,512]{1,0:T(8,128)(2,1)S(1)}, u32[]{:S(2)}, u32[]{:S(2)}) collective-permute-start(bf16[32,512]{1,0:T(8,128)(2,1)S(1)} %broadcast_select_fusion.2), channel_id=1, source_target_pairs={{0,1},{1,0},{2,3},{3,2},{4,5},{5,4},{6,7},{7,6},{8,9},{9,8},{10,11... | collective-permute-start | bytes 98312 | tf_op jit(solution)/shard_map/ppermute | solution.py:247
  20.5 7.9 %collective-permute-start = (bf16[32,1024]{1,0:T(8,128)(2,1)S(1)}, bf16[32,1024]{1,0:T(8,128)(2,1)S(1)}, u32[]{:S(2)}, u32[]{:S(2)}) collective-permute-start(bf16[32,1024]{1,0:T(8,128)(2,1)S(1)} %bitcast.33), channel_id=1, source_target_pairs={{0,64},{64,128},{128,192},{192,0},{1,65},{65,129},{129,193},{193,1... | collective-permute-start | bytes 196616 | tf_op jit(solution)/shard_map/ppermute | solution.py:241
  21.5 8.8 %collective-permute-start.1 = (bf16[32,1024]{1,0:T(8,128)(2,1)S(1)}, bf16[32,1024]{1,0:T(8,128)(2,1)S(1)}, u32[]{:S(2)}, u32[]{:S(2)}) collective-permute-start(bf16[32,1024]{1,0:T(8,128)(2,1)S(1)} %bitcast.34), channel_id=1, source_target_pairs={{0,128},{64,192},{128,0},{192,64},{1,129},{65,193},{129,1},{193,65... | collective-permute-start | bytes 196616 | tf_op jit(solution)/shard_map/ppermute | solution.py:241
  24.3 5.9 %collective-permute-start.2 = (bf16[32,1024]{1,0:T(8,128)(2,1)S(1)}, bf16[32,1024]{1,0:T(8,128)(2,1)S(1)}, u32[]{:S(2)}, u32[]{:S(2)}) collective-permute-start(bf16[32,1024]{1,0:T(8,128)(2,1)S(1)} %bitcast.35), channel_id=1, source_target_pairs={{0,192},{64,0},{128,64},{192,128},{1,193},{65,1},{129,65},{193,129... | collective-permute-start | bytes 196616 | tf_op jit(solution)/shard_map/ppermute | solution.py:241
  25.7 17.2 %collective-permute-start.4 = (bf16[64,512]{1,0:T(8,128)(2,1)S(1)}, bf16[64,512]{1,0:T(8,128)(2,1)S(1)}, u32[]{:S(2)}, u32[]{:S(2)}) collective-permute-start(bf16[64,512]{1,0:T(8,128)(2,1)S(1)} %pad_maximum_fusion.2.refs_6_.refs_0_), channel_id=1, source_target_pairs={{0,2},{2,4},{4,6},{6,8},{8,10},{10,12},{12,14},{14,0},{1,3},{3,5},... | collective-permute-start | bytes 196616 | tf_op jit(solution)/shard_map/ppermute | solution.py:241
  27.0 16.0 %collective-permute-start.5 = (bf16[64,512]{1,0:T(8,128)(2,1)S(1)}, bf16[64,512]{1,0:T(8,128)(2,1)S(1)}, u32[]{:S(2)}, u32[]{:S(2)}) collective-permute-start(bf16[64,512]{1,0:T(8,128)(2,1)S(1)} %pad_maximum_fusion.2.refs_6_.refs_0_), channel_id=1, source_target_pairs={{0,14},{2,0},{4,2},{6,4},{8,6},{10,8},{12,10},{14,12},{1,15},{3,1}... | collective-permute-start | bytes 196616 | tf_op jit(solution)/shard_map/ppermute | solution.py:241
  49.7 5.8 %collective-permute-start.6 = (bf16[1024,512]{1,0:T(8,128)(2,1)S(1)}, bf16[1024,512]{1,0:T(8,128)(2,1)S(1)}, u32[]{:S(2)}, u32[]{:S(2)}) collective-permute-start(bf16[1024,512]{1,0:T(8,128)(2,1)S(1)} %order.1.after_hbm.own_ref), channel_id=1, source_target_pairs={{0,1},{1,0},{2,3},{3,2},{4,5},{5,4},{6,7},{7,6},{8,9},{9,8},{10,11... | collective-permute-start | bytes 3145736 | tf_op jit(solution)/shard_map/ppermute | solution.py:295
  53.1 2.9 %copy-start.1 = (bf16[1,1024,1024]{2,1,0:T(8,128)(2,1)S(1)}, bf16[1,1024,1024]{2,1,0:T(8,128)(2,1)}, u32[]{:S(2)}) copy-start(bf16[1,1024,1024]{2,1,0:T(8,128)(2,1)} %param.12) | copy-start | bytes 6291460
  62.0 2.9 %collective-permute-start.7 = (bf16[1024,512]{1,0:T(8,128)(2,1)S(1)}, bf16[1024,512]{1,0:T(8,128)(2,1)S(1)}, u32[]{:S(2)}, u32[]{:S(2)}) collective-permute-start(bf16[1024,512]{1,0:T(8,128)(2,1)S(1)} %get-tuple-element.15), channel_id=1, source_target_pairs={{0,1},{1,0},{2,3},{3,2},{4,5},{5,4},{6,7},{7,6},{8,9},{9,8},{10,11... | collective-permute-start | bytes 3145736 | tf_op jit(solution)/shard_map/ppermute | solution.py:328
  66.1 13.5 %copy-start.5 = (s32[8]{0:T(128)S(1)}, s32[8]{0:T(128)}, u32[]{:S(2)}) copy-start(s32[8]{0:T(128)} %param.15) | copy-start | bytes 100
  66.1 38.0 %all-to-all-start.1 = ((bf16[128,8,512]{2,1,0:T(8,128)(2,1)}), bf16[128,8,512]{2,1,0:T(8,128)(2,1)S(1)}, u32[]{:S(2)}, u32[]{:S(2)}) async-start(bf16[128,8,512]{2,1,0:T(8,128)(2,1)} %bitcast.10), calls=%async_computation.1 | async-start | bytes 2097152 | tf_op jit(solution)/shard_map/all_to_all | solution.py:346
  72.4 27.7 %collective-permute-start.10 = (bf16[128,1024]{1,0:T(8,128)(2,1)S(1)}, bf16[128,1024]{1,0:T(8,128)(2,1)S(1)}, u32[]{:S(2)}, u32[]{:S(2)}) collective-permute-start(bf16[128,1024]{1,0:T(8,128)(2,1)S(1)} %pad_maximum_fusion.refs_3_.plane0), channel_id=1, source_target_pairs={{0,48},{16,0},{32,16},{48,32},{1,49},{17,1},{33,17},{49,33},{2,50}... | collective-permute-start | bytes 786440 | tf_op jit(solution)/shard_map/ppermute | solution.py:241
  74.3 25.8 %collective-permute-start.8 = (bf16[128,1024]{1,0:T(8,128)(2,1)S(1)}, bf16[128,1024]{1,0:T(8,128)(2,1)S(1)}, u32[]{:S(2)}, u32[]{:S(2)}) collective-permute-start(bf16[128,1024]{1,0:T(8,128)(2,1)S(1)} %pad_maximum_fusion.refs_3_.plane0), channel_id=1, source_target_pairs={{0,16},{16,32},{32,48},{48,0},{1,17},{17,33},{33,49},{49,1},{2,18}... | collective-permute-start | bytes 786440 | tf_op jit(solution)/shard_map/ppermute | solution.py:241
  74.3 25.8 %collective-permute-start.9 = (bf16[128,1024]{1,0:T(8,128)(2,1)S(1)}, bf16[128,1024]{1,0:T(8,128)(2,1)S(1)}, u32[]{:S(2)}, u32[]{:S(2)}) collective-permute-start(bf16[128,1024]{1,0:T(8,128)(2,1)S(1)} %pad_maximum_fusion.refs_3_.plane0), channel_id=1, source_target_pairs={{0,32},{16,48},{32,0},{48,16},{1,33},{17,49},{33,1},{49,17},{2,34}... | collective-permute-start | bytes 786440 | tf_op jit(solution)/shard_map/ppermute | solution.py:241
  76.0 24.1 %collective-permute-start.11 = (bf16[64,512]{1,0:T(8,128)(2,1)S(1)}, bf16[64,512]{1,0:T(8,128)(2,1)S(1)}, u32[]{:S(2)}, u32[]{:S(2)}) collective-permute-start(bf16[64,512]{1,0:T(8,128)(2,1)S(1)} %pad_maximum_fusion.2.refs_6_.refs_0_), channel_id=1, source_target_pairs={{0,4},{2,6},{4,8},{6,10},{8,12},{10,14},{12,0},{14,2},{1,5},{3,7},... | collective-permute-start | bytes 196616 | tf_op jit(solution)/shard_map/ppermute | solution.py:241
  78.1 22.0 %collective-permute-start.12 = (bf16[64,512]{1,0:T(8,128)(2,1)S(1)}, bf16[64,512]{1,0:T(8,128)(2,1)S(1)}, u32[]{:S(2)}, u32[]{:S(2)}) collective-permute-start(bf16[64,512]{1,0:T(8,128)(2,1)S(1)} %pad_maximum_fusion.2.refs_6_.refs_0_), channel_id=1, source_target_pairs={{0,12},{2,14},{4,0},{6,2},{8,4},{10,6},{12,8},{14,10},{1,13},{3,15... | collective-permute-start | bytes 196616 | tf_op jit(solution)/shard_map/ppermute | solution.py:241
  116.7 19.8 %all-to-all-start.3 = ((bf16[16,72,512]{2,1,0:T(8,128)(2,1)}), bf16[16,72,512]{2,1,0:T(8,128)(2,1)S(1)}, u32[]{:S(2)}, u32[]{:S(2)}) async-start(bf16[16,72,512]{2,1,0:T(8,128)(2,1)} %broadcast_in_dim.2), calls=%async_computation.3 | async-start | bytes 2359296 | tf_op jit(solution)/shard_map/all_to_all | solution.py:370
  120.7 16.6 %collective-permute-start.14 = (bf16[64,512]{1,0:T(8,128)(2,1)S(1)}, bf16[64,512]{1,0:T(8,128)(2,1)S(1)}, u32[]{:S(2)}, u32[]{:S(2)}) collective-permute-start(bf16[64,512]{1,0:T(8,128)(2,1)S(1)} %pad_maximum_fusion.2.refs_6_.refs_0_), channel_id=1, source_target_pairs={{0,6},{2,8},{4,10},{6,12},{8,14},{10,0},{12,2},{14,4},{1,7},{3,9},... | collective-permute-start | bytes 196616 | tf_op jit(solution)/shard_map/ppermute | solution.py:241
  121.1 16.3 %collective-permute-start.15 = (bf16[64,512]{1,0:T(8,128)(2,1)S(1)}, bf16[64,512]{1,0:T(8,128)(2,1)S(1)}, u32[]{:S(2)}, u32[]{:S(2)}) collective-permute-start(bf16[64,512]{1,0:T(8,128)(2,1)S(1)} %pad_maximum_fusion.2.refs_6_.refs_0_), channel_id=1, source_target_pairs={{0,8},{2,10},{4,12},{6,14},{8,0},{10,2},{12,4},{14,6},{1,9},{3,11}... | collective-permute-start | bytes 196616 | tf_op jit(solution)/shard_map/ppermute | solution.py:241
  123.6 13.7 %collective-permute-start.16 = (bf16[64,512]{1,0:T(8,128)(2,1)S(1)}, bf16[64,512]{1,0:T(8,128)(2,1)S(1)}, u32[]{:S(2)}, u32[]{:S(2)}) collective-permute-start(bf16[64,512]{1,0:T(8,128)(2,1)S(1)} %pad_maximum_fusion.2.refs_6_.refs_0_), channel_id=1, source_target_pairs={{0,10},{2,12},{4,14},{6,0},{8,2},{10,4},{12,6},{14,8},{1,11},{3,13... | collective-permute-start | bytes 196616 | tf_op jit(solution)/shard_map/ppermute | solution.py:241
  137.7 5.7 %collective-permute-start.17 = (f32[512,256]{1,0:T(8,128)S(1)}, f32[512,256]{1,0:T(8,128)S(1)}, u32[]{:S(2)}, u32[]{:S(2)}) collective-permute-start(f32[512,256]{1,0:T(8,128)S(1)} %line.1.cols_ref), channel_id=1, source_target_pairs={{0,1},{1,0},{2,3},{3,2},{4,5},{5,4},{6,7},{7,6},{8,9},{9,8},{10,11... | collective-permute-start | bytes 1572872 | tf_op jit(solution)/shard_map/ppermute | solution.py:393
  141.5 1.9 %collective-permute-start.13 = (bf16[256,512]{1,0:T(8,128)(2,1)S(1)}, bf16[256,512]{1,0:T(8,128)(2,1)S(1)}, u32[]{:S(2)}, u32[]{:S(2)}) collective-permute-start(bf16[256,512]{1,0:T(8,128)(2,1)S(1)} %clips.1.clips_ref.own_ref), channel_id=1, source_target_pairs={{0,1},{1,0},{2,3},{3,2},{4,5},{5,4},{6,7},{7,6},{8,9},{9,8},{10,11... | collective-permute-start | bytes 786440 | tf_op jit(solution)/shard_map/ppermute | solution.py:381

commit v6 on v5

--- a/solution.py
+++ b/solution.py
@@ -99,20 +99,20 @@
 
 
 def ffn_kernel(
-    step, block, d_ref, own_ref, other_ref, gate_ref, up_ref, down_hbm, hid_ref, out_ref, x_ref, down_ref, sem
+    step, block, d_ref, own_ref, other_ref, gate_ref, up_ref, down_hbm, hid_ref, out_ref, down_ref, sem
 ):
     d = d_ref[0]
     rows, part = own_ref.shape
     load_down = pltpu.make_async_copy(down_hbm, down_ref, sem)
     load_down.start()
-    x_ref[:, half(d, part)] = own_ref[...]
-    x_ref[:, half(1 - d, part)] = other_ref[...]
+    mine, theirs = half(d, part), half(1 - d, part)
     steps = [slice(m * step, (m + 1) * step) for m in range(rows // step)]
     for j in range(gate_ref.shape[1] // block):
         span = slice(j * block, (j + 1) * block)
         for at in steps:
-            gate = dot(x_ref[at, :], gate_ref[:, span])
-            upper = dot(x_ref[at, :], up_ref[:, span])
+            own, other = own_ref[at, :], other_ref[at, :]
+            gate = dot(own, gate_ref[mine, span]) + dot(other, gate_ref[theirs, span])
+            upper = dot(own, up_ref[mine, span]) + dot(other, up_ref[theirs, span])
             hid_ref[at, span] = (gate * jax.nn.sigmoid(gate) * upper).astype(BF16)
     load_down.wait()
     for at in steps:
@@ -314,7 +314,6 @@
         in_specs=[SCALAR] + [vmem] * 4 + [hbm],
         out_specs=(vmem, vmem),
         scratch_shapes=[
-            pltpu.VMEM((rows, width), BF16),
             pltpu.VMEM((hidden, width), BF16),
             pltpu.SemaphoreType.DMA(()),
         ],

time: 160 us -> 160 us (level)
  no operation moved by 1% of the time
where the time goes in v6:
time: 160 us; the launch traced here: 159 us
  waiting for transfers between devices  59.5 us (37%)
  starting transfers between devices  55.1 us (34%)
  blocking collectives  23.8 us (15%)
  Pallas kernels  17.9 us (11%)
  local copies, waits for them, and re-layouts  2.02 us (1%)
    ppermute x13, waiting for transfers between devices, ring(): lax.ppermute(block, axis, [(k, (k + step) % size) for k in range(size)])  34.9 us
    ppermute x13, starting transfers between devices, ring(): lax.ppermute(block, axis, [(k, (k + step) % size) for k in range(size)])  19.8 us
    all_to_all x1, starting transfers between devices, per_device(): lax.all_to_all(outgoing.reshape(n_expert, capacity, part), EXP, split_axi...  16.3 us
    all_to_all x1, blocking collectives, per_device(): lax.all_to_all(blocks, PLANE, split_axis=0, concat_axis=0, tiled=True)  13.4 us
    all_to_all x1, waiting for transfers between devices, per_device(): lax.all_to_all(copies, PLANE, split_axis=0, concat_axis=0, tiled=True)  10.7 us
    all_to_all x1, blocking collectives, per_device(): got = lax.all_to_all(payload, 'z', split_axis=0, concat_axis=0, tiled=True)  10.4 us
    all_to_all x1, waiting for transfers between devices, per_device(): lax.all_to_all(outgoing.reshape(n_expert, capacity, part), EXP, split_axi...  6.72 us
    all_to_all x1, starting transfers between devices, per_device(): lax.all_to_all(summed.reshape(n_expert, capacity, part), EXP, split_axis=...  6.32 us
  transfers between devices with their start and end apart: 21, of which 8 were waited for; matrix products, arithmetic and copies ran while one was open for 0% of the time, Pallas kernels for 3%

profile of v6, /device:TPU:1, one launch (start us, length us, event | category | flops | bytes accessed | tf_op | source)
XLA Modules:
  0.0 159.3 jit_solution(12107635455372888074)
XLA Ops:
  0.7 2.4 %prep.1 = bf16[1024,512]{1,0:T(8,128)(2,1)} custom-call(s32[1]{0:T(128)} %bitcast.d_ref, bf16[128,1024]{1,0:T(8,128)(2,1)} %tok_ref.3, s32[2,128]{1,0:T(2,128)} %bitcast.27), custom_call_target="tpu_custom_call" | custom-call | tf_op jit(solution)/shard_map/prep/pallas_call | solution.py:257
  3.1 16.3 %all-to-all-start = ((bf16[128,8,512]{2,1,0:T(8,128)(2,1)}), bf16[128,8,512]{2,1,0:T(8,128)(2,1)S(1)}, u32[]{:S(2)}, u32[]{:S(2)}) async-start(bf16[128,8,512]{2,1,0:T(8,128)(2,1)} %bitcast.29), calls=%async_computation | async-start | bytes 2097152 | tf_op jit(solution)/shard_map/all_to_all | solution.py:282
  21.5 2.8 %collective-permute-start.1 = (bf16[32,1024]{1,0:T(8,128)(2,1)S(1)}, bf16[32,1024]{1,0:T(8,128)(2,1)S(1)}, u32[]{:S(2)}, u32[]{:S(2)}) collective-permute-start(bf16[32,1024]{1,0:T(8,128)(2,1)S(1)} %bitcast.34), channel_id=1, source_target_pairs={{0,128},{64,192},{128,0},{192,64},{1,129},{65,193},{129,1},{193,65... | collective-permute-start | bytes 196616 | tf_op jit(solution)/shard_map/ppermute | solution.py:241
  25.7 1.3 collective-permute-start.4
  27.0 1.5 collective-permute-start.5
  28.5 1.8 %collective-permute-done.1 = bf16[32,1024]{1,0:T(8,128)(2,1)S(1)} collective-permute-done((bf16[32,1024]{1,0:T(8,128)(2,1)S(1)}, bf16[32,1024]{1,0:T(8,128)(2,1)S(1)}, u32[]{:S(2)}, u32[]{:S(2)}) %collective-permute-start.1) | collective-permute-done | bytes 65568 | tf_op jit(solution)/shard_map/ppermute | solution.py:241
  30.3 12.7 %collective-permute-done.4.refs_4_.refs_1_ = bf16[64,512]{1,0:T(8,128)(2,1)S(1)} collective-permute-done((bf16[64,512]{1,0:T(8,128)(2,1)S(1)}, bf16[64,512]{1,0:T(8,128)(2,1)S(1)}, u32[]{:S(2)}, u32[]{:S(2)}) %collective-permute-start.4) | collective-permute-done | bytes 65568 | tf_op jit(solution)/shard_map/ppermute | solution.py:241
  43.0 6.7 %all-to-all-done = bf16[128,8,512]{2,1,0:T(8,128)(2,1)S(1)} async-done(((bf16[128,8,512]{2,1,0:T(8,128)(2,1)}), bf16[128,8,512]{2,1,0:T(8,128)(2,1)S(1)}, u32[]{:S(2)}, u32[]{:S(2)}) %all-to-all-start) | async-done | bytes 1048608 | tf_op jit(solution)/shard_map/all_to_all | solution.py:282
  49.7 3.4 %collective-permute-start.6 = (bf16[1024,512]{1,0:T(8,128)(2,1)S(1)}, bf16[1024,512]{1,0:T(8,128)(2,1)S(1)}, u32[]{:S(2)}, u32[]{:S(2)}) collective-permute-start(bf16[1024,512]{1,0:T(8,128)(2,1)S(1)} %order.1.after_hbm.own_ref), channel_id=1, source_target_pairs={{0,1},{1,0},{2,3},{3,2},{4,5},{5,4},{6,7},{7,6},{8,9},{9,8},{10,11... | collective-permute-start | bytes 3145736 | tf_op jit(solution)/shard_map/ppermute | solution.py:295
  53.1 2.4 %load.1 = (bf16[1024,1024]{1,0:T(8,128)(2,1)S(1)}, bf16[1024,1024]{1,0:T(8,128)(2,1)S(1)}) custom-call(bf16[1024,1024]{1,0:T(8,128)(2,1)} %bitcast.30, bf16[1024,1024]{1,0:T(8,128)(2,1)} %bitcast.31, bf16[1024,512]{1,0:T(8,128)(2,1)S(1)} %order.1.after_hbm.own_ref), custom_call_target="tpu_custom_call" | custom-call | bytes 8388608 | tf_op jit(solution)/shard_map/load/pallas_call | solution.py:298
  55.9 5.9 %ffn.1 = (bf16[1024,1024]{1,0:T(8,128)(2,1)S(1)}, bf16[1024,512]{1,0:T(8,128)(2,1)S(1)}) custom-call(s32[1]{0:T(128)} %bitcast.d_ref, bf16[1024,512]{1,0:T(8,128)(2,1)S(1)} %order.1.after_hbm.own_ref, bf16[1024,512]{1,0:T(8,128)(2,1)S(1)} %collective-permute-done.6.other_ref, bf16[1024,1024]{1,0:T(8,128)(2,1)S(1)} %get-tuple-element.12.gate_ref, ...), custom_call_target="tpu_custom_call" | custom-call | flops 5368709120 | tf_op jit(solution)/shard_map/ffn/pallas_call | solution.py:308
  62.1 1.3 ours.1.own_ref
  63.4 1.4 collective-permute-done.7.brought_ref
  64.8 1.1 total.1
  65.9 6.3 %all-to-all-start.1 = ((bf16[128,8,512]{2,1,0:T(8,128)(2,1)}), bf16[128,8,512]{2,1,0:T(8,128)(2,1)S(1)}, u32[]{:S(2)}, u32[]{:S(2)}) async-start(bf16[128,8,512]{2,1,0:T(8,128)(2,1)} %bitcast.10), calls=%async_computation.1 | async-start | bytes 2097152 | tf_op jit(solution)/shard_map/all_to_all | solution.py:345
  72.2 1.9 %collective-permute-start.10 = (bf16[128,1024]{1,0:T(8,128)(2,1)S(1)}, bf16[128,1024]{1,0:T(8,128)(2,1)S(1)}, u32[]{:S(2)}, u32[]{:S(2)}) collective-permute-start(bf16[128,1024]{1,0:T(8,128)(2,1)S(1)} %pad_maximum_fusion.refs_3_.plane0), channel_id=1, source_target_pairs={{0,48},{16,0},{32,16},{48,32},{1,49},{17,1},{33,17},{49,33},{2,50}... | collective-permute-start | bytes 786440 | tf_op jit(solution)/shard_map/ppermute | solution.py:241
  74.1 1.7 %collective-permute-start.9 = (bf16[128,1024]{1,0:T(8,128)(2,1)S(1)}, bf16[128,1024]{1,0:T(8,128)(2,1)S(1)}, u32[]{:S(2)}, u32[]{:S(2)}) collective-permute-start(bf16[128,1024]{1,0:T(8,128)(2,1)S(1)} %pad_maximum_fusion.refs_3_.plane0), channel_id=1, source_target_pairs={{0,32},{16,48},{32,0},{48,16},{1,33},{17,49},{33,1},{49,17},{2,34}... | collective-permute-start | bytes 786440 | tf_op jit(solution)/shard_map/ppermute | solution.py:241
  75.8 2.1 %collective-permute-start.11 = (bf16[64,512]{1,0:T(8,128)(2,1)S(1)}, bf16[64,512]{1,0:T(8,128)(2,1)S(1)}, u32[]{:S(2)}, u32[]{:S(2)}) collective-permute-start(bf16[64,512]{1,0:T(8,128)(2,1)S(1)} %pad_maximum_fusion.2.refs_6_.refs_0_), channel_id=1, source_target_pairs={{0,4},{2,6},{4,8},{6,10},{8,12},{10,14},{12,0},{14,2},{1,5},{3,7},... | collective-permute-start | bytes 196616 | tf_op jit(solution)/shard_map/ppermute | solution.py:241
  77.9 1.5 collective-permute-start.12
  79.5 20.4 %collective-permute-done.11.refs_3_.refs_2_ = bf16[64,512]{1,0:T(8,128)(2,1)S(1)} collective-permute-done((bf16[64,512]{1,0:T(8,128)(2,1)S(1)}, bf16[64,512]{1,0:T(8,128)(2,1)S(1)}, u32[]{:S(2)}, u32[]{:S(2)}) %collective-permute-start.11) | collective-permute-done | bytes 65568 | tf_op jit(solution)/shard_map/ppermute | solution.py:241
  100.0 3.9 %all-to-all-done.1 = bf16[128,8,512]{2,1,0:T(8,128)(2,1)S(1)} async-done(((bf16[128,8,512]{2,1,0:T(8,128)(2,1)}), bf16[128,8,512]{2,1,0:T(8,128)(2,1)S(1)}, u32[]{:S(2)}, u32[]{:S(2)}) %all-to-all-start.1) | async-done | bytes 1048608 | tf_op jit(solution)/shard_map/all_to_all | solution.py:345
  103.9 1.2 combine.1
  105.1 10.4 %all_to_all.25 = bf16[8,16,512]{2,1,0:T(8,128)(2,1)S(1)} all-to-all(bf16[8,16,512]{2,1,0:T(8,128)(2,1)S(1)} %get-tuple-element.17), channel_id=1, replica_groups=mesh['x'=4,'y'=4,'z'=8,'dp'=2] {'z'}, dimensions={0} | all-to-all | bytes 262144 | tf_op jit(solution)/shard_map/all_to_all | solution.py:361
  115.5 1.1 broadcast_in_dim.2
  116.6 4.0 %all-to-all-start.3 = ((bf16[16,72,512]{2,1,0:T(8,128)(2,1)}), bf16[16,72,512]{2,1,0:T(8,128)(2,1)S(1)}, u32[]{:S(2)}, u32[]{:S(2)}) async-start(bf16[16,72,512]{2,1,0:T(8,128)(2,1)} %broadcast_in_dim.2), calls=%async_computation.3 | async-start | bytes 2359296 | tf_op jit(solution)/shard_map/all_to_all | solution.py:369
  120.9 2.5 %collective-permute-start.15 = (bf16[64,512]{1,0:T(8,128)(2,1)S(1)}, bf16[64,512]{1,0:T(8,128)(2,1)S(1)}, u32[]{:S(2)}, u32[]{:S(2)}) collective-permute-start(bf16[64,512]{1,0:T(8,128)(2,1)S(1)} %pad_maximum_fusion.2.refs_6_.refs_0_), channel_id=1, source_target_pairs={{0,8},{2,10},{4,12},{6,14},{8,0},{10,2},{12,4},{14,6},{1,9},{3,11}... | collective-permute-start | bytes 196616 | tf_op jit(solution)/shard_map/ppermute | solution.py:241
  123.4 2.2 %collective-permute-start.16 = (bf16[64,512]{1,0:T(8,128)(2,1)S(1)}, bf16[64,512]{1,0:T(8,128)(2,1)S(1)}, u32[]{:S(2)}, u32[]{:S(2)}) collective-permute-start(bf16[64,512]{1,0:T(8,128)(2,1)S(1)} %pad_maximum_fusion.2.refs_6_.refs_0_), channel_id=1, source_target_pairs={{0,10},{2,12},{4,14},{6,0},{8,2},{10,4},{12,6},{14,8},{1,11},{3,13... | collective-permute-start | bytes 196616 | tf_op jit(solution)/shard_map/ppermute | solution.py:241
  125.7 10.7 %all-to-all-done.3.frames_ref = bf16[16,72,512]{2,1,0:T(8,128)(2,1)S(1)} async-done(((bf16[16,72,512]{2,1,0:T(8,128)(2,1)}), bf16[16,72,512]{2,1,0:T(8,128)(2,1)S(1)}, u32[]{:S(2)}, u32[]{:S(2)}) %all-to-all-start.3) | async-done | bytes 1179680 | tf_op jit(solution)/shard_map/all_to_all | solution.py:369
  137.6 3.8 %collective-permute-start.17 = (f32[512,256]{1,0:T(8,128)S(1)}, f32[512,256]{1,0:T(8,128)S(1)}, u32[]{:S(2)}, u32[]{:S(2)}) collective-permute-start(f32[512,256]{1,0:T(8,128)S(1)} %line.1.cols_ref), channel_id=1, source_target_pairs={{0,1},{1,0},{2,3},{3,2},{4,5},{5,4},{6,7},{7,6},{8,9},{9,8},{10,11... | collective-permute-start | bytes 1572872 | tf_op jit(solution)/shard_map/ppermute | solution.py:392
  141.5 1.8 %collective-permute-done.13.other_ref = bf16[256,512]{1,0:T(8,128)(2,1)S(1)} collective-permute-done((bf16[256,512]{1,0:T(8,128)(2,1)S(1)}, bf16[256,512]{1,0:T(8,128)(2,1)S(1)}, u32[]{:S(2)}, u32[]{:S(2)}) %collective-permute-start.13) | collective-permute-done | bytes 262176 | tf_op jit(solution)/shard_map/ppermute | solution.py:380
  143.3 1.5 covariance.1
  144.8 13.4 %all_to_all.26.in_ref = bf16[16,32,512]{2,1,0:T(8,128)(2,1)S(1)} all-to-all(bf16[16,32,512]{2,1,0:T(8,128)(2,1)S(1)} %covariance.1), channel_id=1, replica_groups=mesh['x'=4,'y'=4,'z'=8,'dp'=2] {'x','y'}, dimensions={0} | all-to-all | bytes 1048576 | tf_op jit(solution)/shard_map/all_to_all | solution.py:402
  (48 shorter events, 6.9 us)
Async XLA Ops:
  0.6 24.7 %copy-start.3 = (s32[128,2]{0,1:T(2,128)S(1)}, s32[128,2]{0,1:T(2,128)}, u32[]{:S(2)}) copy-start(s32[128,2]{0,1:T(2,128)} %param.14) | copy-start | bytes 3076
  0.6 24.7 %copy-start = (bf16[128,1024]{1,0:T(8,128)(2,1)S(1)}, bf16[128,1024]{1,0:T(8,128)(2,1)}, u32[]{:S(2)}) copy-start(bf16[128,1024]{1,0:T(8,128)(2,1)} %tok_ref.3) | copy-start | bytes 786436
  0.7 18.8 %copy-start.4 = (bf16[1024,32]{0,1:T(8,128)(2,1)S(1)}, bf16[1024,32]{0,1:T(8,128)(2,1)}, u32[]{:S(2)}) copy-start(bf16[1024,32]{0,1:T(8,128)(2,1)} %param.13) | copy-start | bytes 196612
  0.7 24.7 %copy-start.2 = (bf16[1024,64]{0,1:T(8,128)(2,1)S(1)}, bf16[1024,64]{0,1:T(8,128)(2,1)}, u32[]{:S(2)}) copy-start(bf16[1024,64]{0,1:T(8,128)(2,1)} %param.9) | copy-start | bytes 393220
  3.1 46.6 %all-to-all-start = ((bf16[128,8,512]{2,1,0:T(8,128)(2,1)}), bf16[128,8,512]{2,1,0:T(8,128)(2,1)S(1)}, u32[]{:S(2)}, u32[]{:S(2)}) async-start(bf16[128,8,512]{2,1,0:T(8,128)(2,1)} %bitcast.29), calls=%async_computation | async-start | bytes 2097152 | tf_op jit(solution)/shard_map/all_to_all | solution.py:282
  19.5 6.2 %collective-permute-start.3 = (bf16[32,512]{1,0:T(8,128)(2,1)S(1)}, bf16[32,512]{1,0:T(8,128)(2,1)S(1)}, u32[]{:S(2)}, u32[]{:S(2)}) collective-permute-start(bf16[32,512]{1,0:T(8,128)(2,1)S(1)} %broadcast_select_fusion.2), channel_id=1, source_target_pairs={{0,1},{1,0},{2,3},{3,2},{4,5},{5,4},{6,7},{7,6},{8,9},{9,8},{10,11... | collective-permute-start | bytes 98312 | tf_op jit(solution)/shard_map/ppermute | solution.py:247
  20.5 7.9 %collective-permute-start = (bf16[32,1024]{1,0:T(8,128)(2,1)S(1)}, bf16[32,1024]{1,0:T(8,128)(2,1)S(1)}, u32[]{:S(2)}, u32[]{:S(2)}) collective-permute-start(bf16[32,1024]{1,0:T(8,128)(2,1)S(1)} %bitcast.33), channel_id=1, source_target_pairs={{0,64},{64,128},{128,192},{192,0},{1,65},{65,129},{129,193},{193,1... | collective-permute-start | bytes 196616 | tf_op jit(solution)/shard_map/ppermute | solution.py:241
  21.5 8.8 %collective-permute-start.1 = (bf16[32,1024]{1,0:T(8,128)(2,1)S(1)}, bf16[32,1024]{1,0:T(8,128)(2,1)S(1)}, u32[]{:S(2)}, u32[]{:S(2)}) collective-permute-start(bf16[32,1024]{1,0:T(8,128)(2,1)S(1)} %bitcast.34), channel_id=1, source_target_pairs={{0,128},{64,192},{128,0},{192,64},{1,129},{65,193},{129,1},{193,65... | collective-permute-start | bytes 196616 | tf_op jit(solution)/shard_map/ppermute | solution.py:241
  24.3 5.9 %collective-permute-start.2 = (bf16[32,1024]{1,0:T(8,128)(2,1)S(1)}, bf16[32,1024]{1,0:T(8,128)(2,1)S(1)}, u32[]{:S(2)}, u32[]{:S(2)}) collective-permute-start(bf16[32,1024]{1,0:T(8,128)(2,1)S(1)} %bitcast.35), channel_id=1, source_target_pairs={{0,192},{64,0},{128,64},{192,128},{1,193},{65,1},{129,65},{193,129... | collective-permute-start | bytes 196616 | tf_op jit(solution)/shard_map/ppermute | solution.py:241
  25.7 17.2 %collective-permute-start.4 = (bf16[64,512]{1,0:T(8,128)(2,1)S(1)}, bf16[64,512]{1,0:T(8,128)(2,1)S(1)}, u32[]{:S(2)}, u32[]{:S(2)}) collective-permute-start(bf16[64,512]{1,0:T(8,128)(2,1)S(1)} %pad_maximum_fusion.2.refs_6_.refs_0_), channel_id=1, source_target_pairs={{0,2},{2,4},{4,6},{6,8},{8,10},{10,12},{12,14},{14,0},{1,3},{3,5},... | collective-permute-start | bytes 196616 | tf_op jit(solution)/shard_map/ppermute | solution.py:241
  27.0 16.0 %collective-permute-start.5 = (bf16[64,512]{1,0:T(8,128)(2,1)S(1)}, bf16[64,512]{1,0:T(8,128)(2,1)S(1)}, u32[]{:S(2)}, u32[]{:S(2)}) collective-permute-start(bf16[64,512]{1,0:T(8,128)(2,1)S(1)} %pad_maximum_fusion.2.refs_6_.refs_0_), channel_id=1, source_target_pairs={{0,14},{2,0},{4,2},{6,4},{8,6},{10,8},{12,10},{14,12},{1,15},{3,1}... | collective-permute-start | bytes 196616 | tf_op jit(solution)/shard_map/ppermute | solution.py:241
  49.7 5.8 %collective-permute-start.6 = (bf16[1024,512]{1,0:T(8,128)(2,1)S(1)}, bf16[1024,512]{1,0:T(8,128)(2,1)S(1)}, u32[]{:S(2)}, u32[]{:S(2)}) collective-permute-start(bf16[1024,512]{1,0:T(8,128)(2,1)S(1)} %order.1.after_hbm.own_ref), channel_id=1, source_target_pairs={{0,1},{1,0},{2,3},{3,2},{4,5},{5,4},{6,7},{7,6},{8,9},{9,8},{10,11... | collective-permute-start | bytes 3145736 | tf_op jit(solution)/shard_map/ppermute | solution.py:295
  53.1 2.9 %copy-start.1 = (bf16[1,1024,1024]{2,1,0:T(8,128)(2,1)S(1)}, bf16[1,1024,1024]{2,1,0:T(8,128)(2,1)}, u32[]{:S(2)}) copy-start(bf16[1,1024,1024]{2,1,0:T(8,128)(2,1)} %param.12) | copy-start | bytes 6291460
  61.8 2.9 %collective-permute-start.7 = (bf16[1024,512]{1,0:T(8,128)(2,1)S(1)}, bf16[1024,512]{1,0:T(8,128)(2,1)S(1)}, u32[]{:S(2)}, u32[]{:S(2)}) collective-permute-start(bf16[1024,512]{1,0:T(8,128)(2,1)S(1)} %get-tuple-element.15), channel_id=1, source_target_pairs={{0,1},{1,0},{2,3},{3,2},{4,5},{5,4},{6,7},{7,6},{8,9},{9,8},{10,11... | collective-permute-start | bytes 3145736 | tf_op jit(solution)/shard_map/ppermute | solution.py:327
  65.9 13.5 %copy-start.5 = (s32[8]{0:T(128)S(1)}, s32[8]{0:T(128)}, u32[]{:S(2)}) copy-start(s32[8]{0:T(128)} %param.15) | copy-start | bytes 100
  65.9 38.0 %all-to-all-start.1 = ((bf16[128,8,512]{2,1,0:T(8,128)(2,1)}), bf16[128,8,512]{2,1,0:T(8,128)(2,1)S(1)}, u32[]{:S(2)}, u32[]{:S(2)}) async-start(bf16[128,8,512]{2,1,0:T(8,128)(2,1)} %bitcast.10), calls=%async_computation.1 | async-start | bytes 2097152 | tf_op jit(solution)/shard_map/all_to_all | solution.py:345
  72.2 27.7 %collective-permute-start.10 = (bf16[128,1024]{1,0:T(8,128)(2,1)S(1)}, bf16[128,1024]{1,0:T(8,128)(2,1)S(1)}, u32[]{:S(2)}, u32[]{:S(2)}) collective-permute-start(bf16[128,1024]{1,0:T(8,128)(2,1)S(1)} %pad_maximum_fusion.refs_3_.plane0), channel_id=1, source_target_pairs={{0,48},{16,0},{32,16},{48,32},{1,49},{17,1},{33,17},{49,33},{2,50}... | collective-permute-start | bytes 786440 | tf_op jit(solution)/shard_map/ppermute | solution.py:241
  74.1 25.8 %collective-permute-start.8 = (bf16[128,1024]{1,0:T(8,128)(2,1)S(1)}, bf16[128,1024]{1,0:T(8,128)(2,1)S(1)}, u32[]{:S(2)}, u32[]{:S(2)}) collective-permute-start(bf16[128,1024]{1,0:T(8,128)(2,1)S(1)} %pad_maximum_fusion.refs_3_.plane0), channel_id=1, source_target_pairs={{0,16},{16,32},{32,48},{48,0},{1,17},{17,33},{33,49},{49,1},{2,18}... | collective-permute-start | bytes 786440 | tf_op jit(solution)/shard_map/ppermute | solution.py:241
  74.1 25.8 %collective-permute-start.9 = (bf16[128,1024]{1,0:T(8,128)(2,1)S(1)}, bf16[128,1024]{1,0:T(8,128)(2,1)S(1)}, u32[]{:S(2)}, u32[]{:S(2)}) collective-permute-start(bf16[128,1024]{1,0:T(8,128)(2,1)S(1)} %pad_maximum_fusion.refs_3_.plane0), channel_id=1, source_target_pairs={{0,32},{16,48},{32,0},{48,16},{1,33},{17,49},{33,1},{49,17},{2,34}... | collective-permute-start | bytes 786440 | tf_op jit(solution)/shard_map/ppermute | solution.py:241
  75.8 24.1 %collective-permute-start.11 = (bf16[64,512]{1,0:T(8,128)(2,1)S(1)}, bf16[64,512]{1,0:T(8,128)(2,1)S(1)}, u32[]{:S(2)}, u32[]{:S(2)}) collective-permute-start(bf16[64,512]{1,0:T(8,128)(2,1)S(1)} %pad_maximum_fusion.2.refs_6_.refs_0_), channel_id=1, source_target_pairs={{0,4},{2,6},{4,8},{6,10},{8,12},{10,14},{12,0},{14,2},{1,5},{3,7},... | collective-permute-start | bytes 196616 | tf_op jit(solution)/shard_map/ppermute | solution.py:241
  77.9 22.0 %collective-permute-start.12 = (bf16[64,512]{1,0:T(8,128)(2,1)S(1)}, bf16[64,512]{1,0:T(8,128)(2,1)S(1)}, u32[]{:S(2)}, u32[]{:S(2)}) collective-permute-start(bf16[64,512]{1,0:T(8,128)(2,1)S(1)} %pad_maximum_fusion.2.refs_6_.refs_0_), channel_id=1, source_target_pairs={{0,12},{2,14},{4,0},{6,2},{8,4},{10,6},{12,8},{14,10},{1,13},{3,15... | collective-permute-start | bytes 196616 | tf_op jit(solution)/shard_map/ppermute | solution.py:241
  116.6 19.8 %all-to-all-start.3 = ((bf16[16,72,512]{2,1,0:T(8,128)(2,1)}), bf16[16,72,512]{2,1,0:T(8,128)(2,1)S(1)}, u32[]{:S(2)}, u32[]{:S(2)}) async-start(bf16[16,72,512]{2,1,0:T(8,128)(2,1)} %broadcast_in_dim.2), calls=%async_computation.3 | async-start | bytes 2359296 | tf_op jit(solution)/shard_map/all_to_all | solution.py:369
  120.6 16.6 %collective-permute-start.14 = (bf16[64,512]{1,0:T(8,128)(2,1)S(1)}, bf16[64,512]{1,0:T(8,128)(2,1)S(1)}, u32[]{:S(2)}, u32[]{:S(2)}) collective-permute-start(bf16[64,512]{1,0:T(8,128)(2,1)S(1)} %pad_maximum_fusion.2.refs_6_.refs_0_), channel_id=1, source_target_pairs={{0,6},{2,8},{4,10},{6,12},{8,14},{10,0},{12,2},{14,4},{1,7},{3,9},... | collective-permute-start | bytes 196616 | tf_op jit(solution)/shard_map/ppermute | solution.py:241
  120.9 16.3 %collective-permute-start.15 = (bf16[64,512]{1,0:T(8,128)(2,1)S(1)}, bf16[64,512]{1,0:T(8,128)(2,1)S(1)}, u32[]{:S(2)}, u32[]{:S(2)}) collective-permute-start(bf16[64,512]{1,0:T(8,128)(2,1)S(1)} %pad_maximum_fusion.2.refs_6_.refs_0_), channel_id=1, source_target_pairs={{0,8},{2,10},{4,12},{6,14},{8,0},{10,2},{12,4},{14,6},{1,9},{3,11}... | collective-permute-start | bytes 196616 | tf_op jit(solution)/shard_map/ppermute | solution.py:241
  123.4 13.8 %collective-permute-start.16 = (bf16[64,512]{1,0:T(8,128)(2,1)S(1)}, bf16[64,512]{1,0:T(8,128)(2,1)S(1)}, u32[]{:S(2)}, u32[]{:S(2)}) collective-permute-start(bf16[64,512]{1,0:T(8,128)(2,1)S(1)} %pad_maximum_fusion.2.refs_6_.refs_0_), channel_id=1, source_target_pairs={{0,10},{2,12},{4,14},{6,0},{8,2},{10,4},{12,6},{14,8},{1,11},{3,13... | collective-permute-start | bytes 196616 | tf_op jit(solution)/shard_map/ppermute | solution.py:241
  137.6 5.8 %collective-permute-start.17 = (f32[512,256]{1,0:T(8,128)S(1)}, f32[512,256]{1,0:T(8,128)S(1)}, u32[]{:S(2)}, u32[]{:S(2)}) collective-permute-start(f32[512,256]{1,0:T(8,128)S(1)} %line.1.cols_ref), channel_id=1, source_target_pairs={{0,1},{1,0},{2,3},{3,2},{4,5},{5,4},{6,7},{7,6},{8,9},{9,8},{10,11... | collective-permute-start | bytes 1572872 | tf_op jit(solution)/shard_map/ppermute | solution.py:392
  141.4 1.9 %collective-permute-start.13 = (bf16[256,512]{1,0:T(8,128)(2,1)S(1)}, bf16[256,512]{1,0:T(8,128)(2,1)S(1)}, u32[]{:S(2)}, u32[]{:S(2)}) collective-permute-start(bf16[256,512]{1,0:T(8,128)(2,1)S(1)} %clips.1.clips_ref.own_ref), channel_id=1, source_target_pairs={{0,1},{1,0},{2,3},{3,2},{4,5},{5,4},{6,7},{7,6},{8,9},{9,8},{10,11... | collective-permute-start | bytes 786440 | tf_op jit(solution)/shard_map/ppermute | solution.py:380
